TPU v7x, 256 devices: a whole 4x4x8 slice. The times are simulated.
256 devices in a mesh: shard: 128 (over y, z, x), rep: 2 (over core).
Axes of the slice: x: 4, y: 4, z: 8, core: 2. Of those that a mesh axis runs over, the one named last changes fastest.
Arguments:
- queries: bfloat16 [1024, 768], P(('shard', 'rep')), may hold values from -2 to 2
- slab: bfloat16 [262144, 768], P('shard'), may hold values from -2 to 2
- cand_ids: int32 [1024, 16], P(('shard', 'rep')), may hold values from 0 to 260127, as said below
- patches: bfloat16 [4096, 40, 1024], P('shard'), may hold values from -92 to 92
- text_states: bfloat16 [1024, 16, 768], P(('shard', 'rep')), may hold values from -8 to 8
- w_query: bfloat16 [768, 768], P(None, 'rep'), may hold values from -0.21875 to 0.21875
- w_key: bfloat16 [1024, 768], P(None, 'rep'), may hold values from -0.1875 to 0.1875
- w_value: bfloat16 [1024, 768], P(None, 'rep'), may hold values from -0.1875 to 0.1875
- w_out: bfloat16 [768, 768], P(None, 'rep'), may hold values from -0.21875 to 0.21875
- norm_gain: float32 [768], replicated, may hold values from 0.1 to 1.9
Outputs:
- retrieval: float32 [1024, 16], P(('shard', 'rep'))
- attended: bfloat16 [1024, 16, 16, 768], P(('shard', 'rep'))
Inputs may be any that keep to these rules, and one draw needn't show every extreme that they name: `cand_ids`: each id is c * 2048 + r with r below 32. Among the ids of one device's block of 4 queries (rows b * 4 to b * 4 + 3), at most 1 lie on any one shard c, and on some shard exactly 1.
All inputs are finite; a program needn't handle non-finite values.
Results may differ from a plain program's by a relative error of at most 0.0039.
The roundings to bfloat16 on the way count: a program that leaves them out, or rounds other values in their place, can miss the bound.
Values may be sent and summed in bfloat16 or wider, within the bound.
No kernel may reach another device: no remote copies, remote signals or barrier semaphores. Data moves between devices by JAX's collectives and lax.ppermute only.
A program may use at most 192 MiB of HBM per device.

v0:
```python
import math

import jax
import jax.numpy as jnp
from jax import lax
from jax.sharding import PartitionSpec as P

HEADS = 12


SCALE = 100.0
EPSILON = 1e-06


def combined_all(part, axis, combine):
    gathered = jax.tree.map(lambda a: lax.all_gather(a, axis), part)

    def take(source):
        return jax.tree.map(lambda a: lax.dynamic_index_in_dim(a, source, 0, False), gathered)

    return lax.fori_loop(
        1, lax.axis_size(axis), lambda source, state: combine(state, take(source)), take(0)
    )


def combine_pairs(first, second):
    highest = jnp.maximum(first[0], second[0])
    combined = first[1] * jnp.exp(first[0] - highest) + second[1] * jnp.exp(second[0] - highest)
    return (highest, combined)


def list_ranks(anchor):
    span = anchor.shape[-1]
    same_shard = anchor[..., :, None] == anchor[..., None, :]
    earlier = lax.broadcasted_iota(jnp.int32, (span, span), 1) < lax.broadcasted_iota(
        jnp.int32, (span, span), 0
    )
    return jnp.sum(jnp.where(same_shard & earlier, 1, 0), axis=-1).astype(jnp.int32)


def slot_entries(id_lists, entries, target, capacity, slab_count):
    anchor = id_lists // slab_count
    ranks = list_ranks(anchor)
    slot_ids = lax.broadcasted_iota(jnp.int32, (capacity, 1), 0)
    picked = (anchor[..., None, :] == target) & (ranks[..., None, :] == slot_ids)
    return jnp.sum(jnp.where(picked, entries[..., None, :], 0), axis=-1)


def attend(projected, key_rows, value_rows, head_count):
    batch, text_count, width = projected.shape
    patch_count = key_rows.shape[1]
    head_size = width // head_count
    query_heads = projected.reshape(batch, text_count, head_count, head_size)
    key_heads = key_rows.reshape(batch, patch_count, head_count, head_size)
    value_heads = value_rows.reshape(batch, patch_count, head_count, head_size)
    scores = jnp.einsum(
        "bthd,bphd->bhtp", query_heads, key_heads, preferred_element_type=jnp.float32
    ) * head_size ** (-0.5)
    highest = jnp.max(scores, axis=-1, keepdims=True)
    weights = jnp.exp(scores - highest)
    weights = (weights / jnp.sum(weights, axis=-1, keepdims=True)).astype(jnp.bfloat16)
    context = jnp.einsum(
        "bhtp,bphd->bthd", weights, value_heads, preferred_element_type=jnp.float32
    )
    return context.reshape(batch, text_count, width).astype(jnp.bfloat16)


def project_rows(rows_in, weight):
    return jnp.einsum("spc,cd->spd", rows_in, weight, preferred_element_type=jnp.float32).astype(
        jnp.bfloat16
    )


def on_device(
    queries, slab, cand_ids, patches, text_states, w_query, w_key, w_value, w_out, norm_gain
):
    shard_count = lax.axis_size("shard")
    shard_here = lax.axis_index("shard")
    query_count, embed_width = queries.shape
    slab_count = slab.shape[0]
    top_count = cand_ids.shape[1]
    list_length = query_count * top_count
    capacity = (list_length + shard_count - 1) // shard_count
    text_count = text_states.shape[1]
    model_width = text_states.shape[2]
    patch_count = patches.shape[1]
    patch_width = patches.shape[2]
    head_count = HEADS
    w_query, w_key, w_value, w_out = (
        lax.all_gather(w_query, "rep", axis=1, tiled=True),
        lax.all_gather(w_key, "rep", axis=1, tiled=True),
        lax.all_gather(w_value, "rep", axis=1, tiled=True),
        lax.all_gather(w_out, "rep", axis=1, tiled=True),
    )
    gathered_count = query_count * shard_count
    initial = (
        jnp.full((gathered_count,), -jnp.inf, jnp.float32),
        jnp.zeros((gathered_count,), jnp.float32),
    )
    logits = SCALE * jnp.einsum(
        "qe,re->qr",
        lax.all_gather(queries, "shard", axis=0, tiled=True),
        slab,
        preferred_element_type=jnp.float32,
    )
    block_peak = jnp.max(logits, axis=1)
    block_total = jnp.sum(jnp.exp(logits - block_peak[:, None]), axis=1)
    earlier = (initial[0], initial[1])
    merged = combine_pairs(earlier, (block_peak, block_total))
    peaks = merged[0]
    totals = merged[1]
    own_start = shard_here * query_count
    peaks, totals = combined_all((peaks, totals), "shard", combine_pairs)
    own_peak = lax.dynamic_slice_in_dim(peaks, own_start, query_count)
    own_total = lax.dynamic_slice_in_dim(totals, own_start, query_count)
    normalizer = own_peak + jnp.log(own_total)
    id_lists = lax.all_gather(cand_ids, "shard", axis=0, tiled=True).reshape(
        shard_count, list_length
    )
    slot_local = slot_entries(
        id_lists, id_lists % slab_count, shard_here, capacity, slab_count
    ).reshape(shard_count * capacity)
    own_list = cand_ids.reshape(list_length)
    own_anchor = own_list // slab_count
    own_flat = own_anchor * capacity + list_ranks(own_anchor)
    projected_text = jnp.dot(
        text_states.reshape(query_count * text_count, model_width),
        w_query,
        preferred_element_type=jnp.float32,
    )
    projected_text = projected_text.astype(jnp.bfloat16).reshape(
        query_count, text_count, model_width
    )
    chosen_rows = jnp.take(slab, slot_local, axis=0).reshape(shard_count, capacity, embed_width)
    chosen_patches = jnp.take(patches, slot_local, axis=0).reshape(
        shard_count, capacity, patch_count, patch_width
    )
    got_patches, got_rows = (
        lax.all_to_all(chosen_patches, "shard", split_axis=0, concat_axis=0, tiled=True),
        lax.all_to_all(chosen_rows, "shard", split_axis=0, concat_axis=0, tiled=True),
    )
    picked = jnp.take(
        got_patches.reshape(shard_count * capacity, patch_count, patch_width), own_flat, axis=0
    )
    cand_rows = jnp.take(got_rows.reshape(shard_count * capacity, embed_width), own_flat, axis=0)
    key_rows = project_rows(picked, w_key)
    value_rows = project_rows(picked, w_value)
    spread_text = jnp.broadcast_to(
        projected_text[:, None], (query_count, top_count, text_count, model_width)
    )
    context = attend(
        spread_text.reshape(list_length, text_count, model_width), key_rows, value_rows, head_count
    )
    cand_logits = SCALE * jnp.einsum(
        "qe,qke->qk",
        queries,
        cand_rows.reshape(query_count, top_count, embed_width),
        preferred_element_type=jnp.float32,
    )
    retrieval = cand_logits - normalizer[:, None] + math.log(slab_count * shard_count)
    mixed = jnp.dot(
        context.reshape(list_length * text_count, model_width),
        w_out,
        preferred_element_type=jnp.float32,
    )
    summed = text_states.astype(jnp.float32)[:, None] + mixed.reshape(
        query_count, top_count, text_count, model_width
    )
    mean = jnp.mean(summed, axis=-1, keepdims=True)
    centred = summed - mean
    variance = jnp.mean(centred * centred, axis=-1, keepdims=True)
    attended = (centred * lax.rsqrt(variance + EPSILON) * norm_gain).astype(jnp.bfloat16)
    return (retrieval, attended)


def solution(mesh):
    in_specs = (
        P(("shard", "rep"), None),
        P("shard", None),
        P(("shard", "rep"), None),
        P("shard", None, None),
        P(("shard", "rep"), None, None),
        P(None, "rep"),
        P(None, "rep"),
        P(None, "rep"),
        P(None, "rep"),
        P(),
    )
    out_specs = (P(("shard", "rep"), None), P(("shard", "rep"), None, None, None))
    return jax.shard_map(
        on_device, mesh=mesh, in_specs=in_specs, out_specs=out_specs, check_vma=False
    )
```

profile of v0, /device:TPU:32, one launch (start us, length us, event | category | flops | bytes accessed | tf_op | source)
XLA Modules:
  0.0 1687.8 jit_solution(18282921757069442839)
XLA Ops:
  9.4 339.1 %all-gather.1 = s32[128,4,16]{2,1,0:T(4,128)S(1)} all-gather(s32[1,4,16]{2,1,0:T(4,128)} %bitcast.117), channel_id=1, replica_groups=mesh['shard'=128,'rep'=2] {'shard'}, dimensions={0}, use_global_device_ids=true | all-gather | bytes 33024 | tf_op jit(solution)/shard_map/all_gather | solution.py:117
  348.6 0.7 select_reduce_fusion
  349.5 0.9 gather_fusion
  351.0 0.7 reduce.1
  351.7 0.7 reshape.522
  352.4 16.0 all-to-all-start
  369.0 359.3 %all-gather.2 = bf16[128,4,768]{2,1,0:T(4,128)(2,1)} all-gather(bf16[1,4,768]{2,1,0:T(4,128)(2,1)S(1)} %bitcast.120), channel_id=1, replica_groups=mesh['shard'=128,'rep'=2] {'shard'}, dimensions={0}, use_global_device_ids=true | all-gather | bytes 792576 | tf_op jit(solution)/shard_map/all_gather | solution.py:102
  728.3 2.3 reshape.505
  730.6 4.9 multiply_reduce_fusion.1
  735.5 9.1 gather_fusion.2
  744.6 10.3 bitcast_select_fusion
  754.9 0.8 exponential_reduce_fusion
  755.7 339.0 %all-gather.4 = f32[128,1,512]{2,1,0:T(1,128)S(1)} all-gather(f32[1,1,512]{2,1,0:T(1,128)S(1)} %bitcast.119), channel_id=1, replica_groups=mesh['shard'=128,'rep'=2] {'shard'}, dimensions={0}, use_global_device_ids=true | all-gather | bytes 264192 | tf_op jit(solution)/shard_map/all_gather | solution.py:16
  1094.8 361.8 %all-gather.3 = f32[128,1,512]{2,1,0:T(1,128)S(1)} all-gather(f32[1,1,512]{2,1,0:T(1,128)S(1)} %bitcast.118), channel_id=2, replica_groups=mesh['shard'=128,'rep'=2] {'shard'}, dimensions={0}, use_global_device_ids=true | all-gather | bytes 264192 | tf_op jit(solution)/shard_map/all_gather | solution.py:16
  1456.6 17.7 %all-to-all-start.1 = ((bf16[128,1,40,1024]{3,2,1,0:T(8,128)(2,1)}), bf16[128,1,40,1024]{3,2,1,0:T(8,128)(2,1)}, u32[]{:S(2)}, u32[]{:S(2)}) async-start(bf16[128,1,40,1024]{3,2,1,0:T(8,128)(2,1)} %bitcast_select_fusion), calls=%async_computation.1 | async-start | bytes 20971520 | tf_op jit(solution)/shard_map/all_to_all | solution.py:139
  1474.4 7.5 while.17
  1482.7 0.7 gather_fusion.1
  1484.3 1.6 convolution_convert_fusion.2
  1486.0 3.9 reshape_reshape.3
  1489.9 103.5 %all-to-all-done.1 = bf16[128,1,40,1024]{3,2,1,0:T(8,128)(2,1)} async-done(((bf16[128,1,40,1024]{3,2,1,0:T(8,128)(2,1)}), bf16[128,1,40,1024]{3,2,1,0:T(8,128)(2,1)}, u32[]{:S(2)}, u32[]{:S(2)}) %all-to-all-start.1) | async-done | bytes 10485792 | tf_op jit(solution)/shard_map/all_to_all | solution.py:139
  1593.4 7.2 gather_fusion.3
  1600.5 9.4 convolution_convert_fusion
  1609.9 13.0 reshape.457
  1622.9 9.4 fusion.3
  1632.3 5.1 fusion.40
  1637.5 9.3 convolution_convert_fusion.1
  1646.8 13.0 reshape.455
  1659.8 7.6 convert_bitcast_fusion
  1667.4 3.1 copy.46
  1670.5 5.2 convert_element_type.36
  1675.7 2.7 add_reduce_fusion
  1679.1 1.7 multiply_convert_fusion
  (314 shorter events, 10.2 us)
Async XLA Ops:
  7.2 342.3 %copy-start = (bf16[2048,768]{1,0:T(8,128)(2,1)S(1)}, bf16[2048,768]{1,0:T(8,128)(2,1)}, u32[]{:S(2)}) copy-start(bf16[2048,768]{1,0:T(8,128)(2,1)} %param.13) | copy-start | bytes 9437188
  7.2 361.8 %copy-start.5 = (bf16[4,768]{1,0:T(4,128)(2,1)S(1)}, bf16[4,768]{1,0:T(4,128)(2,1)}, u32[]{:S(2)}) copy-start(bf16[4,768]{1,0:T(4,128)(2,1)} %param.12) | copy-start | bytes 18436
  7.2 1477.1 %all-gather.12.cloned.1.call-start = ((), (), s32[]{:S(2)}) async-start(), calls=%async_computation.3 | async-start | bytes 1769472 | tf_op jit(solution)/shard_map/all_gather | solution.py:90
  7.9 1592.6 %all-gather.14.cloned.1.call-start = ((), (), s32[]{:S(2)}) async-start(), calls=%async_computation.4 | async-start | bytes 2359296 | tf_op jit(solution)/shard_map/all_gather | solution.py:91
  8.7 1628.8 %all-gather.10.cloned.1.call-start = ((), (), s32[]{:S(2)}) async-start(), calls=%async_computation.2 | async-start | bytes 2359296 | tf_op jit(solution)/shard_map/all_gather | solution.py:92
  352.4 1104.2 %all-to-all-start = ((bf16[128,2,384]{2,1,0:T(2,128)(2,1)}), bf16[128,2,384]{2,1,0:T(2,128)(2,1)S(1)}, u32[]{:S(2)}, u32[]{:S(2)}) async-start(bf16[128,2,384]{2,1,0:T(2,128)(2,1)} %reshape.522), calls=%async_computation | async-start | bytes 393216 | tf_op jit(solution)/shard_map/all_to_all | solution.py:140
  368.4 1307.3 %all-gather.16.cloned.1.call-start = ((), (), s32[]{:S(2)}) async-start(), calls=%async_computation.5 | async-start | bytes 1769472 | tf_op jit(solution)/shard_map/all_gather | solution.py:93
  744.6 10.3 copy-start.2
  1456.6 25.3 %copy-start.4 = (s32[4,16]{1,0:T(4,128)S(1)}, s32[4,16]{1,0:T(4,128)}, u32[]{:S(2)}) copy-start(s32[4,16]{1,0:T(4,128)} %param.14) | copy-start | bytes 772
  1456.6 25.4 %copy-start.3 = (bf16[4,16,768]{2,1,0:T(8,128)(2,1)S(1)}, bf16[4,16,768]{2,1,0:T(8,128)(2,1)}, u32[]{:S(2)}) copy-start(bf16[4,16,768]{2,1,0:T(8,128)(2,1)} %param.16) | copy-start | bytes 294916
  1456.6 136.8 %all-to-all-start.1 = ((bf16[128,1,40,1024]{3,2,1,0:T(8,128)(2,1)}), bf16[128,1,40,1024]{3,2,1,0:T(8,128)(2,1)}, u32[]{:S(2)}, u32[]{:S(2)}) async-start(bf16[128,1,40,1024]{3,2,1,0:T(8,128)(2,1)} %bitcast_select_fusion), calls=%async_computation.1 | async-start | bytes 20971520 | tf_op jit(solution)/shard_map/all_to_all | solution.py:139
  1675.7 3.4 copy-start.6
  1678.5 2.4 copy-start.1
Sparse Core Ops, SparseCore 0:
  9.8 17.1 all-gather.11
  28.8 16.3 all-gather.13
  47.0 16.3 all-gather.9
  370.7 16.0 all-gather.15
where the time goes:
time: 1700 us; the launch traced here: 1690 us
  blocking collectives  1400 us (82%)
  waiting for transfers between devices  106 us (6%)
  local copies, waits for them, and re-layouts  61.8 us (4%)
  matrix products  45.2 us (3%)
  starting transfers between devices  33.9 us (2%)
  other arithmetic  23.8 us (1%)
    all_gather x2, blocking collectives, combined_all(): gathered = jax.tree.map(lambda a: lax.all_gather(a, axis), part)  701 us
    all_gather x1, blocking collectives, on_device(): lax.all_gather(queries, 'shard', axis=0, tiled=True)  359 us
    all_gather x1, blocking collectives, on_device(): lax.all_gather(cand_ids, 'shard', axis=0, tiled=True)  339 us
    all_to_all x1, waiting for transfers between devices, on_device(): lax.all_to_all(chosen_patches, 'shard', split_axis=0, concat_axis=0, tile...  103 us
  transfers between devices with their start and end apart: 6, of which 1 were waited for; matrix products, arithmetic and copies ran while one was open for 7% of the time, Pallas kernels for 0%

commit v1 on v0

v1 whole, which is shorter than its diff:
```python
import functools
import math

import jax
import jax.numpy as jnp
from jax import lax
from jax.experimental import pallas as pl
from jax.experimental.pallas import tpu as pltpu
from jax.sharding import PartitionSpec as P

HEADS = 12
SCALE = 100.0
EPSILON = 1e-06
LANES = 128
EXTRA = 8
UNROLL = 4
VMEM_LIMIT = 48 * 1024 * 1024


def row_of(shape, dim):
    return lax.broadcasted_iota(jnp.int32, shape, dim)


def request_kernel(row_ids, list_ids, text, w_own, w_other, out, projected, *, top_count, query_count):
    step = pl.program_id(0)
    block = out.shape[0]
    rows = text.shape[0] // query_count

    @pl.when(step == 0)
    def _():
        at = 0
        for weight in (w_own, w_other):
            half = jnp.dot(text[...], weight[...], preferred_element_type=jnp.float32).astype(jnp.bfloat16)
            for c in range(half.shape[1] // LANES):
                for q in range(query_count):
                    projected[q, at : at + rows, :] = half[q * rows : (q + 1) * rows, c * LANES : (c + 1) * LANES]
                at += rows

    body = projected.shape[1]
    tile_row = row_of((EXTRA, LANES), 0)
    for i in range(block):
        slot = step * block + i
        listed = list_ids[slot]
        out[i, :body, :] = projected[lax.div(jnp.maximum(listed, 0), top_count)]
        code = jnp.where(tile_row == 0, row_ids[slot].astype(jnp.float32), listed.astype(jnp.float32))
        out[i, body:, :] = code.astype(jnp.bfloat16)


def make_request(row_ids, list_ids, text, w_own, w_other, top_count, query_count):
    slots = row_ids.shape[0]
    rows = text.shape[0] // query_count
    width = w_own.shape[1] + w_other.shape[1]
    body = width // LANES * rows
    block = min(16, slots)
    whole = lambda shape: pl.BlockSpec(shape, lambda i, *_: (0, 0))
    return pl.pallas_call(
        functools.partial(request_kernel, top_count=top_count, query_count=query_count),
        grid_spec=pltpu.PrefetchScalarGridSpec(
            num_scalar_prefetch=2,
            grid=(slots // block,),
            in_specs=[whole(text.shape), whole(w_own.shape), whole(w_other.shape)],
            out_specs=pl.BlockSpec((block, body + EXTRA, LANES), lambda i, *_: (i, 0, 0)),
            scratch_shapes=[pltpu.VMEM((query_count, body, LANES), jnp.bfloat16)],
        ),
        out_shape=jax.ShapeDtypeStruct((slots, body + EXTRA, LANES), jnp.bfloat16),
        compiler_params=pltpu.CompilerParams(vmem_limit_bytes=VMEM_LIMIT),
        cost_estimate=pl.CostEstimate(flops=2 * text.shape[0] * text.shape[1] * width, bytes_accessed=6 << 20, transcendentals=0),
        name="request",
    )(row_ids, list_ids, text, w_own, w_other)


def attend_group(query, keys, values, masks, head_size):
    rows = query.shape[0]
    heads = query.shape[1] // head_size
    spread = jnp.concatenate([query * masks[h].astype(query.dtype) for h in range(heads)], axis=0)
    scores = lax.dot_general(
        spread, keys, (((1,), (1,)), ((), ())), preferred_element_type=jnp.float32
    ) * head_size ** (-0.5)
    highest = jnp.max(scores, axis=-1, keepdims=True)
    weights = jnp.exp(scores - highest)
    weights = (weights / jnp.sum(weights, axis=-1, keepdims=True)).astype(jnp.bfloat16)
    mixed = jnp.dot(weights, values, preferred_element_type=jnp.float32)
    context = mixed[:rows] * masks[0]
    for h in range(1, heads):
        context = context + mixed[h * rows : (h + 1) * rows] * masks[h]
    return context.astype(jnp.bfloat16)


def attend_kernel(row_ids, got, keys, values, *rest, head_size, rows):
    stats = rest[0] if len(rest) == 3 else None
    out, listed = rest[-2:]
    slots = got.shape[0]
    body = got.shape[1]
    columns = keys.shape[2]

    def build(slot, count):
        listed[count] = slot
        return count + jnp.where(row_ids[slot] >= 0, 1, 0)

    count = lax.fori_loop(0, slots, build, 0)
    last = listed[jnp.maximum(count - 1, 0)]
    for g in range(UNROLL):
        listed[count + g] = last

    spans = []
    at = 0
    while at < columns:
        width = min(2 * LANES, columns - at)
        lane_head = row_of((rows, width), 1) // head_size
        spans.append((at, width, [jnp.where(lane_head == h, 1.0, 0.0) for h in range(width // head_size)]))
        at += width

    def group(index, carry):
        for g in range(UNROLL):
            slot = listed[index * UNROLL + g]
            image = row_ids[slot]
            for at, width, masks in spans:
                pieces = [
                    got[slot, (at // LANES + c) * rows : (at // LANES + c + 1) * rows, :] for c in range(width // LANES)
                ]
                query = pieces[0] if len(pieces) == 1 else jnp.concatenate(pieces, axis=1)
                context = attend_group(
                    query, keys[image, :, at : at + width], values[image, :, at : at + width], masks, head_size
                )
                for c in range(width // LANES):
                    out[slot, (at // LANES + c) * rows : (at // LANES + c + 1) * rows, :] = context[
                        :, c * LANES : (c + 1) * LANES
                    ]
        return carry

    lax.fori_loop(0, lax.div(count + UNROLL - 1, UNROLL), group, 0)

    if stats is not None:
        tile_row = row_of((EXTRA, LANES), 0)

        def put(slot, carry):
            exact = jnp.broadcast_to(stats[pl.ds(slot, 1), :], (EXTRA, LANES))
            high = exact.astype(jnp.bfloat16).astype(jnp.float32)
            rest_1 = exact - high
            middle = rest_1.astype(jnp.bfloat16).astype(jnp.float32)
            low = rest_1 - middle
            out[slot, body:, :] = jnp.where(
                tile_row == 0, high, jnp.where(tile_row == 1, middle, jnp.where(tile_row == 2, low, 0.0))
            ).astype(jnp.bfloat16)
            return carry

        lax.fori_loop(0, slots, put, 0)


def attend(row_ids, got, part, keys, values, stats, rows, head_size):
    slots = got.shape[0]
    body = keys.shape[2] // LANES * rows
    height = body + (0 if stats is None else EXTRA)
    operands = [got, keys, values] + ([] if stats is None else [stats])
    in_specs = [
        pl.BlockSpec((slots, body, LANES), lambda i, *_: (0, part, 0)),
        pl.BlockSpec(keys.shape, lambda i, *_: (0, 0, 0)),
        pl.BlockSpec(values.shape, lambda i, *_: (0, 0, 0)),
    ] + ([] if stats is None else [pl.BlockSpec(stats.shape, lambda i, *_: (0, 0))])
    return pl.pallas_call(
        functools.partial(attend_kernel, head_size=head_size, rows=rows),
        grid_spec=pltpu.PrefetchScalarGridSpec(
            num_scalar_prefetch=1,
            grid=(1,),
            in_specs=in_specs,
            out_specs=pl.BlockSpec((slots, height, LANES), lambda i, *_: (0, 0, 0)),
            scratch_shapes=[pltpu.SMEM((slots + UNROLL,), jnp.int32)],
        ),
        out_shape=jax.ShapeDtypeStruct((slots, height, LANES), jnp.bfloat16),
        compiler_params=pltpu.CompilerParams(vmem_limit_bytes=VMEM_LIMIT),
        cost_estimate=pl.CostEstimate(flops=4 << 30, bytes_accessed=6 << 20, transcendentals=1 << 20),
        name="attend",
    )(row_ids, *operands)


def logits_kernel(queries, slab, picked, out, logits):
    query = queries[...].astype(jnp.bfloat16)
    tile = min(256, slab.shape[0])
    peak = None
    for t in range(slab.shape[0] // tile):
        part = SCALE * lax.dot_general(
            slab[t * tile : (t + 1) * tile, :], query, (((1,), (1,)), ((), ())), preferred_element_type=jnp.float32
        )
        logits[t * tile : (t + 1) * tile, :] = part
        top = jnp.max(part, axis=0, keepdims=True)
        peak = top if peak is None else jnp.maximum(peak, top)
    total = jnp.zeros_like(peak)
    for t in range(slab.shape[0] // tile):
        total = total + jnp.sum(jnp.exp(logits[t * tile : (t + 1) * tile, :] - peak), axis=0, keepdims=True)
    store = min(tile, slab.shape[0])
    chosen = row_of((store, queries.shape[0]), 0) == picked[...]
    candidate = jnp.sum(jnp.where(chosen, logits[:store, :], 0.0), axis=0, keepdims=True)
    tile_row = row_of(out.shape, 0)
    out[...] = jnp.where(tile_row == 0, peak, jnp.where(tile_row == 1, total, candidate))


def index_stats(queries, slab, picked):
    count = queries.shape[0]
    return pl.pallas_call(
        logits_kernel,
        out_shape=jax.ShapeDtypeStruct((8, count), jnp.float32),
        scratch_shapes=[pltpu.VMEM((slab.shape[0], count), jnp.float32)],
        compiler_params=pltpu.CompilerParams(vmem_limit_bytes=VMEM_LIMIT),
        cost_estimate=pl.CostEstimate(
            flops=2 * count * slab.shape[0] * slab.shape[1], bytes_accessed=5 << 20, transcendentals=count * slab.shape[0]
        ),
        name="index_stats",
    )(queries, slab, picked)


def finish_kernel(shards, first, second, text, w_out, gain, out, merged, gathered, *, top_count, query_count):
    step = pl.program_id(0)
    rows = text.shape[1]
    half = first.shape[1]

    @pl.when(step == 0)
    def _():
        sent = second[:, half:, :].astype(jnp.float32)
        exact = jnp.sum(jnp.where(row_of(sent.shape, 1) < 3, sent, 0.0), axis=1)
        peak = jnp.max(exact, axis=0, keepdims=True)
        scaled = jnp.exp(exact - peak) * pltpu.roll(exact, LANES - query_count, 1)
        lane = row_of(peak.shape, 1)
        total = jnp.sum(scaled, axis=0, keepdims=True)
        normalizer = peak + jnp.log(jnp.where(lane < query_count, total, 1.0))
        candidate = jnp.sum(exact, axis=0, keepdims=True)
        tile_row = row_of(merged.shape, 0)
        merged[...] = jnp.where(tile_row == 0, normalizer, candidate)

    for k in range(top_count):
        shard = shards[step * top_count + k]
        for j in range(half // rows):
            gathered[k * rows : (k + 1) * rows, j * LANES : (j + 1) * LANES] = first[shard, j * rows : (j + 1) * rows, :]
            column = half // rows + j
            gathered[k * rows : (k + 1) * rows, column * LANES : (column + 1) * LANES] = second[
                shard, j * rows : (j + 1) * rows, :
            ]
    mixed = jnp.dot(gathered[...], w_out[...], preferred_element_type=jnp.float32)
    width = mixed.shape[1]
    summed = mixed.reshape(top_count, rows, width) + text[...].astype(jnp.float32)
    mean = jnp.mean(summed, axis=-1, keepdims=True)
    centred = summed - mean
    variance = jnp.mean(centred * centred, axis=-1, keepdims=True)
    normed = centred * lax.rsqrt(variance + EPSILON) * gain[...].reshape(1, 1, width)
    out[...] = normed.astype(jnp.bfloat16).reshape(out.shape)


def finish(shards, first, second, text, w_out, gain, top_count):
    query_count, rows, width = text.shape
    full = lambda a: pl.BlockSpec(a.shape, lambda i, *_: (0,) * a.ndim)
    return pl.pallas_call(
        functools.partial(finish_kernel, top_count=top_count, query_count=query_count),
        grid_spec=pltpu.PrefetchScalarGridSpec(
            num_scalar_prefetch=1,
            grid=(query_count,),
            in_specs=[
                full(first),
                full(second),
                pl.BlockSpec((1, rows, width), lambda i, *_: (i, 0, 0)),
                full(w_out),
                full(gain),
            ],
            out_specs=[
                pl.BlockSpec((1, top_count, rows, width), lambda i, *_: (i, 0, 0, 0)),
                pl.BlockSpec((8, LANES), lambda i, *_: (0, 0)),
            ],
            scratch_shapes=[pltpu.VMEM((top_count * rows, width), jnp.bfloat16)],
        ),
        out_shape=[
            jax.ShapeDtypeStruct((query_count, top_count, rows, width), jnp.bfloat16),
            jax.ShapeDtypeStruct((8, LANES), jnp.float32),
        ],
        compiler_params=pltpu.CompilerParams(vmem_limit_bytes=VMEM_LIMIT),
        cost_estimate=pl.CostEstimate(
            flops=2 * query_count * top_count * rows * width * width, bytes_accessed=7 << 20, transcendentals=0
        ),
        name="finish",
    )(shards, first, second, text, w_out, gain)


def project_rows(rows_in, weight):
    return jnp.einsum("spc,cd->spd", rows_in, weight, preferred_element_type=jnp.float32).astype(jnp.bfloat16)


def on_device(queries, slab, cand_ids, patches, text_states, w_query, w_key, w_value, w_out, norm_gain):
    shard_count = lax.axis_size("shard")
    core = lax.axis_index("rep")
    query_count, embed_width = queries.shape
    slab_count = slab.shape[0]
    top_count = cand_ids.shape[1]
    list_length = query_count * top_count
    text_count, model_width = text_states.shape[1:]
    head_size = model_width // HEADS
    swap = [(0, 1), (1, 0)]
    w_query_other = lax.ppermute(w_query, "rep", swap)

    own_list = cand_ids.reshape(list_length)
    own_anchor = own_list // slab_count
    here = own_anchor[None, :] == row_of((shard_count, 1), 0)
    row_ids = jnp.sum(jnp.where(here, own_list[None, :] % slab_count + 1, 0), axis=1) - 1
    list_ids = jnp.sum(jnp.where(here, row_of((1, list_length), 1) + 1, 0), axis=1) - 1

    request = make_request(
        row_ids,
        list_ids,
        text_states.reshape(query_count * text_count, model_width),
        w_query,
        w_query_other,
        top_count,
        query_count,
    )
    got = lax.all_to_all(request, "shard", split_axis=0, concat_axis=0, tiled=True)
    all_queries = lax.all_gather(queries.astype(jnp.float32), "shard", axis=0, tiled=True)

    w_key_other = lax.ppermute(w_key, "rep", swap)
    w_value_other = lax.ppermute(w_value, "rep", swap)
    w_out_other = lax.ppermute(w_out, "rep", swap)
    keys = (project_rows(patches, w_key), project_rows(patches, w_key_other))
    values = (project_rows(patches, w_value), project_rows(patches, w_value_other))
    half = model_width // 2
    w_out_whole = jnp.where(
        core == 0,
        jnp.concatenate([w_out, w_out_other], axis=1),
        jnp.concatenate(
            [
                jnp.concatenate([w_out_other[half:], w_out[half:]], axis=1),
                jnp.concatenate([w_out_other[:half], w_out[:half]], axis=1),
            ],
            axis=0,
        ),
    )

    body = got.shape[1] - EXTRA
    got_row = got[:, body, 0].astype(jnp.int32)
    got_list = got[:, body + 1, 0].astype(jnp.int32)
    context_first = attend(got_row, got, 0, keys[0], values[0], None, text_count, head_size)
    back_first = lax.all_to_all(context_first, "shard", split_axis=0, concat_axis=0, tiled=True)

    got_query = jnp.where(got_list >= 0, got_list // top_count, -1)
    picked = jnp.where(got_query[:, None] == row_of((1, query_count), 1), got_row[:, None], -1)
    found = index_stats(all_queries, slab, picked.reshape(1, shard_count * query_count))
    by_owner = found[:3].reshape(3, shard_count, query_count)
    candidate = jnp.sum(by_owner[2], axis=1)
    placed = jnp.where(got_list[:, None] == row_of((1, list_length), 1), candidate[:, None], 0.0)
    stats = jnp.concatenate(
        [
            by_owner[0],
            by_owner[1],
            placed,
            jnp.zeros((shard_count, LANES - 2 * query_count - list_length), jnp.float32),
        ],
        axis=1,
    )
    context_second = attend(got_row, got, 1, keys[1], values[1], stats, text_count, head_size)
    back_second = lax.all_to_all(context_second, "shard", split_axis=0, concat_axis=0, tiled=True)

    attended, merged = finish(
        own_anchor, back_first, back_second, text_states, w_out_whole, norm_gain.reshape(1, model_width), top_count
    )
    cand_logits = merged[1, 2 * query_count : 2 * query_count + list_length].reshape(query_count, top_count)
    retrieval = cand_logits - merged[0, :query_count, None] + math.log(slab_count * shard_count)
    return (retrieval, attended)


def solution(mesh):
    in_specs = (
        P(("shard", "rep"), None),
        P("shard", None),
        P(("shard", "rep"), None),
        P("shard", None, None),
        P(("shard", "rep"), None, None),
        P(None, "rep"),
        P(None, "rep"),
        P(None, "rep"),
        P(None, "rep"),
        P(),
    )
    out_specs = (P(("shard", "rep"), None), P(("shard", "rep"), None, None, None))
    return jax.shard_map(
        on_device, mesh=mesh, in_specs=in_specs, out_specs=out_specs, check_vma=False
    )
```

time: 1700 us -> 295 us (0.17)
  blocking collectives: 1400 us -> 0 us
  Pallas kernels: 0 us -> 71.9 us
  local copies, waits for them, and re-layouts: 61.8 us -> 22.2 us
  matrix products: 45.2 us -> 12.3 us
    all_gather x4 -> x0, blocking collectives: 1400 us -> none  [the longest x2 701 us: combined_all(): gathered = jax.tree.map(lambda a: lax.all_gather(a, axis), part)]
    pallas_call x0 -> x5, Pallas kernels: none -> 71.9 us  [the longest x2 61.4 us: attend(): pl.pallas_call(functools.partial(attend_kernel, head_size=head_size, rows...]
    dot_general x6 -> x0, matrix products: 26.4 us -> none  [the longest x1 9.41 us: attend(): jnp.einsum('bthd,bphd->bhtp', query_heads, key_heads, preferred_element_t...]
    reshape x2 -> x1, local copies, waits for them, and re-layouts: 26 us -> 0.01 us  [on_device(): norm_gain.reshape(1, model_width)]
    gather x4 -> x0, local copies, waits for them, and re-layouts: 17.9 us -> none  [the longest x1 9.12 us: on_device(): jnp.take(patches, slot_local, axis=0)]
    all_to_all x2 -> x3, starting transfers between devices: 33.7 us -> 45.4 us  [the longest x1 18.1 us: on_device(): lax.all_to_all(context_second, 'shard', split_axis=0, concat_axis=0, tile...]
    all_to_all x2 -> x3, waiting for transfers between devices: 103 us -> 112 us  [the longest x1 73.8 us: on_device(): lax.all_to_all(request, 'shard', split_axis=0, concat_axis=0, tiled=True)]
  transfers between devices with their start and end apart: 6 -> 8, of which waited for: 1 -> 5; matrix products, arithmetic and copies ran while one was open for 7% -> 10% of each run, Pallas kernels for 0% -> 22%
where the time goes in v1:
time: 295 us; the launch traced here: 293 us
  waiting for transfers between devices  116 us (39%)
  Pallas kernels  71.9 us (24%)
  starting transfers between devices  46.2 us (16%)
  local copies, waits for them, and re-layouts  22.2 us (8%)
  between operations  14.3 us (5%)
  matrix products  12.3 us (4%)
  other arithmetic  10.1 us (3%)
    all_to_all x1, waiting for transfers between devices, on_device(): lax.all_to_all(request, 'shard', split_axis=0, concat_axis=0, tiled=True)  73.8 us
    pallas_call x2, Pallas kernels, attend(): pl.pallas_call(functools.partial(attend_kernel, head_size=head_size, rows...  61.4 us
    all_to_all x1, waiting for transfers between devices, on_device(): lax.all_to_all(context_second, 'shard', split_axis=0, concat_axis=0, tile...  38 us
    unnamed x33, local copies, waits for them, and re-layouts  18.4 us
    all_to_all x1, starting transfers between devices, on_device(): lax.all_to_all(context_second, 'shard', split_axis=0, concat_axis=0, tile...  18.1 us
    all_to_all x1, starting transfers between devices, on_device(): lax.all_to_all(request, 'shard', split_axis=0, concat_axis=0, tiled=True)  15.5 us
    dot_general x4, matrix products, project_rows(): jnp.einsum('spc,cd->spd', rows_in, weight, preferred_element_type=jnp.flo...  12.3 us
    all_to_all x1, starting transfers between devices, on_device(): lax.all_to_all(context_first, 'shard', split_axis=0, concat_axis=0, tiled...  11.8 us
  transfers between devices with their start and end apart: 8, of which 5 were waited for; matrix products, arithmetic and copies ran while one was open for 10% of the time, Pallas kernels for 22%

profile of v1, /device:TPU:32, one launch (start us, length us, event | category | flops | bytes accessed | tf_op | source)
XLA Modules:
  0.0 293.0 jit_solution(921878649030611999)
XLA Ops:
  8.3 1.1 collective-permute-done.w_other
  11.4 1.3 request.1
  12.8 1.8 copy-done.1
  14.6 15.5 %all-to-all-start = ((bf16[128,104,128]{2,1,0:T(8,128)(2,1)}), bf16[128,104,128]{2,1,0:T(8,128)(2,1)}, u32[]{:S(2)}, u32[]{:S(2)}) async-start(bf16[128,104,128]{2,1,0:T(8,128)(2,1)} %copy-done.1), calls=%async_computation | async-start | bytes 6815744 | tf_op jit(solution)/shard_map/all_to_all | solution.py:311
  30.9 3.6 %convolution_convert_fusion.2.values = bf16[32,40,384]{2,1,0:T(8,128)(2,1)} fusion(bf16[32,40,1024]{2,1,0:T(8,128)(2,1)S(1)} %copy-done, bf16[1024,384]{1,0:T(8,128)(2,1)} %param.17), kind=kOutput, calls=%fused_computation.2 | convolution fusion | flops 1007124480 | bytes 4390912 | tf_op jit(solution)/shard_map/spc,cd->spd/dot_general | solution.py:281
  34.5 3.6 %convolution_convert_fusion.3.keys = bf16[32,40,384]{2,1,0:T(8,128)(2,1)} fusion(bf16[32,40,1024]{2,1,0:T(8,128)(2,1)S(1)} %copy-done, bf16[1024,384]{1,0:T(8,128)(2,1)} %param.16), kind=kOutput, calls=%fused_computation.3 | convolution fusion | flops 1007124480 | bytes 4390912 | tf_op jit(solution)/shard_map/spc,cd->spd/dot_general | solution.py:281
  38.1 73.8 %all-to-all-done.got = bf16[128,104,128]{2,1,0:T(8,128)(2,1)} async-done(((bf16[128,104,128]{2,1,0:T(8,128)(2,1)}), bf16[128,104,128]{2,1,0:T(8,128)(2,1)}, u32[]{:S(2)}, u32[]{:S(2)}) %all-to-all-start) | async-done | bytes 3407904 | tf_op jit(solution)/shard_map/all_to_all | solution.py:311
  111.9 5.7 %fusion.4 = (s32[128]{0:T(128)S(1)}, s32[128]{0:T(128)S(1)}) fusion(bf16[128,104,128]{2,1,0:T(8,128)(2,1)} %all-to-all-done.got), kind=kLoop, calls=%fused_computation.10 | loop fusion | flops 256 | bytes 1536 | tf_op jit(solution)/shard_map/convert_element_type | solution.py:334
  117.6 1.2 copy-done.12
  118.8 1.2 copy-done.13
  120.0 30.1 %attend.2 = bf16[128,48,128]{2,1,0:T(8,128)(2,1)S(1)} custom-call(s32[128]{0:T(128)S(1)} %get-tuple-element.7.row_ids, bf16[128,104,128]{2,1,0:T(8,128)(2,1)} %all-to-all-done.got, bf16[32,40,384]{2,1,0:T(8,128)(2,1)S(1)} %copy-done.13, bf16[32,40,384]{2,1,0:T(8,128)(2,1)S(1)} %copy-done.12), custom_call_target="tpu_custom_call" | custom-call | flops 4294967296 | bytes 6291456 | tf_op jit(solution)/shard_map/attend/pallas_call | solution.py:160
  150.1 1.1 copy-done.4
  151.2 11.8 %all-to-all-start.1 = ((bf16[128,48,128]{2,1,0:T(8,128)(2,1)}), bf16[128,48,128]{2,1,0:T(8,128)(2,1)}, u32[]{:S(2)}, u32[]{:S(2)}) async-start(bf16[128,48,128]{2,1,0:T(8,128)(2,1)} %copy-done.4), calls=%async_computation.1 | async-start | bytes 3145728 | tf_op jit(solution)/shard_map/all_to_all | solution.py:336
  163.8 1.9 collective-permute-done.2
  165.7 2.6 convolution_convert_fusion.values
  168.2 2.5 convolution_convert_fusion.1.keys
  170.7 2.8 reshape.162.queries
  173.8 1.4 copy-done.5
  175.2 1.9 copy-done.9
  177.1 2.6 index_stats.1
  180.4 1.2 copy-done.10
  181.6 1.2 copy-done.11
  182.8 31.4 %attend.3 = bf16[128,56,128]{2,1,0:T(8,128)(2,1)S(1)} custom-call(s32[128]{0:T(128)S(1)} %get-tuple-element.7.row_ids, bf16[128,104,128]{2,1,0:T(8,128)(2,1)} %all-to-all-done.got, bf16[32,40,384]{2,1,0:T(8,128)(2,1)S(1)} %copy-done.11, bf16[32,40,384]{2,1,0:T(8,128)(2,1)S(1)} %copy-done.10, f32[128,128]{1,0:T(8,128)S(1)} %maximum_maximum_fusion.rest_0_), custom_call_target="tpu_custom_call" | custom-call | flops 4294967296 | bytes 6291456 | tf_op jit(solution)/shard_map/attend/pallas_call | solution.py:160
  214.2 1.3 copy-done.3
  215.5 18.1 %all-to-all-start.2 = ((bf16[128,56,128]{2,1,0:T(8,128)(2,1)}), bf16[128,56,128]{2,1,0:T(8,128)(2,1)}, u32[]{:S(2)}, u32[]{:S(2)}) async-start(bf16[128,56,128]{2,1,0:T(8,128)(2,1)} %copy-done.3), calls=%async_computation.2 | async-start | bytes 3670016 | tf_op jit(solution)/shard_map/all_to_all | solution.py:354
  233.7 1.1 fusion.10
  234.8 1.2 collective-permute-done.3
  236.0 1.1 fusion.9
  237.1 2.6 maximum_select_fusion.w_out
  239.6 38.0 %all-to-all-done.2.second = bf16[128,56,128]{2,1,0:T(8,128)(2,1)} async-done(((bf16[128,56,128]{2,1,0:T(8,128)(2,1)}), bf16[128,56,128]{2,1,0:T(8,128)(2,1)}, u32[]{:S(2)}, u32[]{:S(2)}) %all-to-all-start.2) | async-done | bytes 1835040 | tf_op jit(solution)/shard_map/all_to_all | solution.py:354
  277.6 1.3 copy-done.2
  278.9 6.4 %finish.1 = (bf16[4,16,16,768]{3,2,1,0:T(8,128)(2,1)}, f32[8,128]{1,0:T(8,128)S(1)}) custom-call(s32[64]{0:T(128)S(1)} %get-tuple-element.18.shards, bf16[128,48,128]{2,1,0:T(8,128)(2,1)} %all-to-all-done.1.first, bf16[128,56,128]{2,1,0:T(8,128)(2,1)} %all-to-all-done.2.second, bf16[4,16,768]{2,1,0:T(8,128)(2,1)S(1)} %copy-done.8, ...), custom_call_target="tpu_custom_call" | custom-call | flops 1207959552 | bytes 7340032 | tf_op jit(solution)/shard_map/finish/pallas_call | solution.py:250
  (54 shorter events, 6.3 us)
Async XLA Ops:
  7.2 23.7 %copy-start = (bf16[32,40,1024]{2,1,0:T(8,128)(2,1)S(1)}, bf16[32,40,1024]{2,1,0:T(8,128)(2,1)}, u32[]{:S(2)}) copy-start(bf16[32,40,1024]{2,1,0:T(8,128)(2,1)} %param.13) | copy-start | bytes 7864324
  7.2 2.3 collective-permute-start
  9.5 1.1 copy-start.6
  10.5 0.9 copy-start.7
  12.8 1.8 copy-start.1
  14.6 15.6 %copy-start.14 = (bf16[4,768]{1,0:T(4,128)(2,1)S(1)}, bf16[4,768]{1,0:T(4,128)(2,1)}, u32[]{:S(2)}) copy-start(bf16[4,768]{1,0:T(4,128)(2,1)} %param.10) | copy-start | bytes 18436
  14.6 97.3 %all-to-all-start = ((bf16[128,104,128]{2,1,0:T(8,128)(2,1)}), bf16[128,104,128]{2,1,0:T(8,128)(2,1)}, u32[]{:S(2)}, u32[]{:S(2)}) async-start(bf16[128,104,128]{2,1,0:T(8,128)(2,1)} %copy-done.1), calls=%async_computation | async-start | bytes 6815744 | tf_op jit(solution)/shard_map/all_to_all | solution.py:311
  30.1 140.6 %all-gather.3.cloned.1.call-start = ((), (), s32[]{:S(2)}) async-start(), calls=%async_computation.3 | async-start | bytes 1585152 | tf_op jit(solution)/shard_map/all_gather | solution.py:312
  117.6 1.2 copy-start.12
  118.8 1.2 copy-start.13
  150.1 1.2 copy-start.4
  151.2 64.2 %all-to-all-start.1 = ((bf16[128,48,128]{2,1,0:T(8,128)(2,1)}), bf16[128,48,128]{2,1,0:T(8,128)(2,1)}, u32[]{:S(2)}, u32[]{:S(2)}) async-start(bf16[128,48,128]{2,1,0:T(8,128)(2,1)} %copy-done.4), calls=%async_computation.1 | async-start | bytes 3145728 | tf_op jit(solution)/shard_map/all_to_all | solution.py:336
  163.1 2.6 collective-permute-start.2
  163.2 5.0 %collective-permute-start.1 = (bf16[1024,384]{1,0:T(8,128)(2,1)}, bf16[1024,384]{1,0:T(8,128)(2,1)S(1)}, u32[]{:S(2)}, u32[]{:S(2)}) collective-permute-start(bf16[1024,384]{1,0:T(8,128)(2,1)} %param.16), channel_id=1, source_target_pairs={{0,1},{1,0},{2,3},{3,2},{4,5},{5,4},{6,7},{7,6},{8,9},{9,8},{10,11... | collective-permute-start | bytes 2359304 | tf_op jit(solution)/shard_map/ppermute | solution.py:314
  173.8 1.4 copy-start.5
  175.2 1.9 copy-start.9
  180.4 1.2 copy-start.10
  181.6 1.2 copy-start.11
  214.2 1.3 copy-start.3
  215.4 18.2 %copy-start.15 = (f32[768]{0:T(1024)S(1)}, f32[768]{0:T(1024)}, u32[]{:S(2)}) copy-start(f32[768]{0:T(1024)} %param.19) | copy-start | bytes 9220
  215.5 62.2 %all-to-all-start.2 = ((bf16[128,56,128]{2,1,0:T(8,128)(2,1)}), bf16[128,56,128]{2,1,0:T(8,128)(2,1)}, u32[]{:S(2)}, u32[]{:S(2)}) async-start(bf16[128,56,128]{2,1,0:T(8,128)(2,1)} %copy-done.3), calls=%async_computation.2 | async-start | bytes 3670016 | tf_op jit(solution)/shard_map/all_to_all | solution.py:354
  233.5 2.4 collective-permute-start.3
  234.8 42.8 %copy-start.8 = (bf16[4,16,768]{2,1,0:T(8,128)(2,1)S(1)}, bf16[4,16,768]{2,1,0:T(8,128)(2,1)}, u32[]{:S(2)}) copy-start(bf16[4,16,768]{2,1,0:T(8,128)(2,1)} %text.1) | copy-start | bytes 294916
  277.6 1.3 copy-start.2
Sparse Core Ops, SparseCore 0:
  34.4 113.3 all-gather.2

commit v2 on v1

--- a/solution.py
+++ b/solution.py
@@ -13,7 +13,7 @@
 EPSILON = 1e-06
 LANES = 128
 EXTRA = 8
-UNROLL = 4
+UNROLL = 8
 VMEM_LIMIT = 48 * 1024 * 1024
 
 
@@ -62,40 +62,31 @@
             out_specs=pl.BlockSpec((block, body + EXTRA, LANES), lambda i, *_: (i, 0, 0)),
             scratch_shapes=[pltpu.VMEM((query_count, body, LANES), jnp.bfloat16)],
         ),
-        out_shape=jax.ShapeDtypeStruct((slots, body + EXTRA, LANES), jnp.bfloat16),
+        out_shape=pltpu.HBM((slots, body + EXTRA, LANES), jnp.bfloat16),
         compiler_params=pltpu.CompilerParams(vmem_limit_bytes=VMEM_LIMIT),
         cost_estimate=pl.CostEstimate(flops=2 * text.shape[0] * text.shape[1] * width, bytes_accessed=6 << 20, transcendentals=0),
         name="request",
-    )(row_ids, list_ids, text, w_own, w_other)
-
-
-def attend_group(query, keys, values, masks, head_size):
-    rows = query.shape[0]
-    heads = query.shape[1] // head_size
-    spread = jnp.concatenate([query * masks[h].astype(query.dtype) for h in range(heads)], axis=0)
-    scores = lax.dot_general(
-        spread, keys, (((1,), (1,)), ((), ())), preferred_element_type=jnp.float32
-    ) * head_size ** (-0.5)
-    highest = jnp.max(scores, axis=-1, keepdims=True)
-    weights = jnp.exp(scores - highest)
-    weights = (weights / jnp.sum(weights, axis=-1, keepdims=True)).astype(jnp.bfloat16)
-    mixed = jnp.dot(weights, values, preferred_element_type=jnp.float32)
-    context = mixed[:rows] * masks[0]
-    for h in range(1, heads):
-        context = context + mixed[h * rows : (h + 1) * rows] * masks[h]
-    return context.astype(jnp.bfloat16)
-
-
-def attend_kernel(row_ids, got, keys, values, *rest, head_size, rows):
-    stats = rest[0] if len(rest) == 3 else None
-    out, listed = rest[-2:]
-    slots = got.shape[0]
-    body = got.shape[1]
+    )(row_ids, list_ids, in_hbm(text), in_hbm(w_own), in_hbm(w_other))
+
+
+def attend_kernel(got, codes, keys, values, *rest, head_size, rows):
+    stats = rest[0] if len(rest) == 6 else None
+    out, decoded, table, listed, sem = rest[-5:]
+    slots, body = got.shape[:2]
     columns = keys.shape[2]
+
+    lane = row_of((EXTRA, LANES), 1)
+    code = jnp.zeros((EXTRA, LANES), jnp.float32)
+    for slot in range(slots):
+        code = jnp.where(lane == slot, codes[slot].astype(jnp.float32), code)
+    decoded[...] = code.astype(jnp.int32)
+    copy = pltpu.make_async_copy(decoded, table, sem)
+    copy.start()
+    copy.wait()
 
     def build(slot, count):
         listed[count] = slot
-        return count + jnp.where(row_ids[slot] >= 0, 1, 0)
+        return count + jnp.where(table[0, slot] >= 0, 1, 0)
 
     count = lax.fori_loop(0, slots, build, 0)
     last = listed[jnp.maximum(count - 1, 0)]
@@ -111,66 +102,96 @@
         at += width
 
     def group(index, carry):
-        for g in range(UNROLL):
-            slot = listed[index * UNROLL + g]
-            image = row_ids[slot]
-            for at, width, masks in spans:
-                pieces = [
-                    got[slot, (at // LANES + c) * rows : (at // LANES + c + 1) * rows, :] for c in range(width // LANES)
+        chosen = [listed[index * UNROLL + g] for g in range(UNROLL)]
+        images = [table[0, slot] for slot in chosen]
+        work = [(g, span) for g in range(UNROLL) for span in spans]
+        scores = []
+        for g, (at, width, masks) in work:
+            pieces = [
+                got[chosen[g], (at // LANES + c) * rows : (at // LANES + c + 1) * rows, :] for c in range(width // LANES)
+            ]
+            query = pieces[0] if len(pieces) == 1 else jnp.concatenate(pieces, axis=1)
+            spread = jnp.concatenate([query * mask.astype(query.dtype) for mask in masks], axis=0)
+            scores.append(
+                lax.dot_general(
+                    spread,
+                    keys[images[g], :, at : at + width],
+                    (((1,), (1,)), ((), ())),
+                    preferred_element_type=jnp.float32,
+                )
+            )
+        scores = [score * head_size ** (-0.5) for score in scores]
+        highest = [jnp.max(score, axis=-1, keepdims=True) for score in scores]
+        powers = [jnp.exp(score - top) for score, top in zip(scores, highest)]
+        totals = [jnp.sum(power, axis=-1, keepdims=True) for power in powers]
+        weights = [(power / total).astype(jnp.bfloat16) for power, total in zip(powers, totals)]
+        mixed = [
+            jnp.dot(weight, values[images[g], :, at : at + width], preferred_element_type=jnp.float32)
+            for weight, (g, (at, width, _)) in zip(weights, work)
+        ]
+        for mix, (g, (at, width, masks)) in zip(mixed, work):
+            context = mix[:rows] * masks[0]
+            for h in range(1, len(masks)):
+                context = context + mix[h * rows : (h + 1) * rows] * masks[h]
+            context = context.astype(jnp.bfloat16)
+            for c in range(width // LANES):
+                out[chosen[g], (at // LANES + c) * rows : (at // LANES + c + 1) * rows, :] = context[
+                    :, c * LANES : (c + 1) * LANES
                 ]
-                query = pieces[0] if len(pieces) == 1 else jnp.concatenate(pieces, axis=1)
-                context = attend_group(
-                    query, keys[image, :, at : at + width], values[image, :, at : at + width], masks, head_size
-                )
-                for c in range(width // LANES):
-                    out[slot, (at // LANES + c) * rows : (at // LANES + c + 1) * rows, :] = context[
-                        :, c * LANES : (c + 1) * LANES
-                    ]
         return carry
 
     lax.fori_loop(0, lax.div(count + UNROLL - 1, UNROLL), group, 0)
 
     if stats is not None:
         tile_row = row_of((EXTRA, LANES), 0)
-
-        def put(slot, carry):
-            exact = jnp.broadcast_to(stats[pl.ds(slot, 1), :], (EXTRA, LANES))
+        for slot in range(slots):
+            exact = jnp.broadcast_to(stats[slot : slot + 1, :], (EXTRA, LANES))
             high = exact.astype(jnp.bfloat16).astype(jnp.float32)
-            rest_1 = exact - high
-            middle = rest_1.astype(jnp.bfloat16).astype(jnp.float32)
-            low = rest_1 - middle
+            left = exact - high
+            middle = left.astype(jnp.bfloat16).astype(jnp.float32)
+            low = left - middle
             out[slot, body:, :] = jnp.where(
                 tile_row == 0, high, jnp.where(tile_row == 1, middle, jnp.where(tile_row == 2, low, 0.0))
             ).astype(jnp.bfloat16)
-            return carry
-
-        lax.fori_loop(0, slots, put, 0)
-
-
-def attend(row_ids, got, part, keys, values, stats, rows, head_size):
-    slots = got.shape[0]
+
+
+def in_hbm(array):
+    return pltpu.with_memory_space_constraint(array, pltpu.HBM)
+
+
+def attend(got, part, keys, values, stats, rows, head_size):
+    slots, sent = got.shape[:2]
     body = keys.shape[2] // LANES * rows
     height = body + (0 if stats is None else EXTRA)
-    operands = [got, keys, values] + ([] if stats is None else [stats])
+    last = (sent - EXTRA) // EXTRA
+    operands = [in_hbm(got), in_hbm(got), in_hbm(keys), in_hbm(values)] + ([] if stats is None else [stats])
     in_specs = [
-        pl.BlockSpec((slots, body, LANES), lambda i, *_: (0, part, 0)),
-        pl.BlockSpec(keys.shape, lambda i, *_: (0, 0, 0)),
-        pl.BlockSpec(values.shape, lambda i, *_: (0, 0, 0)),
-    ] + ([] if stats is None else [pl.BlockSpec(stats.shape, lambda i, *_: (0, 0))])
+        pl.BlockSpec((slots, body, LANES), lambda i: (0, part, 0)),
+        pl.BlockSpec((slots, EXTRA, LANES), lambda i: (0, last, 0)),
+        pl.BlockSpec(keys.shape, lambda i: (0, 0, 0)),
+        pl.BlockSpec(values.shape, lambda i: (0, 0, 0)),
+    ] + ([] if stats is None else [pl.BlockSpec(stats.shape, lambda i: (0, 0))])
     return pl.pallas_call(
         functools.partial(attend_kernel, head_size=head_size, rows=rows),
-        grid_spec=pltpu.PrefetchScalarGridSpec(
-            num_scalar_prefetch=1,
-            grid=(1,),
-            in_specs=in_specs,
-            out_specs=pl.BlockSpec((slots, height, LANES), lambda i, *_: (0, 0, 0)),
-            scratch_shapes=[pltpu.SMEM((slots + UNROLL,), jnp.int32)],
-        ),
-        out_shape=jax.ShapeDtypeStruct((slots, height, LANES), jnp.bfloat16),
+        grid=(1,),
+        in_specs=in_specs,
+        out_specs=[
+            pl.BlockSpec((slots, height, LANES), lambda i: (0, 0, 0)),
+            pl.BlockSpec((EXTRA, LANES), lambda i: (0, 0)),
+        ],
+        scratch_shapes=[
+            pltpu.SMEM((EXTRA, LANES), jnp.int32),
+            pltpu.SMEM((slots + UNROLL,), jnp.int32),
+            pltpu.SemaphoreType.DMA,
+        ],
+        out_shape=[
+            pltpu.HBM((slots, height, LANES), jnp.bfloat16),
+            jax.ShapeDtypeStruct((EXTRA, LANES), jnp.int32),
+        ],
         compiler_params=pltpu.CompilerParams(vmem_limit_bytes=VMEM_LIMIT),
         cost_estimate=pl.CostEstimate(flops=4 << 30, bytes_accessed=6 << 20, transcendentals=1 << 20),
         name="attend",
-    )(row_ids, *operands)
+    )(*operands)
 
 
 def logits_kernel(queries, slab, picked, out, logits):
@@ -274,7 +295,7 @@
             flops=2 * query_count * top_count * rows * width * width, bytes_accessed=7 << 20, transcendentals=0
         ),
         name="finish",
-    )(shards, first, second, text, w_out, gain)
+    )(shards, in_hbm(first), in_hbm(second), text, in_hbm(w_out), gain)
 
 
 def project_rows(rows_in, weight):
@@ -329,10 +350,8 @@
         ),
     )
 
-    body = got.shape[1] - EXTRA
-    got_row = got[:, body, 0].astype(jnp.int32)
-    got_list = got[:, body + 1, 0].astype(jnp.int32)
-    context_first = attend(got_row, got, 0, keys[0], values[0], None, text_count, head_size)
+    context_first, decoded = attend(got, 0, keys[0], values[0], None, text_count, head_size)
+    got_row, got_list = decoded[0, :shard_count], decoded[1, :shard_count]
     back_first = lax.all_to_all(context_first, "shard", split_axis=0, concat_axis=0, tiled=True)
 
     got_query = jnp.where(got_list >= 0, got_list // top_count, -1)
@@ -350,7 +369,7 @@
         ],
         axis=1,
     )
-    context_second = attend(got_row, got, 1, keys[1], values[1], stats, text_count, head_size)
+    context_second, _ = attend(got, 1, keys[1], values[1], stats, text_count, head_size)
     back_second = lax.all_to_all(context_second, "shard", split_axis=0, concat_axis=0, tiled=True)
 
     attended, merged = finish(

time: 295 us -> 253 us (0.86)
  Pallas kernels: 71.9 us -> 35.1 us
  waiting for transfers between devices: 116 us -> 139 us
  local copies, waits for them, and re-layouts: 22.2 us -> 9.72 us
  starting transfers between devices: 46.2 us -> 35.6 us
  other arithmetic: 10.1 us -> 4.21 us
    pallas_call x2, Pallas kernels: 61.4 us -> 20.2 us  [attend(): pl.pallas_call(functools.partial(attend_kernel, head_size=head_size, rows...]
    all_gather x1, waiting for transfers between devices: 0.01 us -> 23.7 us  [on_device(): lax.all_gather(queries.astype(jnp.float32), 'shard', axis=0, tiled=True)]
    unnamed x33 -> x17, local copies, waits for them, and re-layouts: 18.4 us -> 6.92 us
    all_to_all x1, starting transfers between devices: 18.1 us -> 11.8 us  [on_device(): lax.all_to_all(context_second, 'shard', split_axis=0, concat_axis=0, tile...]
    convert_element_type x1 -> x0, other arithmetic: 5.71 us -> none  [on_device(): got_list = got[:, body + 1, 0].astype(jnp.int32)]
    all_to_all x1, starting transfers between devices: 11.8 us -> 7.6 us  [on_device(): lax.all_to_all(context_first, 'shard', split_axis=0, concat_axis=0, tiled...]
    pallas_call x1, Pallas kernels: 1.35 us -> 5.55 us  [make_request(): pl.pallas_call(functools.partial(request_kernel, top_count=top_count, que...]
  transfers between devices with their start and end apart: 8 -> 8, of which waited for: 5 -> 5; matrix products, arithmetic and copies ran while one was open for 10% -> 9% of each run, Pallas kernels for 22% -> 9%
where the time goes in v2:
time: 253 us; the launch traced here: 251 us
  waiting for transfers between devices  139 us (55%)
  starting transfers between devices  35.6 us (14%)
  Pallas kernels  35.1 us (14%)
  between operations  14.3 us (6%)
  matrix products  13.5 us (5%)
  local copies, waits for them, and re-layouts  9.72 us (4%)
  other arithmetic  4.21 us (2%)
    all_to_all x1, waiting for transfers between devices, on_device(): lax.all_to_all(request, 'shard', split_axis=0, concat_axis=0, tiled=True)  73.6 us
    all_to_all x1, waiting for transfers between devices, on_device(): lax.all_to_all(context_second, 'shard', split_axis=0, concat_axis=0, tile...  38.2 us
    all_gather x1, waiting for transfers between devices, on_device(): lax.all_gather(queries.astype(jnp.float32), 'shard', axis=0, tiled=True)  23.7 us
    pallas_call x2, Pallas kernels, attend(): pl.pallas_call(functools.partial(attend_kernel, head_size=head_size, rows...  20.2 us
    all_to_all x1, starting transfers between devices, on_device(): lax.all_to_all(request, 'shard', split_axis=0, concat_axis=0, tiled=True)  15.5 us
    dot_general x4, matrix products, project_rows(): jnp.einsum('spc,cd->spd', rows_in, weight, preferred_element_type=jnp.flo...  13.5 us
    all_to_all x1, starting transfers between devices, on_device(): lax.all_to_all(context_second, 'shard', split_axis=0, concat_axis=0, tile...  11.8 us
    all_to_all x1, starting transfers between devices, on_device(): lax.all_to_all(context_first, 'shard', split_axis=0, concat_axis=0, tiled...  7.6 us
  transfers between devices with their start and end apart: 8, of which 5 were waited for; matrix products, arithmetic and copies ran while one was open for 9% of the time, Pallas kernels for 9%

profile of v2, /device:TPU:32, one launch (start us, length us, event | category | flops | bytes accessed | tf_op | source)
XLA Modules:
  0.0 251.1 jit_solution(14192254825614515770)
XLA Ops:
  7.3 0.9 reshape.157
  8.2 0.1 select_reduce_fusion
  8.3 1.1 collective-permute-done.w_other
  9.5 0.8 copy-done.5
  10.3 5.5 %request.1 = bf16[128,104,128]{2,1,0:T(8,128)(2,1)} custom-call(s32[128]{0:T(128)S(1)} %get-tuple-element.26.row_ids, s32[128]{0:T(128)S(1)} %get-tuple-element.25.list_ids, bf16[64,768]{1,0:T(8,128)(2,1)} %bitcast.28, bf16[768,384]{1,0:T(8,128)(2,1)} %w_own.1, bf16[768,384]{1,0:T(8,128)(2,1)} %copy-done.5), custom_call_target="tpu_custom_call" | custom-call | flops 75497472 | bytes 6291456 | tf_op jit(solution)/shard_map/request/pallas_call | solution.py:56
  15.8 15.5 %all-to-all-start = ((bf16[128,104,128]{2,1,0:T(8,128)(2,1)}), bf16[128,104,128]{2,1,0:T(8,128)(2,1)}, u32[]{:S(2)}, u32[]{:S(2)}) async-start(bf16[128,104,128]{2,1,0:T(8,128)(2,1)} %request.1), calls=%async_computation | async-start | bytes 6815744 | tf_op jit(solution)/shard_map/all_to_all | solution.py:332
  31.5 0.6 bitcast_convert_fusion
  32.2 3.6 %convolution_convert_fusion.2.values = bf16[32,40,384]{2,1,0:T(8,128)(2,1)} fusion(bf16[32,40,1024]{2,1,0:T(8,128)(2,1)S(1)} %copy-done, bf16[1024,384]{1,0:T(8,128)(2,1)} %param.17), kind=kOutput, calls=%fused_computation.2 | convolution fusion | flops 1007124480 | bytes 4390912 | tf_op jit(solution)/shard_map/spc,cd->spd/dot_general | solution.py:302
  35.8 3.7 %convolution_convert_fusion.3.keys = bf16[32,40,384]{2,1,0:T(8,128)(2,1)} fusion(bf16[32,40,1024]{2,1,0:T(8,128)(2,1)S(1)} %copy-done, bf16[1024,384]{1,0:T(8,128)(2,1)} %param.16), kind=kOutput, calls=%fused_computation.3 | convolution fusion | flops 1007124480 | bytes 4390912 | tf_op jit(solution)/shard_map/spc,cd->spd/dot_general | solution.py:302
  39.5 73.6 %all-to-all-done.got.codes = bf16[128,104,128]{2,1,0:T(8,128)(2,1)} async-done(((bf16[128,104,128]{2,1,0:T(8,128)(2,1)}), bf16[128,104,128]{2,1,0:T(8,128)(2,1)}, u32[]{:S(2)}, u32[]{:S(2)}) %all-to-all-start) | async-done | bytes 3407904 | tf_op jit(solution)/shard_map/all_to_all | solution.py:332
  113.2 10.0 %attend.2 = (bf16[128,48,128]{2,1,0:T(8,128)(2,1)}, s32[8,128]{1,0:T(8,128)S(1)}) custom-call(bf16[128,104,128]{2,1,0:T(8,128)(2,1)} %all-to-all-done.got.codes, bf16[128,104,128]{2,1,0:T(8,128)(2,1)} %all-to-all-done.got.codes, bf16[32,40,384]{2,1,0:T(8,128)(2,1)} %convolution_convert_fusion.3.keys, bf16[32,40,384]{2,1,0:T(8,128)(2,1)} %convolution_convert_fusion.2.values), custom_call_target="tpu_custom_call" | custom-call | flops 4294967296 | bytes 6291456 | tf_op jit(solution)/shard_map/attend/pallas_call | solution.py:174
  123.2 7.6 %all-to-all-start.1 = ((bf16[128,48,128]{2,1,0:T(8,128)(2,1)}), bf16[128,48,128]{2,1,0:T(8,128)(2,1)}, u32[]{:S(2)}, u32[]{:S(2)}) async-start(bf16[128,48,128]{2,1,0:T(8,128)(2,1)} %get-tuple-element.7), calls=%async_computation.1 | async-start | bytes 3145728 | tf_op jit(solution)/shard_map/all_to_all | solution.py:355
  130.8 0.3 collective-permute-start.1
  131.1 3.7 %convolution_convert_fusion.values = bf16[32,40,384]{2,1,0:T(8,128)(2,1)} fusion(bf16[32,40,1024]{2,1,0:T(8,128)(2,1)S(1)} %copy-done, bf16[1024,384]{1,0:T(8,128)(2,1)} %collective-permute-done.2), kind=kOutput, calls=%fused_computation | convolution fusion | flops 1007124480 | bytes 4390912 | tf_op jit(solution)/shard_map/spc,cd->spd/dot_general | solution.py:302
  134.8 2.5 convolution_convert_fusion.1.keys
  137.3 23.7 %all-gather.3.cloned.1.call-done = f32[128,4,768]{2,1,0:T(4,128)} async-done(((f32[1,4,768]{2,1,0:T(4,128)}), f32[128,4,768]{2,1,0:T(4,128)}) %all-gather.3.cloned.1.call-update) | async-done | bytes 1572880 | tf_op jit(solution)/shard_map/all_gather | solution.py:333
  161.0 2.8 %reshape.161.queries = f32[512,768]{1,0:T(8,128)} reshape(f32[128,4,768]{2,1,0:T(4,128)} %all-gather.3.cloned.1.call-done) | data formatting | bytes 3145728
  163.9 0.1 select_n.74.picked
  164.0 1.4 copy-done.1
  165.4 1.9 copy-done.3
  167.3 2.6 %index_stats.1 = f32[8,512]{1,0:T(8,128)S(1)} custom-call(f32[512,768]{1,0:T(8,128)S(1)} %copy-done.1, bf16[2048,768]{1,0:T(8,128)(2,1)S(1)} %copy-done.3, s32[1,512]{1,0:T(1,128)S(1)} %select_n.74.picked), custom_call_target="tpu_custom_call" | custom-call | flops 1610612736 | bytes 5242880 | tf_op jit(solution)/shard_map/index_stats/pallas_call | solution.py:220
  170.0 0.1 squeeze.15
  170.1 0.1 reduce_sum.29
  170.2 0.1 squeeze.13
  170.6 10.2 %attend.3 = (bf16[128,56,128]{2,1,0:T(8,128)(2,1)}, s32[8,128]{1,0:T(8,128)}) custom-call(bf16[128,104,128]{2,1,0:T(8,128)(2,1)} %all-to-all-done.got.codes, bf16[128,104,128]{2,1,0:T(8,128)(2,1)} %all-to-all-done.got.codes, bf16[32,40,384]{2,1,0:T(8,128)(2,1)} %convolution_convert_fusion.1.keys, bf16[32,40,384]{2,1,0:T(8,128)(2,1)} %convolution_convert_fusion.values, ...), custom_call_target="tpu_custom_call" | custom-call | flops 4294967296 | bytes 6291456 | tf_op jit(solution)/shard_map/attend/pallas_call | solution.py:174
  180.9 11.8 %all-to-all-start.2 = ((bf16[128,56,128]{2,1,0:T(8,128)(2,1)}), bf16[128,56,128]{2,1,0:T(8,128)(2,1)}, u32[]{:S(2)}, u32[]{:S(2)}) async-start(bf16[128,56,128]{2,1,0:T(8,128)(2,1)} %get-tuple-element.9), calls=%async_computation.2 | async-start | bytes 3670016 | tf_op jit(solution)/shard_map/all_to_all | solution.py:373
  193.0 2.0 collective-permute-done.3
  195.0 1.1 fusion.7
  196.1 2.4 maximum_select_fusion.w_out
  198.5 38.2 %all-to-all-done.2.second = bf16[128,56,128]{2,1,0:T(8,128)(2,1)} async-done(((bf16[128,56,128]{2,1,0:T(8,128)(2,1)}), bf16[128,56,128]{2,1,0:T(8,128)(2,1)}, u32[]{:S(2)}, u32[]{:S(2)}) %all-to-all-start.2) | async-done | bytes 1835040 | tf_op jit(solution)/shard_map/all_to_all | solution.py:373
  236.7 6.7 %finish.1 = (bf16[4,16,16,768]{3,2,1,0:T(8,128)(2,1)}, f32[8,128]{1,0:T(8,128)S(1)}) custom-call(s32[64]{0:T(128)S(1)} %get-tuple-element.24.shards, bf16[128,48,128]{2,1,0:T(8,128)(2,1)} %all-to-all-done.1.first, bf16[128,56,128]{2,1,0:T(8,128)(2,1)} %all-to-all-done.2.second, bf16[4,16,768]{2,1,0:T(8,128)(2,1)S(1)} %copy-done.2, ...), custom_call_target="tpu_custom_call" | custom-call | flops 1207959552 | bytes 7340032 | tf_op jit(solution)/shard_map/finish/pallas_call | solution.py:271
  243.6 0.7 subtract_add_fusion
  (38 shorter events, 1.2 us)
Async XLA Ops:
  7.2 25.1 %copy-start = (bf16[32,40,1024]{2,1,0:T(8,128)(2,1)S(1)}, bf16[32,40,1024]{2,1,0:T(8,128)(2,1)}, u32[]{:S(2)}) copy-start(bf16[32,40,1024]{2,1,0:T(8,128)(2,1)} %param.13) | copy-start | bytes 7864324
  7.2 2.3 collective-permute-start
  9.5 0.8 copy-start.5
  15.8 15.6 %copy-start.6 = (bf16[4,768]{1,0:T(4,128)(2,1)S(1)}, bf16[4,768]{1,0:T(4,128)(2,1)}, u32[]{:S(2)}) copy-start(bf16[4,768]{1,0:T(4,128)(2,1)} %param.10) | copy-start | bytes 18436
  15.8 97.3 %all-to-all-start = ((bf16[128,104,128]{2,1,0:T(8,128)(2,1)}), bf16[128,104,128]{2,1,0:T(8,128)(2,1)}, u32[]{:S(2)}, u32[]{:S(2)}) async-start(bf16[128,104,128]{2,1,0:T(8,128)(2,1)} %request.1), calls=%async_computation | async-start | bytes 6815744 | tf_op jit(solution)/shard_map/all_to_all | solution.py:332
  31.4 129.6 %all-gather.3.cloned.1.call-start = ((), (), s32[]{:S(2)}) async-start(), calls=%async_computation.3 | async-start | bytes 1585152 | tf_op jit(solution)/shard_map/all_gather | solution.py:333
  32.1 99.0 %collective-permute-start.2 = (bf16[1024,384]{1,0:T(8,128)(2,1)}, bf16[1024,384]{1,0:T(8,128)(2,1)}, u32[]{:S(2)}, u32[]{:S(2)}) collective-permute-start(bf16[1024,384]{1,0:T(8,128)(2,1)} %param.17), channel_id=1, source_target_pairs={{0,1},{1,0},{2,3},{3,2},{4,5},{5,4},{6,7},{7,6},{8,9},{9,8},{10,11... | collective-permute-start | bytes 2359304 | tf_op jit(solution)/shard_map/ppermute | solution.py:336
  123.2 57.8 %all-to-all-start.1 = ((bf16[128,48,128]{2,1,0:T(8,128)(2,1)}), bf16[128,48,128]{2,1,0:T(8,128)(2,1)}, u32[]{:S(2)}, u32[]{:S(2)}) async-start(bf16[128,48,128]{2,1,0:T(8,128)(2,1)} %get-tuple-element.7), calls=%async_computation.1 | async-start | bytes 3145728 | tf_op jit(solution)/shard_map/all_to_all | solution.py:355
  130.8 4.1 %collective-permute-start.1 = (bf16[1024,384]{1,0:T(8,128)(2,1)}, bf16[1024,384]{1,0:T(8,128)(2,1)S(1)}, u32[]{:S(2)}, u32[]{:S(2)}) collective-permute-start(bf16[1024,384]{1,0:T(8,128)(2,1)} %param.16), channel_id=1, source_target_pairs={{0,1},{1,0},{2,3},{3,2},{4,5},{5,4},{6,7},{7,6},{8,9},{9,8},{10,11... | collective-permute-start | bytes 2359304 | tf_op jit(solution)/shard_map/ppermute | solution.py:335
  164.0 1.4 copy-start.1
  165.4 1.9 copy-start.3
  180.9 11.9 %copy-start.4 = (bf16[768,384]{1,0:T(8,128)(2,1)S(1)}, bf16[768,384]{1,0:T(8,128)(2,1)}, u32[]{:S(2)}) copy-start(bf16[768,384]{1,0:T(8,128)(2,1)} %param.18) | copy-start | bytes 1769476
  180.9 12.0 %copy-start.7 = (f32[768]{0:T(1024)S(1)}, f32[768]{0:T(1024)}, u32[]{:S(2)}) copy-start(f32[768]{0:T(1024)} %param.19) | copy-start | bytes 9220
  180.9 55.8 %all-to-all-start.2 = ((bf16[128,56,128]{2,1,0:T(8,128)(2,1)}), bf16[128,56,128]{2,1,0:T(8,128)(2,1)}, u32[]{:S(2)}, u32[]{:S(2)}) async-start(bf16[128,56,128]{2,1,0:T(8,128)(2,1)} %get-tuple-element.9), calls=%async_computation.2 | async-start | bytes 3670016 | tf_op jit(solution)/shard_map/all_to_all | solution.py:373
  192.8 2.2 collective-permute-start.3
  193.0 43.7 %copy-start.2 = (bf16[4,16,768]{2,1,0:T(8,128)(2,1)S(1)}, bf16[4,16,768]{2,1,0:T(8,128)(2,1)}, u32[]{:S(2)}) copy-start(bf16[4,16,768]{2,1,0:T(8,128)(2,1)} %text.1) | copy-start | bytes 294916
Sparse Core Ops, SparseCore 0:
  35.6 125.3 all-gather.2

commit v3 on v2

v3 whole, which is shorter than its diff:
```python
import functools
import math

import jax
import jax.numpy as jnp
from jax import lax
from jax.experimental import pallas as pl
from jax.experimental.pallas import tpu as pltpu
from jax.sharding import PartitionSpec as P

HEADS = 12
SCALE = 100.0
EPSILON = 1e-06
LANES = 128
EXTRA = 8
UNROLL = 8
GRIDS = {128: (4, 8, 4), 8: (2, 2, 2)}
VMEM_LIMIT = 48 * 1024 * 1024


def row_of(shape, dim):
    return lax.broadcasted_iota(jnp.int32, shape, dim)


def in_hbm(array):
    return pltpu.with_memory_space_constraint(array, pltpu.HBM)


def project_kernel(text, queries, codes, w_own, w_other, out):
    rows = text.shape[0]
    half = w_own.shape[1]
    out[:rows, :half] = jnp.dot(text[...], w_own[...], preferred_element_type=jnp.float32).astype(jnp.bfloat16)
    out[:rows, half:] = jnp.dot(text[...], w_other[...], preferred_element_type=jnp.float32).astype(jnp.bfloat16)
    count, width = queries.shape
    pieces = [queries[...].astype(jnp.float32)]
    if count < EXTRA:
        pieces.append(jnp.zeros((EXTRA - count, width), jnp.float32))
    code = [jnp.broadcast_to(codes[i : i + 1, :].astype(jnp.float32), (EXTRA, LANES)) for i in range(2)]
    code.append(jnp.zeros((EXTRA, width - 2 * LANES), jnp.float32))
    pieces.append(jnp.concatenate(code, axis=1))
    out[rows:, :] = jnp.concatenate(pieces, axis=0).astype(jnp.bfloat16)


def project(text, queries, codes, w_own, w_other):
    width = w_own.shape[1] + w_other.shape[1]
    return pl.pallas_call(
        project_kernel,
        out_shape=jax.ShapeDtypeStruct((text.shape[0] + 2 * EXTRA, width), jnp.bfloat16),
        compiler_params=pltpu.CompilerParams(vmem_limit_bytes=VMEM_LIMIT),
        cost_estimate=pl.CostEstimate(
            flops=2 * text.shape[0] * text.shape[1] * width, bytes_accessed=2 << 20, transcendentals=0
        ),
        name="project",
    )(text, queries, codes, w_own, w_other)


def to_scalars(vectors, decoded, table, sem):
    decoded[...] = vectors
    copy = pltpu.make_async_copy(decoded, table, sem)
    copy.start()
    copy.wait()


def request_kernel(place, owners, out, decoded, table, shared, sem, *, grid_x, rows, query_count, top_count):
    step = pl.program_id(0)
    depth, height = owners.shape[:2]
    texts = height - 2 * EXTRA
    slot_rows = depth * rows
    shared_rows = shared.shape[0]
    tile_row = row_of((EXTRA, LANES), 0)

    @pl.when(step == 0)
    def _():
        found = [jnp.zeros((EXTRA, LANES), jnp.float32) for _ in range(2)]
        for z in range(depth):
            code = owners[z, texts + EXTRA :, :].astype(jnp.float32)
            found = [jnp.where(tile_row == z, code[:, i * LANES : (i + 1) * LANES], found[i]) for i in range(2)]
        to_scalars(jnp.concatenate(found, axis=0).astype(jnp.int32), decoded, table, sem)
        picked = [owners[z, texts : texts + EXTRA, :].astype(jnp.float32)[:query_count] for z in range(depth)]
        shared[...] = jnp.concatenate(picked, axis=0).astype(jnp.bfloat16)

    shard = (lax.div(step, grid_x) * depth + place[0]) * grid_x + lax.rem(step, grid_x)
    lane = row_of((EXTRA, LANES), 1)
    code = jnp.full((EXTRA, LANES), -1.0, jnp.float32)
    for z in range(depth):
        image, listed = table[z, shard], table[EXTRA + z, shard]
        first = lax.div(jnp.maximum(listed, 0), top_count) * rows
        out[0, z * rows : (z + 1) * rows, :] = owners[z, pl.ds(pl.multiple_of(first, rows), rows), :]
        code = jnp.where(lane == z, image.astype(jnp.float32), code)
        code = jnp.where(lane == EXTRA + z, listed.astype(jnp.float32), code)
    out[0, slot_rows : slot_rows + shared_rows, :] = shared[...]
    out[0, slot_rows + shared_rows :, :LANES] = code.astype(jnp.bfloat16)


def make_request(place, owners, grid_y, grid_x, rows, query_count, top_count):
    depth, height, width = owners.shape
    shared_rows = depth * query_count
    total = depth * rows + shared_rows + EXTRA
    return pl.pallas_call(
        functools.partial(
            request_kernel, grid_x=grid_x, rows=rows, query_count=query_count, top_count=top_count
        ),
        grid_spec=pltpu.PrefetchScalarGridSpec(
            num_scalar_prefetch=1,
            grid=(grid_y * grid_x,),
            in_specs=[pl.BlockSpec(owners.shape, lambda i, *_: (0, 0, 0))],
            out_specs=pl.BlockSpec((1, total, width), lambda i, *_: (i, 0, 0)),
            scratch_shapes=[
                pltpu.VMEM((2 * EXTRA, LANES), jnp.int32),
                pltpu.SMEM((2 * EXTRA, LANES), jnp.int32),
                pltpu.VMEM((shared_rows, width), jnp.bfloat16),
                pltpu.SemaphoreType.DMA,
            ],
        ),
        out_shape=pltpu.HBM((grid_y * grid_x, total, width), jnp.bfloat16),
        compiler_params=pltpu.CompilerParams(vmem_limit_bytes=VMEM_LIMIT),
        cost_estimate=pl.CostEstimate(flops=1 << 20, bytes_accessed=6 << 20, transcendentals=0),
        name="request",
    )(place, in_hbm(owners))


def index_stats(query, slab, picked, logits):
    count = query.shape[0]
    tile = min(256, slab.shape[0])
    peak = None
    for t in range(slab.shape[0] // tile):
        part = SCALE * lax.dot_general(
            slab[t * tile : (t + 1) * tile, :], query, (((1,), (1,)), ((), ())), preferred_element_type=jnp.float32
        )
        logits[t * tile : (t + 1) * tile, :] = part
        top = jnp.max(part, axis=0, keepdims=True)
        peak = top if peak is None else jnp.maximum(peak, top)
    total = jnp.zeros_like(peak)
    for t in range(slab.shape[0] // tile):
        total = total + jnp.sum(jnp.exp(logits[t * tile : (t + 1) * tile, :] - peak), axis=0, keepdims=True)
    chosen = row_of((tile, count), 0) == picked
    candidate = jnp.sum(jnp.where(chosen, logits[:tile, :], 0.0), axis=0, keepdims=True)
    return peak, total, candidate


def split_rows(exact):
    tile_row = row_of((EXTRA, LANES), 0)
    exact = jnp.broadcast_to(exact, (EXTRA, LANES))
    high = exact.astype(jnp.bfloat16).astype(jnp.float32)
    left = exact - high
    middle = left.astype(jnp.bfloat16).astype(jnp.float32)
    parts = jnp.where(tile_row == 0, high, jnp.where(tile_row == 1, middle, left - middle))
    return jnp.where(tile_row < 3, parts, 0.0)


def serve_kernel(
    got_hbm, slab_hbm, keys_hbm, values_hbm, out,
    got, slab, keys, values, logits, decoded, table, listed, sems, *, grid_x, depth, rows, query_count, top_count, head_size
):
    copies = [
        pltpu.make_async_copy(source, target, sems.at[i])
        for i, (source, target) in enumerate(
            [(got_hbm, got), (slab_hbm, slab), (keys_hbm, keys), (values_hbm, values)]
        )
    ]
    for copy in copies:
        copy.start()
    sources, height = got.shape[:2]
    slots = sources * depth
    columns = keys.shape[2]
    slot_rows = depth * rows
    shared_rows = depth * query_count
    body = columns // LANES * rows
    per_chunk = LANES // query_count
    lane = row_of((EXTRA, LANES), 1)
    tile_row = row_of((EXTRA, LANES), 0)

    copies[0].wait()
    found = [jnp.zeros((EXTRA, LANES), jnp.float32) for _ in range(-(-sources // EXTRA))]
    for source in range(sources):
        code = got[source, slot_rows + shared_rows :, :LANES].astype(jnp.float32)
        found[source // EXTRA] = jnp.where(tile_row == source % EXTRA, code, found[source // EXTRA])
    found = found[0] if len(found) == 1 else jnp.concatenate(found, axis=0)
    to_scalars(found.astype(jnp.int32), decoded, table, sems.at[4])

    count = 0
    chunks = [jnp.full((EXTRA, LANES), -1, jnp.int32) for _ in range(-(-slots // per_chunk))]
    for slot in range(slots):
        image, entry = table[slot // depth, slot % depth], table[slot // depth, EXTRA + slot % depth]
        query = lax.div(jnp.maximum(entry, 0), top_count)
        at = slot % per_chunk * query_count + query
        chunks[slot // per_chunk] = jnp.where(lane == at, image, chunks[slot // per_chunk])
        listed[count] = slot
        count = count + jnp.where(image >= 0, 1, 0)
    last = listed[jnp.maximum(count - 1, 0)]
    for g in range(UNROLL):
        listed[count + g] = last

    queries = jnp.concatenate([got[source, slot_rows : slot_rows + shared_rows, :] for source in range(sources)], axis=0)
    missing = len(chunks) * LANES - queries.shape[0]
    if missing:
        queries = jnp.concatenate([queries, jnp.zeros((missing, queries.shape[1]), queries.dtype)], axis=0)
    copies[1].wait()
    stats = index_stats(queries, slab, jnp.concatenate([chunk[:1] for chunk in chunks], axis=1), logits)
    for c in range(len(chunks)):
        tiles = [split_rows(stat[:, c * LANES : (c + 1) * LANES]) for stat in stats]
        tiles = [tiles[0], pltpu.roll(tiles[1], query_count, 1), pltpu.roll(tiles[2], 2 * query_count, 1)]
        for slot in range(c * per_chunk, min((c + 1) * per_chunk, slots)):
            source, z = slot // depth, slot % depth
            at = slot % per_chunk
            owner = (source // grid_x * depth + z) * grid_x + source % grid_x
            place = lane // query_count
            tile = jnp.where(place == at, tiles[0], jnp.where(place == (at + 1) % per_chunk, tiles[1], tiles[2]))
            out[owner, body:, :] = tile.astype(jnp.bfloat16)

    copies[2].wait()
    copies[3].wait()
    spans = []
    at = 0
    while at < columns:
        width = min(2 * LANES, columns - at)
        lane_head = row_of((rows, width), 1) // head_size
        spans.append((at, width, [jnp.where(lane_head == h, 1.0, 0.0) for h in range(width // head_size)]))
        at += width

    def group(index, carry):
        chosen = [listed[index * UNROLL + g] for g in range(UNROLL)]
        places = [(lax.div(slot, depth), lax.rem(slot, depth)) for slot in chosen]
        images = [table[source, z] for source, z in places]
        owners = [
            (lax.div(source, grid_x) * depth + z) * grid_x + lax.rem(source, grid_x) for source, z in places
        ]
        work = [(g, span) for g in range(UNROLL) for span in spans]
        scores = []
        for g, (at, width, masks) in work:
            source, z = places[g]
            query = got[source, pl.ds(pl.multiple_of(z * rows, rows), rows), at : at + width]
            spread = jnp.concatenate([query * mask.astype(query.dtype) for mask in masks], axis=0)
            scores.append(
                lax.dot_general(
                    spread,
                    keys[images[g], :, at : at + width],
                    (((1,), (1,)), ((), ())),
                    preferred_element_type=jnp.float32,
                )
            )
        scores = [score * head_size ** (-0.5) for score in scores]
        highest = [jnp.max(score, axis=-1, keepdims=True) for score in scores]
        powers = [jnp.exp(score - top) for score, top in zip(scores, highest)]
        totals = [jnp.sum(power, axis=-1, keepdims=True) for power in powers]
        weights = [(power / total).astype(jnp.bfloat16) for power, total in zip(powers, totals)]
        mixed = [
            jnp.dot(weight, values[images[g], :, at : at + width], preferred_element_type=jnp.float32)
            for weight, (g, (at, width, _)) in zip(weights, work)
        ]
        for mix, (g, (at, width, masks)) in zip(mixed, work):
            context = mix[:rows] * masks[0]
            for h in range(1, len(masks)):
                context = context + mix[h * rows : (h + 1) * rows] * masks[h]
            context = context.astype(jnp.bfloat16)
            for c in range(width // LANES):
                out[owners[g], (at // LANES + c) * rows : (at // LANES + c + 1) * rows, :] = context[
                    :, c * LANES : (c + 1) * LANES
                ]
        return carry

    lax.fori_loop(0, lax.div(count + UNROLL - 1, UNROLL), group, 0)


def serve(got, slab, keys, values, grid_x, depth, rows, query_count, top_count, head_size):
    sources = got.shape[0]
    slots = sources * depth
    body = keys.shape[2] // LANES * rows
    lanes = -(-slots * query_count // LANES) * LANES
    operands = [got, slab, keys, values]
    codes = (-(-sources // EXTRA) * EXTRA, LANES)
    return pl.pallas_call(
        functools.partial(
            serve_kernel,
            grid_x=grid_x,
            depth=depth,
            rows=rows,
            query_count=query_count,
            top_count=top_count,
            head_size=head_size,
        ),
        grid=(1,),
        in_specs=[pl.BlockSpec(memory_space=pltpu.HBM)] * 4,
        out_specs=pl.BlockSpec((slots, body + EXTRA, LANES), lambda i: (0, 0, 0)),
        scratch_shapes=[pltpu.VMEM(a.shape, a.dtype) for a in operands]
        + [
            pltpu.VMEM((slab.shape[0], lanes), jnp.float32),
            pltpu.VMEM(codes, jnp.int32),
            pltpu.SMEM(codes, jnp.int32),
            pltpu.SMEM((slots + UNROLL,), jnp.int32),
            pltpu.SemaphoreType.DMA((5,)),
        ],
        out_shape=pltpu.HBM((slots, body + EXTRA, LANES), jnp.bfloat16),
        compiler_params=pltpu.CompilerParams(vmem_limit_bytes=VMEM_LIMIT),
        cost_estimate=pl.CostEstimate(flops=8 << 30, bytes_accessed=14 << 20, transcendentals=2 << 20),
        name="serve",
    )(*[in_hbm(a) for a in operands])


def finish_kernel(
    shards, place, back, text, w_out, gain, found, out, exact, normalizers, gathered, *, top_count, query_count, shift
):
    step = pl.program_id(0)
    rows = text.shape[1]
    body = back.shape[1] - EXTRA

    @pl.when(step == 0)
    def _():
        sent = back[:, body:, :].astype(jnp.float32)
        joined = jnp.sum(jnp.where(row_of(sent.shape, 1) < 3, sent, 0.0), axis=1)
        joined = pltpu.roll(joined, lax.rem(LANES - place[0] * query_count, LANES), 1)
        exact[...] = joined
        peak = jnp.max(joined, axis=0, keepdims=True)
        scaled = jnp.exp(joined - peak) * pltpu.roll(joined, LANES - query_count, 1)
        total = jnp.sum(scaled, axis=0, keepdims=True)
        total = jnp.where(row_of(total.shape, 1) < query_count, total, 1.0)
        normalizers[...] = jnp.broadcast_to(peak + jnp.log(total), normalizers.shape)

    picked = jnp.concatenate([exact[pl.ds(shards[step * top_count + k], 1), :] for k in range(top_count)], axis=0)
    lane = row_of(picked.shape, 1)
    candidate = jnp.sum(jnp.where(lane == 2 * query_count + step, picked, 0.0), axis=1, keepdims=True)
    normalizer = jnp.sum(jnp.where(lane[:1] == step, normalizers[:1, :], 0.0), axis=1, keepdims=True)
    result = candidate - normalizer + shift
    result = jnp.sum(jnp.where(lane == row_of(picked.shape, 0), result, 0.0), axis=0, keepdims=True)
    found[pl.ds(step, 1), :] = result[:, :top_count]

    for k in range(top_count):
        shard = shards[step * top_count + k]
        for j in range(body // rows):
            gathered[k * rows : (k + 1) * rows, j * LANES : (j + 1) * LANES] = back[shard, j * rows : (j + 1) * rows, :]
    mixed = jnp.dot(gathered[...], w_out[...], preferred_element_type=jnp.float32)
    width = mixed.shape[1]
    summed = mixed.reshape(top_count, rows, width) + text[...].astype(jnp.float32)
    mean = jnp.mean(summed, axis=-1, keepdims=True)
    centred = summed - mean
    variance = jnp.mean(centred * centred, axis=-1, keepdims=True)
    normed = centred * lax.rsqrt(variance + EPSILON) * gain[...].reshape(1, 1, width)
    out[...] = normed.astype(jnp.bfloat16).reshape(out.shape)


def finish(shards, place, back, text, w_out, gain, top_count, shift):
    query_count, rows, width = text.shape
    full = lambda a: pl.BlockSpec(a.shape, lambda i, *_: (0,) * a.ndim)
    return pl.pallas_call(
        functools.partial(finish_kernel, top_count=top_count, query_count=query_count, shift=shift),
        grid_spec=pltpu.PrefetchScalarGridSpec(
            num_scalar_prefetch=2,
            grid=(query_count,),
            in_specs=[
                full(back),
                pl.BlockSpec((1, rows, width), lambda i, *_: (i, 0, 0)),
                full(w_out),
                full(gain),
            ],
            out_specs=[
                pl.BlockSpec((query_count, top_count), lambda i, *_: (0, 0)),
                pl.BlockSpec((1, top_count, rows, width), lambda i, *_: (i, 0, 0, 0)),
            ],
            scratch_shapes=[
                pltpu.VMEM((back.shape[0], LANES), jnp.float32),
                pltpu.VMEM((EXTRA, LANES), jnp.float32),
                pltpu.VMEM((top_count * rows, width), jnp.bfloat16),
            ],
        ),
        out_shape=[
            jax.ShapeDtypeStruct((query_count, top_count), jnp.float32),
            jax.ShapeDtypeStruct((query_count, top_count, rows, width), jnp.bfloat16),
        ],
        compiler_params=pltpu.CompilerParams(vmem_limit_bytes=VMEM_LIMIT),
        cost_estimate=pl.CostEstimate(
            flops=2 * query_count * top_count * rows * width * width, bytes_accessed=7 << 20, transcendentals=0
        ),
        name="finish",
    )(shards, place, in_hbm(back), text, in_hbm(w_out), gain)


def project_rows(rows_in, weight):
    return jnp.einsum("spc,cd->spd", rows_in, weight, preferred_element_type=jnp.float32).astype(jnp.bfloat16)


def on_device(queries, slab, cand_ids, patches, text_states, w_query, w_key, w_value, w_out, norm_gain):
    shard_count = lax.axis_size("shard")
    shard_here = lax.axis_index("shard")
    core = lax.axis_index("rep")
    grid_y, depth, grid_x = GRIDS[shard_count]
    query_count = queries.shape[0]
    slab_count = slab.shape[0]
    top_count = cand_ids.shape[1]
    list_length = query_count * top_count
    text_count, model_width = text_states.shape[1:]
    head_size = model_width // HEADS
    here_x, here_z, here_y = shard_here % grid_x, shard_here // grid_x % depth, shard_here // (grid_x * depth)
    columns = [
        [(y * depth + z) * grid_x + x for z in range(depth)] for y in range(grid_y) for x in range(grid_x)
    ]
    planes = [
        [(y * depth + z) * grid_x + x for y in range(grid_y) for x in range(grid_x)] for z in range(depth)
    ]
    swap = [(0, 1), (1, 0)]
    w_query_other = lax.ppermute(w_query, "rep", swap)

    own_list = cand_ids.reshape(list_length)
    own_anchor = own_list // slab_count
    here = own_anchor[None, :] == row_of((LANES, 1), 0)
    row_ids = jnp.sum(jnp.where(here, own_list[None, :] % slab_count + 1, 0), axis=1) - 1
    list_ids = jnp.sum(jnp.where(here, row_of((1, list_length), 1) + 1, 0), axis=1) - 1

    sent = project(
        text_states.reshape(query_count * text_count, model_width),
        queries,
        jnp.stack([row_ids, list_ids]),
        w_query,
        w_query_other,
    )
    owners = lax.all_gather(sent, "shard", axis=0, tiled=True, axis_index_groups=columns)
    request = make_request(
        here_z.reshape(1),
        owners.reshape(depth, sent.shape[0], model_width),
        grid_y,
        grid_x,
        text_count,
        query_count,
        top_count,
    )
    got = lax.all_to_all(request, "shard", split_axis=0, concat_axis=0, tiled=True, axis_index_groups=planes)

    keys = project_rows(patches, jnp.concatenate([w_key, lax.ppermute(w_key, "rep", swap)], axis=1))
    values = project_rows(patches, jnp.concatenate([w_value, lax.ppermute(w_value, "rep", swap)], axis=1))
    w_out_other = lax.ppermute(w_out, "rep", swap)
    half = model_width // 2
    w_out_whole = jnp.where(
        core == 0,
        jnp.concatenate([w_out, w_out_other], axis=1),
        jnp.concatenate(
            [
                jnp.concatenate([w_out_other[half:], w_out[half:]], axis=1),
                jnp.concatenate([w_out_other[:half], w_out[:half]], axis=1),
            ],
            axis=0,
        ),
    )

    context = serve(got, slab, keys, values, grid_x, depth, text_count, query_count, top_count, head_size)
    back = lax.all_to_all(context, "shard", split_axis=0, concat_axis=0, tiled=True)

    place = ((here_y * grid_x + here_x) * depth + here_z) % (LANES // query_count)
    retrieval, attended = finish(
        own_anchor,
        place.reshape(1),
        back,
        text_states,
        w_out_whole,
        norm_gain.reshape(1, model_width),
        top_count,
        math.log(slab_count * shard_count),
    )
    return (retrieval, attended)


def solution(mesh):
    in_specs = (
        P(("shard", "rep"), None),
        P("shard", None),
        P(("shard", "rep"), None),
        P("shard", None, None),
        P(("shard", "rep"), None, None),
        P(None, "rep"),
        P(None, "rep"),
        P(None, "rep"),
        P(None, "rep"),
        P(),
    )
    out_specs = (P(("shard", "rep"), None), P(("shard", "rep"), None, None, None))
    return jax.shard_map(
        on_device, mesh=mesh, in_specs=in_specs, out_specs=out_specs, check_vma=False
    )
```

time: 253 us -> 214 us (0.85)
  blocking collectives: 0 us -> 31.3 us
  waiting for transfers between devices: 139 us -> 118 us
  starting transfers between devices: 35.6 us -> 17.3 us
  between operations: 14.3 us -> 0.91 us
  matrix products: 13.5 us -> 7.06 us
  local copies, waits for them, and re-layouts: 9.72 us -> 4.78 us
  Pallas kernels: 35.1 us -> 30.3 us
    all_gather x0 -> x1, blocking collectives: none -> 31.3 us  [on_device(): lax.all_gather(sent, 'shard', axis=0, tiled=True, axis_index_groups=columns)]
    all_gather x1 -> x0, waiting for transfers between devices: 23.7 us -> none  [on_device(): lax.all_gather(queries.astype(jnp.float32), 'shard', axis=0, tiled=True)]
    all_to_all x3 -> x2, starting transfers between devices: 35 us -> 16.5 us  [the longest x1 9.27 us: on_device(): lax.all_to_all(context, 'shard', split_axis=0, concat_axis=0, tiled=True)]
    dot_general x4 -> x2, matrix products: 13.5 us -> 7.06 us  [project_rows(): jnp.einsum('spc,cd->spd', rows_in, weight, preferred_element_type=jnp.flo...]
    pallas_call x4 -> x3, Pallas kernels: 28.4 us -> 23.5 us  [the longest x1 15.3 us: serve(): pl.pallas_call(functools.partial(serve_kernel, grid_x=grid_x, depth=depth...]
    unnamed x17 -> x18, local copies, waits for them, and re-layouts: 6.92 us -> 2.69 us
    all_to_all x3 -> x2, waiting for transfers between devices: 112 us -> 113 us  [the longest x1 73.9 us: on_device(): lax.all_to_all(context, 'shard', split_axis=0, concat_axis=0, tiled=True)]
  transfers between devices with their start and end apart: 8 -> 6, of which waited for: 5 -> 5; matrix products, arithmetic and copies ran while one was open for 9% -> 6% of each run, Pallas kernels for 9% -> 0%
where the time goes in v3:
time: 214 us; the launch traced here: 213 us
  waiting for transfers between devices  118 us (55%)
  blocking collectives  31.3 us (15%)
  Pallas kernels  30.3 us (14%)
  starting transfers between devices  17.3 us (8%)
  matrix products  7.06 us (3%)
  local copies, waits for them, and re-layouts  4.78 us (2%)
  other arithmetic  2.64 us (1%)
    all_to_all x1, waiting for transfers between devices, on_device(): lax.all_to_all(context, 'shard', split_axis=0, concat_axis=0, tiled=True)  73.9 us
    all_to_all x1, waiting for transfers between devices, on_device(): lax.all_to_all(request, 'shard', split_axis=0, concat_axis=0, tiled=True,...  39.4 us
    all_gather x1, blocking collectives, on_device(): lax.all_gather(sent, 'shard', axis=0, tiled=True, axis_index_groups=columns)  31.3 us
    pallas_call x1, Pallas kernels, serve(): pl.pallas_call(functools.partial(serve_kernel, grid_x=grid_x, depth=depth...  15.3 us
    all_to_all x1, starting transfers between devices, on_device(): lax.all_to_all(context, 'shard', split_axis=0, concat_axis=0, tiled=True)  9.27 us
    pallas_call x1, Pallas kernels, make_request(): pl.pallas_call(functools.partial(request_kernel, grid_x=grid_x, rows=rows...  7.96 us
    all_to_all x1, starting transfers between devices, on_device(): lax.all_to_all(request, 'shard', split_axis=0, concat_axis=0, tiled=True,...  7.22 us
    dot_general x2, matrix products, project_rows(): jnp.einsum('spc,cd->spd', rows_in, weight, preferred_element_type=jnp.flo...  7.06 us
  transfers between devices with their start and end apart: 6, of which 5 were waited for; matrix products, arithmetic and copies ran while one was open for 6% of the time, Pallas kernels for 0%

profile of v3, /device:TPU:32, one launch (start us, length us, event | category | flops | bytes accessed | tf_op | source)
XLA Modules:
  0.0 212.6 jit_solution(14282572511075812485)
XLA Ops:
  0.6 0.0 copy-start
  0.6 0.1 collective-permute-start
  0.7 0.9 reshape.103
  1.7 0.1 select_reduce_fusion.1
  1.9 1.1 collective-permute-done.w_other
  2.9 1.1 copy-done.1
  4.0 0.9 copy-done.2
  4.9 0.7 copy-done.4
  5.6 0.3 project.1
  5.9 31.3 %all_gather.3 = bf16[640,768]{1,0:T(8,128)(2,1)} all-gather(bf16[80,768]{1,0:T(8,128)(2,1)S(1)} %project.1), channel_id=1, replica_groups={{0,8,16,24,32,40,48,56},{2,10,18,26,34,42,50,58},{4,12,20,28,36,44,52,6..., dimensions={0}, use_global_device_ids=true | all-gather | bytes 1105920 | tf_op jit(solution)/shard_map/all_gather | solution.py:415
  37.2 8.0 %request.1 = bf16[16,168,768]{2,1,0:T(8,128)(2,1)} custom-call(s32[1]{0:T(128)} %bitcast.1.place, bf16[8,80,768]{2,1,0:T(8,128)(2,1)} %bitcast.21), custom_call_target="tpu_custom_call" | custom-call | flops 1048576 | bytes 6291456 | tf_op jit(solution)/shard_map/request/pallas_call | solution.py:99
  45.2 0.0 copy-start.7
  45.2 7.2 %all-to-all-start = ((bf16[16,168,768]{2,1,0:T(8,128)(2,1)}), bf16[16,168,768]{2,1,0:T(8,128)(2,1)}, u32[]{:S(2)}, u32[]{:S(2)}) async-start(bf16[16,168,768]{2,1,0:T(8,128)(2,1)} %request.1), calls=%async_computation | async-start | bytes 8257536 | tf_op jit(solution)/shard_map/all_to_all | solution.py:425
  52.5 0.0 copy-start.8
  52.5 0.1 collective-permute-start.1
  52.6 0.5 collective-permute-start.2
  53.1 1.9 collective-permute-done.1
  55.0 3.6 %convert_bitcast_fusion.1.keys_hbm = bf16[32,40,768]{2,1,0:T(8,128)(2,1)} fusion(bf16[32,40,1024]{2,1,0:T(8,128)(2,1)S(1)} %copy-done, bf16[1024,384]{1,0:T(8,128)(2,1)S(1)} %collective-permute-done.1, bf16[1024,384]{1,0:T(8,128)(2,1)S(1)} %copy-done.7), kind=kOutput, calls=%fused_computation.1 | convolution fusion | flops 2017394688 | bytes 6160384 | tf_op jit(solution)/shard_map/spc,cd->spd/dot_general | solution.py:378
  58.5 3.5 %convert_bitcast_fusion.values_hbm = bf16[32,40,768]{2,1,0:T(8,128)(2,1)} fusion(bf16[32,40,1024]{2,1,0:T(8,128)(2,1)S(1)} %copy-done, bf16[1024,384]{1,0:T(8,128)(2,1)S(1)} %collective-permute-done.2, bf16[1024,384]{1,0:T(8,128)(2,1)S(1)} %copy-done.8), kind=kOutput, calls=%fused_computation | convolution fusion | flops 2017394688 | bytes 6160384 | tf_op jit(solution)/shard_map/spc,cd->spd/dot_general | solution.py:378
  62.0 39.4 %all-to-all-done.got_hbm = bf16[16,168,768]{2,1,0:T(8,128)(2,1)} async-done(((bf16[16,168,768]{2,1,0:T(8,128)(2,1)}), bf16[16,168,768]{2,1,0:T(8,128)(2,1)}, u32[]{:S(2)}, u32[]{:S(2)}) %all-to-all-start) | async-done | bytes 4128800 | tf_op jit(solution)/shard_map/all_to_all | solution.py:425
  101.4 15.3 %serve.1 = bf16[128,104,128]{2,1,0:T(8,128)(2,1)} custom-call(bf16[16,168,768]{2,1,0:T(8,128)(2,1)} %all-to-all-done.got_hbm, bf16[2048,768]{1,0:T(8,128)(2,1)} %slab_hbm.1, bf16[32,40,768]{2,1,0:T(8,128)(2,1)} %convert_bitcast_fusion.1.keys_hbm, bf16[32,40,768]{2,1,0:T(8,128)(2,1)} %convert_bitcast_fusion.values_hbm), custom_call_target="tpu_custom_call" | custom-call | flops 8589934592 | bytes 14680064 | tf_op jit(solution)/shard_map/serve/pallas_call | solution.py:272
  116.7 0.0 copy-start.5
  116.7 0.0 copy-start.6
  116.7 9.3 %all-to-all-start.1 = ((bf16[128,104,128]{2,1,0:T(8,128)(2,1)}), bf16[128,104,128]{2,1,0:T(8,128)(2,1)}, u32[]{:S(2)}, u32[]{:S(2)}) async-start(bf16[128,104,128]{2,1,0:T(8,128)(2,1)} %serve.1), calls=%async_computation.1 | async-start | bytes 6815744 | tf_op jit(solution)/shard_map/all_to_all | solution.py:444
  126.0 0.1 collective-permute-start.3
  126.2 0.1 fusion.8
  126.2 0.0 copy-start.3
  126.3 2.0 collective-permute-done.3
  128.2 1.1 fusion.7
  129.3 2.5 %maximum_select_fusion.w_out = bf16[768,768]{1,0:T(8,128)(2,1)} fusion(bf16[768,384]{1,0:T(8,128)(2,1)} %collective-permute-done.3, bf16[768,384]{1,0:T(8,128)(2,1)S(1)} %copy-done.5, bf16[384,384]{1,0:T(8,128)(2,1)S(1)} %get-tuple-element.7, bf16[384,384]{1,0:T(8,128)(2,1)S(1)} %get-tuple-element.5, bf16[384,384]{1,0:T(8,128)(2,1)S(1)} %get-tuple-element.6, ...), kind=kLoop, calls=%fused_computation.8 | loop fusion | flops 7667712 | bytes 3538945 | tf_op jit(solution)/shard_map/jit(_where)/select_n | solution.py:431
  131.8 73.9 %all-to-all-done.1.back = bf16[128,104,128]{2,1,0:T(8,128)(2,1)} async-done(((bf16[128,104,128]{2,1,0:T(8,128)(2,1)}), bf16[128,104,128]{2,1,0:T(8,128)(2,1)}, u32[]{:S(2)}, u32[]{:S(2)}) %all-to-all-start.1) | async-done | bytes 3407904 | tf_op jit(solution)/shard_map/all_to_all | solution.py:444
  205.8 6.8 %finish.1 = (f32[4,16]{1,0:T(4,128)}, bf16[4,16,16,768]{3,2,1,0:T(8,128)(2,1)}) custom-call(s32[64]{0:T(128)S(1)} %get-tuple-element.9.shards, s32[1]{0:T(128)} %bitcast.place, bf16[128,104,128]{2,1,0:T(8,128)(2,1)} %all-to-all-done.1.back, bf16[4,16,768]{2,1,0:T(8,128)(2,1)S(1)} %copy-done.3, bf16[768,768]{1,0:T(8,128)(2,1)} %maximum_select_fusion.w_out, ...), custom_call_target="tpu_custom_call" | custom-call | flops 1207959552 | bytes 7340032 | tf_op jit(solution)/shard_map/finish/pallas_call | solution.py:344
  (15 shorter events, 0.1 us)
Async XLA Ops:
  0.6 54.3 %copy-start = (bf16[32,40,1024]{2,1,0:T(8,128)(2,1)S(1)}, bf16[32,40,1024]{2,1,0:T(8,128)(2,1)}, u32[]{:S(2)}) copy-start(bf16[32,40,1024]{2,1,0:T(8,128)(2,1)} %param.13) | copy-start | bytes 7864324
  0.6 2.3 %collective-permute-start = (bf16[768,384]{1,0:T(8,128)(2,1)}, bf16[768,384]{1,0:T(8,128)(2,1)S(1)}, u32[]{:S(2)}, u32[]{:S(2)}) collective-permute-start(bf16[768,384]{1,0:T(8,128)(2,1)} %w_own.1), channel_id=1, source_target_pairs={{0,1},{1,0},{2,3},{3,2},{4,5},{5,4},{6,7},{7,6},{8,9},{9,8},{10,11... | collective-permute-start | bytes 1769480 | tf_op jit(solution)/shard_map/ppermute | solution.py:400
  2.9 1.1 copy-start.1
  4.0 0.9 copy-start.2
  4.9 0.7 copy-start.4
  45.2 7.2 %copy-start.7 = (bf16[1024,384]{1,0:T(8,128)(2,1)S(1)}, bf16[1024,384]{1,0:T(8,128)(2,1)}, u32[]{:S(2)}) copy-start(bf16[1024,384]{1,0:T(8,128)(2,1)} %param.16) | copy-start | bytes 2359300
  45.2 56.2 %all-to-all-start = ((bf16[16,168,768]{2,1,0:T(8,128)(2,1)}), bf16[16,168,768]{2,1,0:T(8,128)(2,1)}, u32[]{:S(2)}, u32[]{:S(2)}) async-start(bf16[16,168,768]{2,1,0:T(8,128)(2,1)} %request.1), calls=%async_computation | async-start | bytes 8257536 | tf_op jit(solution)/shard_map/all_to_all | solution.py:425
  52.5 6.1 %copy-start.8 = (bf16[1024,384]{1,0:T(8,128)(2,1)S(1)}, bf16[1024,384]{1,0:T(8,128)(2,1)}, u32[]{:S(2)}) copy-start(bf16[1024,384]{1,0:T(8,128)(2,1)} %param.17) | copy-start | bytes 2359300
  52.5 2.5 %collective-permute-start.1 = (bf16[1024,384]{1,0:T(8,128)(2,1)S(1)}, bf16[1024,384]{1,0:T(8,128)(2,1)S(1)}, u32[]{:S(2)}, u32[]{:S(2)}) collective-permute-start(bf16[1024,384]{1,0:T(8,128)(2,1)S(1)} %copy-done.7), channel_id=1, source_target_pairs={{0,1},{1,0},{2,3},{3,2},{4,5},{5,4},{6,7},{7,6},{8,9},{9,8},{10,11... | collective-permute-start | bytes 2359304 | tf_op jit(solution)/shard_map/ppermute | solution.py:427
  52.6 6.0 %collective-permute-start.2 = (bf16[1024,384]{1,0:T(8,128)(2,1)}, bf16[1024,384]{1,0:T(8,128)(2,1)S(1)}, u32[]{:S(2)}, u32[]{:S(2)}) collective-permute-start(bf16[1024,384]{1,0:T(8,128)(2,1)} %param.17), channel_id=1, source_target_pairs={{0,1},{1,0},{2,3},{3,2},{4,5},{5,4},{6,7},{7,6},{8,9},{9,8},{10,11... | collective-permute-start | bytes 2359304 | tf_op jit(solution)/shard_map/ppermute | solution.py:428
  116.7 9.3 %copy-start.5 = (bf16[768,384]{1,0:T(8,128)(2,1)S(1)}, bf16[768,384]{1,0:T(8,128)(2,1)}, u32[]{:S(2)}) copy-start(bf16[768,384]{1,0:T(8,128)(2,1)} %param.18) | copy-start | bytes 1769476
  116.7 9.5 %copy-start.6 = (f32[768]{0:T(1024)S(1)}, f32[768]{0:T(1024)}, u32[]{:S(2)}) copy-start(f32[768]{0:T(1024)} %param.19) | copy-start | bytes 9220
  116.7 89.1 %all-to-all-start.1 = ((bf16[128,104,128]{2,1,0:T(8,128)(2,1)}), bf16[128,104,128]{2,1,0:T(8,128)(2,1)}, u32[]{:S(2)}, u32[]{:S(2)}) async-start(bf16[128,104,128]{2,1,0:T(8,128)(2,1)} %serve.1), calls=%async_computation.1 | async-start | bytes 6815744 | tf_op jit(solution)/shard_map/all_to_all | solution.py:444
  126.0 2.2 %collective-permute-start.3 = (bf16[768,384]{1,0:T(8,128)(2,1)S(1)}, bf16[768,384]{1,0:T(8,128)(2,1)}, u32[]{:S(2)}, u32[]{:S(2)}) collective-permute-start(bf16[768,384]{1,0:T(8,128)(2,1)S(1)} %copy-done.5), channel_id=1, source_target_pairs={{0,1},{1,0},{2,3},{3,2},{4,5},{5,4},{6,7},{7,6},{8,9},{9,8},{10,11... | collective-permute-start | bytes 1769480 | tf_op jit(solution)/shard_map/ppermute | solution.py:429
  126.2 79.5 %copy-start.3 = (bf16[4,16,768]{2,1,0:T(8,128)(2,1)S(1)}, bf16[4,16,768]{2,1,0:T(8,128)(2,1)}, u32[]{:S(2)}) copy-start(bf16[4,16,768]{2,1,0:T(8,128)(2,1)} %text.1) | copy-start | bytes 294916

commit v4 on v3

--- a/solution.py
+++ b/solution.py
@@ -13,7 +13,7 @@
 EPSILON = 1e-06
 LANES = 128
 EXTRA = 8
-UNROLL = 8
+UNROLL = 16
 GRIDS = {128: (4, 8, 4), 8: (2, 2, 2)}
 VMEM_LIMIT = 48 * 1024 * 1024
 
@@ -26,32 +26,47 @@
     return pltpu.with_memory_space_constraint(array, pltpu.HBM)
 
 
-def project_kernel(text, queries, codes, w_own, w_other, out):
+def project_kernel(ids, text, queries, w_own, w_other, out, *, slab_count):
     rows = text.shape[0]
     half = w_own.shape[1]
-    out[:rows, :half] = jnp.dot(text[...], w_own[...], preferred_element_type=jnp.float32).astype(jnp.bfloat16)
-    out[:rows, half:] = jnp.dot(text[...], w_other[...], preferred_element_type=jnp.float32).astype(jnp.bfloat16)
     count, width = queries.shape
+    lane = row_of((EXTRA, LANES), 1)
+    image = jnp.full((EXTRA, LANES), -1, jnp.int32)
+    listed = image
+    for entry in range(ids.shape[0] * ids.shape[1]):
+        row = ids[entry // ids.shape[1], entry % ids.shape[1]]
+        here = lane == lax.div(row, slab_count)
+        image = jnp.where(here, lax.rem(row, slab_count), image)
+        listed = jnp.where(here, entry, listed)
     pieces = [queries[...].astype(jnp.float32)]
     if count < EXTRA:
         pieces.append(jnp.zeros((EXTRA - count, width), jnp.float32))
-    code = [jnp.broadcast_to(codes[i : i + 1, :].astype(jnp.float32), (EXTRA, LANES)) for i in range(2)]
+    code = [image.astype(jnp.float32), listed.astype(jnp.float32)]
     code.append(jnp.zeros((EXTRA, width - 2 * LANES), jnp.float32))
     pieces.append(jnp.concatenate(code, axis=1))
     out[rows:, :] = jnp.concatenate(pieces, axis=0).astype(jnp.bfloat16)
-
-
-def project(text, queries, codes, w_own, w_other):
+    out[:rows, :half] = jnp.dot(text[...], w_own[...], preferred_element_type=jnp.float32).astype(jnp.bfloat16)
+    out[:rows, half:] = jnp.dot(text[...], w_other[...], preferred_element_type=jnp.float32).astype(jnp.bfloat16)
+
+
+def project(ids, text, queries, w_own, w_other, slab_count):
     width = w_own.shape[1] + w_other.shape[1]
+    operands = [text, queries, w_own, w_other]
     return pl.pallas_call(
-        project_kernel,
+        functools.partial(project_kernel, slab_count=slab_count),
+        grid_spec=pltpu.PrefetchScalarGridSpec(
+            num_scalar_prefetch=1,
+            grid=(1,),
+            in_specs=[pl.BlockSpec(a.shape, lambda i, *_: (0, 0)) for a in operands],
+            out_specs=pl.BlockSpec((text.shape[0] + 2 * EXTRA, width), lambda i, *_: (0, 0)),
+        ),
         out_shape=jax.ShapeDtypeStruct((text.shape[0] + 2 * EXTRA, width), jnp.bfloat16),
         compiler_params=pltpu.CompilerParams(vmem_limit_bytes=VMEM_LIMIT),
         cost_estimate=pl.CostEstimate(
             flops=2 * text.shape[0] * text.shape[1] * width, bytes_accessed=2 << 20, transcendentals=0
         ),
         name="project",
-    )(text, queries, codes, w_own, w_other)
+    )(ids, *[in_hbm(a) for a in operands])
 
 
 def to_scalars(vectors, decoded, table, sem):
@@ -79,17 +94,19 @@
         picked = [owners[z, texts : texts + EXTRA, :].astype(jnp.float32)[:query_count] for z in range(depth)]
         shared[...] = jnp.concatenate(picked, axis=0).astype(jnp.bfloat16)
 
-    shard = (lax.div(step, grid_x) * depth + place[0]) * grid_x + lax.rem(step, grid_x)
     lane = row_of((EXTRA, LANES), 1)
-    code = jnp.full((EXTRA, LANES), -1.0, jnp.float32)
-    for z in range(depth):
-        image, listed = table[z, shard], table[EXTRA + z, shard]
-        first = lax.div(jnp.maximum(listed, 0), top_count) * rows
-        out[0, z * rows : (z + 1) * rows, :] = owners[z, pl.ds(pl.multiple_of(first, rows), rows), :]
-        code = jnp.where(lane == z, image.astype(jnp.float32), code)
-        code = jnp.where(lane == EXTRA + z, listed.astype(jnp.float32), code)
-    out[0, slot_rows : slot_rows + shared_rows, :] = shared[...]
-    out[0, slot_rows + shared_rows :, :LANES] = code.astype(jnp.bfloat16)
+    for i in range(out.shape[0]):
+        target = step * out.shape[0] + i
+        shard = (lax.div(target, grid_x) * depth + place[0]) * grid_x + lax.rem(target, grid_x)
+        code = jnp.full((EXTRA, LANES), -1.0, jnp.float32)
+        for z in range(depth):
+            image, listed = table[z, shard], table[EXTRA + z, shard]
+            first = lax.div(jnp.maximum(listed, 0), top_count) * rows
+            out[i, z * rows : (z + 1) * rows, :] = owners[z, pl.ds(pl.multiple_of(first, rows), rows), :]
+            code = jnp.where(lane == z, image.astype(jnp.float32), code)
+            code = jnp.where(lane == EXTRA + z, listed.astype(jnp.float32), code)
+        out[i, slot_rows : slot_rows + shared_rows, :] = shared[...]
+        out[i, slot_rows + shared_rows :, :LANES] = code.astype(jnp.bfloat16)
 
 
 def make_request(place, owners, grid_y, grid_x, rows, query_count, top_count):
@@ -102,9 +119,9 @@
         ),
         grid_spec=pltpu.PrefetchScalarGridSpec(
             num_scalar_prefetch=1,
-            grid=(grid_y * grid_x,),
+            grid=(grid_y * grid_x // 4,),
             in_specs=[pl.BlockSpec(owners.shape, lambda i, *_: (0, 0, 0))],
-            out_specs=pl.BlockSpec((1, total, width), lambda i, *_: (i, 0, 0)),
+            out_specs=pl.BlockSpec((4, total, width), lambda i, *_: (i, 0, 0)),
             scratch_shapes=[
                 pltpu.VMEM((2 * EXTRA, LANES), jnp.int32),
                 pltpu.SMEM((2 * EXTRA, LANES), jnp.int32),
@@ -149,21 +166,28 @@
 
 
 def serve_kernel(
-    got_hbm, slab_hbm, keys_hbm, values_hbm, out,
-    got, slab, keys, values, logits, decoded, table, listed, sems, *, grid_x, depth, rows, query_count, top_count, head_size
+    got_hbm, slab_hbm, keys_hbm, values_hbm, out_hbm,
+    out, got, slab, keys, values, logits, decoded, table, listed, sems, *, grid_x, depth, rows, query_count, top_count, head_size
 ):
+    sources = got.shape[0]
+    slots = sources * depth
+    columns = keys.shape[2]
+    slot_rows = depth * rows
+    late = got.shape[1] - slot_rows
     copies = [
         pltpu.make_async_copy(source, target, sems.at[i])
         for i, (source, target) in enumerate(
-            [(got_hbm, got), (slab_hbm, slab), (keys_hbm, keys), (values_hbm, values)]
+            [
+                (got_hbm.at[:, pl.ds(slot_rows, late), :], got.at[:, pl.ds(slot_rows, late), :]),
+                (slab_hbm, slab),
+                (got_hbm.at[:, pl.ds(0, slot_rows), :], got.at[:, pl.ds(0, slot_rows), :]),
+                (keys_hbm, keys),
+                (values_hbm, values),
+            ]
         )
     ]
     for copy in copies:
         copy.start()
-    sources, height = got.shape[:2]
-    slots = sources * depth
-    columns = keys.shape[2]
-    slot_rows = depth * rows
     shared_rows = depth * query_count
     body = columns // LANES * rows
     per_chunk = LANES // query_count
@@ -176,7 +200,7 @@
         code = got[source, slot_rows + shared_rows :, :LANES].astype(jnp.float32)
         found[source // EXTRA] = jnp.where(tile_row == source % EXTRA, code, found[source // EXTRA])
     found = found[0] if len(found) == 1 else jnp.concatenate(found, axis=0)
-    to_scalars(found.astype(jnp.int32), decoded, table, sems.at[4])
+    to_scalars(found.astype(jnp.int32), decoded, table, sems.at[5])
 
     count = 0
     chunks = [jnp.full((EXTRA, LANES), -1, jnp.int32) for _ in range(-(-slots // per_chunk))]
@@ -208,8 +232,17 @@
             tile = jnp.where(place == at, tiles[0], jnp.where(place == (at + 1) % per_chunk, tiles[1], tiles[2]))
             out[owner, body:, :] = tile.astype(jnp.bfloat16)
 
+    stats_out = pltpu.make_async_copy(
+        out.at[:, pl.ds(body, EXTRA), :], out_hbm.at[:, pl.ds(body, EXTRA), :], sems.at[6]
+    )
+    stats_out.start()
+
+    def send(owner):
+        return pltpu.make_async_copy(out.at[owner, pl.ds(0, body), :], out_hbm.at[owner, pl.ds(0, body), :], sems.at[7])
+
     copies[2].wait()
     copies[3].wait()
+    copies[4].wait()
     spans = []
     at = 0
     while at < columns:
@@ -257,9 +290,19 @@
                 out[owners[g], (at // LANES + c) * rows : (at // LANES + c + 1) * rows, :] = context[
                     :, c * LANES : (c + 1) * LANES
                 ]
+        for owner in owners:
+            send(owner).start()
         return carry
 
-    lax.fori_loop(0, lax.div(count + UNROLL - 1, UNROLL), group, 0)
+    def drain(index, carry):
+        for _ in range(UNROLL):
+            send(0).wait()
+        return carry
+
+    groups = lax.div(count + UNROLL - 1, UNROLL)
+    lax.fori_loop(0, groups, group, 0)
+    lax.fori_loop(0, groups, drain, 0)
+    stats_out.wait()
 
 
 def serve(got, slab, keys, values, grid_x, depth, rows, query_count, top_count, head_size):
@@ -281,14 +324,15 @@
         ),
         grid=(1,),
         in_specs=[pl.BlockSpec(memory_space=pltpu.HBM)] * 4,
-        out_specs=pl.BlockSpec((slots, body + EXTRA, LANES), lambda i: (0, 0, 0)),
-        scratch_shapes=[pltpu.VMEM(a.shape, a.dtype) for a in operands]
+        out_specs=pl.BlockSpec(memory_space=pltpu.HBM),
+        scratch_shapes=[pltpu.VMEM((slots, body + EXTRA, LANES), jnp.bfloat16)]
+        + [pltpu.VMEM(a.shape, a.dtype) for a in operands]
         + [
             pltpu.VMEM((slab.shape[0], lanes), jnp.float32),
             pltpu.VMEM(codes, jnp.int32),
             pltpu.SMEM(codes, jnp.int32),
             pltpu.SMEM((slots + UNROLL,), jnp.int32),
-            pltpu.SemaphoreType.DMA((5,)),
+            pltpu.SemaphoreType.DMA((8,)),
         ],
         out_shape=pltpu.HBM((slots, body + EXTRA, LANES), jnp.bfloat16),
         compiler_params=pltpu.CompilerParams(vmem_limit_bytes=VMEM_LIMIT),
@@ -298,16 +342,26 @@
 
 
 def finish_kernel(
-    shards, place, back, text, w_out, gain, found, out, exact, normalizers, gathered, *, top_count, query_count, shift
+    shards, place, back_hbm, text, w_out, gain, found, out,
+    exact, normalizers, gathered, back, sent, sems, *, top_count, query_count, shift
 ):
     step = pl.program_id(0)
     rows = text.shape[1]
-    body = back.shape[1] - EXTRA
+    body = back.shape[1]
+
+    def fetch(entry, query):
+        return pltpu.make_async_copy(back_hbm.at[shards[entry], pl.ds(0, body), :], back.at[entry], sems.at[query])
 
     @pl.when(step == 0)
     def _():
-        sent = back[:, body:, :].astype(jnp.float32)
-        joined = jnp.sum(jnp.where(row_of(sent.shape, 1) < 3, sent, 0.0), axis=1)
+        stats = pltpu.make_async_copy(back_hbm.at[:, pl.ds(body, EXTRA), :], sent, sems.at[query_count])
+        stats.start()
+        for query in range(query_count):
+            for k in range(top_count):
+                fetch(query * top_count + k, query // text.shape[0]).start()
+        stats.wait()
+        parts = sent[...].astype(jnp.float32)
+        joined = jnp.sum(jnp.where(row_of(parts.shape, 1) < 3, parts, 0.0), axis=1)
         joined = pltpu.roll(joined, lax.rem(LANES - place[0] * query_count, LANES), 1)
         exact[...] = joined
         peak = jnp.max(joined, axis=0, keepdims=True)
@@ -316,50 +370,63 @@
         total = jnp.where(row_of(total.shape, 1) < query_count, total, 1.0)
         normalizers[...] = jnp.broadcast_to(peak + jnp.log(total), normalizers.shape)
 
-    picked = jnp.concatenate([exact[pl.ds(shards[step * top_count + k], 1), :] for k in range(top_count)], axis=0)
-    lane = row_of(picked.shape, 1)
-    candidate = jnp.sum(jnp.where(lane == 2 * query_count + step, picked, 0.0), axis=1, keepdims=True)
-    normalizer = jnp.sum(jnp.where(lane[:1] == step, normalizers[:1, :], 0.0), axis=1, keepdims=True)
-    result = candidate - normalizer + shift
-    result = jnp.sum(jnp.where(lane == row_of(picked.shape, 0), result, 0.0), axis=0, keepdims=True)
-    found[pl.ds(step, 1), :] = result[:, :top_count]
-
-    for k in range(top_count):
-        shard = shards[step * top_count + k]
+    per_step = text.shape[0]
+    for i in range(per_step):
+        query = step * per_step + i
+        picked = jnp.concatenate(
+            [exact[pl.ds(shards[query * top_count + k], 1), :] for k in range(top_count)], axis=0
+        )
+        lane = row_of(picked.shape, 1)
+        candidate = jnp.sum(jnp.where(lane == 2 * query_count + query, picked, 0.0), axis=1, keepdims=True)
+        normalizer = jnp.sum(jnp.where(lane[:1] == query, normalizers[:1, :], 0.0), axis=1, keepdims=True)
+        result = candidate - normalizer + shift
+        result = jnp.sum(jnp.where(lane == row_of(picked.shape, 0), result, 0.0), axis=0, keepdims=True)
+        found[pl.ds(query, 1), :] = result[:, :top_count]
+
+    entries = per_step * top_count
+    for k in range(entries):
+        fetch(step * entries + k, step).wait()
+    for k in range(entries):
         for j in range(body // rows):
-            gathered[k * rows : (k + 1) * rows, j * LANES : (j + 1) * LANES] = back[shard, j * rows : (j + 1) * rows, :]
+            gathered[k * rows : (k + 1) * rows, j * LANES : (j + 1) * LANES] = back[
+                step * entries + k, j * rows : (j + 1) * rows, :
+            ]
     mixed = jnp.dot(gathered[...], w_out[...], preferred_element_type=jnp.float32)
     width = mixed.shape[1]
-    summed = mixed.reshape(top_count, rows, width) + text[...].astype(jnp.float32)
+    summed = mixed.reshape(per_step, top_count, rows, width) + text[...].astype(jnp.float32).reshape(per_step, 1, rows, width)
     mean = jnp.mean(summed, axis=-1, keepdims=True)
     centred = summed - mean
     variance = jnp.mean(centred * centred, axis=-1, keepdims=True)
-    normed = centred * lax.rsqrt(variance + EPSILON) * gain[...].reshape(1, 1, width)
-    out[...] = normed.astype(jnp.bfloat16).reshape(out.shape)
+    normed = centred * lax.rsqrt(variance + EPSILON) * gain[...].reshape(1, 1, 1, width)
+    out[...] = normed.astype(jnp.bfloat16)
 
 
 def finish(shards, place, back, text, w_out, gain, top_count, shift):
     query_count, rows, width = text.shape
+    per_step = 2
     full = lambda a: pl.BlockSpec(a.shape, lambda i, *_: (0,) * a.ndim)
     return pl.pallas_call(
         functools.partial(finish_kernel, top_count=top_count, query_count=query_count, shift=shift),
         grid_spec=pltpu.PrefetchScalarGridSpec(
             num_scalar_prefetch=2,
-            grid=(query_count,),
+            grid=(query_count // per_step,),
             in_specs=[
-                full(back),
-                pl.BlockSpec((1, rows, width), lambda i, *_: (i, 0, 0)),
+                pl.BlockSpec(memory_space=pltpu.HBM),
+                pl.BlockSpec((per_step, rows, width), lambda i, *_: (i, 0, 0)),
                 full(w_out),
                 full(gain),
             ],
             out_specs=[
                 pl.BlockSpec((query_count, top_count), lambda i, *_: (0, 0)),
-                pl.BlockSpec((1, top_count, rows, width), lambda i, *_: (i, 0, 0, 0)),
+                pl.BlockSpec((per_step, top_count, rows, width), lambda i, *_: (i, 0, 0, 0)),
             ],
             scratch_shapes=[
                 pltpu.VMEM((back.shape[0], LANES), jnp.float32),
                 pltpu.VMEM((EXTRA, LANES), jnp.float32),
-                pltpu.VMEM((top_count * rows, width), jnp.bfloat16),
+                pltpu.VMEM((per_step * top_count * rows, width), jnp.bfloat16),
+                pltpu.VMEM((query_count * top_count, back.shape[1] - EXTRA, LANES), jnp.bfloat16),
+                pltpu.VMEM((back.shape[0], EXTRA, LANES), jnp.bfloat16),
+                pltpu.SemaphoreType.DMA((query_count + 1,)),
             ],
         ),
         out_shape=[
@@ -401,16 +468,13 @@
 
     own_list = cand_ids.reshape(list_length)
     own_anchor = own_list // slab_count
-    here = own_anchor[None, :] == row_of((LANES, 1), 0)
-    row_ids = jnp.sum(jnp.where(here, own_list[None, :] % slab_count + 1, 0), axis=1) - 1
-    list_ids = jnp.sum(jnp.where(here, row_of((1, list_length), 1) + 1, 0), axis=1) - 1
-
     sent = project(
+        cand_ids,
         text_states.reshape(query_count * text_count, model_width),
         queries,
-        jnp.stack([row_ids, list_ids]),
         w_query,
         w_query_other,
+        slab_count,
     )
     owners = lax.all_gather(sent, "shard", axis=0, tiled=True, axis_index_groups=columns)
     request = make_request(

time: 214 us -> 209 us (0.977)
  Pallas kernels: 30.3 us -> 26.6 us
    pallas_call x1, Pallas kernels: 7.96 us -> 4.54 us  [make_request(): pl.pallas_call(functools.partial(request_kernel, grid_x=grid_x, rows=rows...]
  transfers between devices with their start and end apart: 6 -> 6, of which waited for: 5 -> 5; matrix products, arithmetic and copies ran while one was open for 6% -> 5% of each run, Pallas kernels for 0% -> 0%
where the time goes in v4:
time: 209 us; the launch traced here: 208 us
  waiting for transfers between devices  119 us (57%)
  blocking collectives  31.3 us (15%)
  Pallas kernels  26.6 us (13%)
  starting transfers between devices  17.2 us (8%)
  matrix products  6.97 us (3%)
  local copies, waits for them, and re-layouts  2.8 us (1%)
  other arithmetic  2.49 us (1%)
    all_to_all x1, waiting for transfers between devices, on_device(): lax.all_to_all(context, 'shard', split_axis=0, concat_axis=0, tiled=True)  73.8 us
    all_to_all x1, waiting for transfers between devices, on_device(): lax.all_to_all(request, 'shard', split_axis=0, concat_axis=0, tiled=True,...  39.5 us
    all_gather x1, blocking collectives, on_device(): lax.all_gather(sent, 'shard', axis=0, tiled=True, axis_index_groups=columns)  31.3 us
    pallas_call x1, Pallas kernels, serve(): pl.pallas_call(functools.partial(serve_kernel, grid_x=grid_x, depth=depth...  13.3 us
    all_to_all x1, starting transfers between devices, on_device(): lax.all_to_all(context, 'shard', split_axis=0, concat_axis=0, tiled=True)  9.24 us
    all_to_all x1, starting transfers between devices, on_device(): lax.all_to_all(request, 'shard', split_axis=0, concat_axis=0, tiled=True,...  7.22 us
    dot_general x2, matrix products, project_rows(): jnp.einsum('spc,cd->spd', rows_in, weight, preferred_element_type=jnp.flo...  6.97 us
    pallas_call x1, Pallas kernels, finish(): pl.pallas_call(functools.partial(finish_kernel, top_count=top_count, quer...  6.6 us
  transfers between devices with their start and end apart: 6, of which 5 were waited for; matrix products, arithmetic and copies ran while one was open for 5% of the time, Pallas kernels for 0%

profile of v4, /device:TPU:32, one launch (start us, length us, event | category | flops | bytes accessed | tf_op | source)
XLA Modules:
  0.0 207.7 jit_solution(8271919345023572866)
XLA Ops:
  0.6 0.0 copy-start
  0.6 0.1 collective-permute-start
  0.8 2.2 %collective-permute-done.w_other = bf16[768,384]{1,0:T(8,128)(2,1)S(1)} collective-permute-done((bf16[768,384]{1,0:T(8,128)(2,1)}, bf16[768,384]{1,0:T(8,128)(2,1)S(1)}, u32[]{:S(2)}, u32[]{:S(2)}) %collective-permute-start) | collective-permute-done | bytes 589856 | tf_op jit(solution)/shard_map/ppermute | solution.py:467
  2.9 0.8 copy-done.5
  3.8 0.7 copy-done.2
  4.4 2.2 %project.1 = bf16[80,768]{1,0:T(8,128)(2,1)S(1)} custom-call(s32[4,16]{1,0:T(4,128)S(1)} %copy-done.2, bf16[64,768]{1,0:T(8,128)(2,1)} %bitcast.16, bf16[4,768]{1,0:T(4,128)(2,1)} %queries.1, bf16[768,384]{1,0:T(8,128)(2,1)} %w_own.1, bf16[768,384]{1,0:T(8,128)(2,1)} %copy-done.5), custom_call_target="tpu_custom_call" | custom-call | flops 75497472 | bytes 2097152 | tf_op jit(solution)/shard_map/project/pallas_call | solution.py:55
  6.6 31.3 %all_gather.3 = bf16[640,768]{1,0:T(8,128)(2,1)} all-gather(bf16[80,768]{1,0:T(8,128)(2,1)S(1)} %project.1), channel_id=1, replica_groups={{0,8,16,24,32,40,48,56},{2,10,18,26,34,42,50,58},{4,12,20,28,36,44,52,6..., dimensions={0}, use_global_device_ids=true | all-gather | bytes 1105920 | tf_op jit(solution)/shard_map/all_gather | solution.py:479
  38.0 4.5 %request.1 = bf16[16,168,768]{2,1,0:T(8,128)(2,1)} custom-call(s32[1]{0:T(128)} %bitcast.1.place, bf16[8,80,768]{2,1,0:T(8,128)(2,1)} %bitcast.17), custom_call_target="tpu_custom_call" | custom-call | flops 1048576 | bytes 6291456 | tf_op jit(solution)/shard_map/request/pallas_call | solution.py:116
  42.5 0.0 copy-start.7
  42.5 7.2 %all-to-all-start = ((bf16[16,168,768]{2,1,0:T(8,128)(2,1)}), bf16[16,168,768]{2,1,0:T(8,128)(2,1)}, u32[]{:S(2)}, u32[]{:S(2)}) async-start(bf16[16,168,768]{2,1,0:T(8,128)(2,1)} %request.1), calls=%async_computation | async-start | bytes 8257536 | tf_op jit(solution)/shard_map/all_to_all | solution.py:489
  49.8 0.0 copy-start.8
  49.8 0.1 collective-permute-start.1
  49.9 0.5 collective-permute-start.2
  50.4 1.9 collective-permute-done.1
  52.3 3.5 %convert_bitcast_fusion.1.keys_hbm = bf16[32,40,768]{2,1,0:T(8,128)(2,1)} fusion(bf16[32,40,1024]{2,1,0:T(8,128)(2,1)S(1)} %copy-done, bf16[1024,384]{1,0:T(8,128)(2,1)S(1)} %collective-permute-done.1, bf16[1024,384]{1,0:T(8,128)(2,1)S(1)} %copy-done.7), kind=kOutput, calls=%fused_computation.1 | convolution fusion | flops 2017394688 | bytes 6160384 | tf_op jit(solution)/shard_map/spc,cd->spd/dot_general | solution.py:445
  55.8 0.0 collective-permute-done.2
  55.8 3.4 %convert_bitcast_fusion.values_hbm = bf16[32,40,768]{2,1,0:T(8,128)(2,1)} fusion(bf16[32,40,1024]{2,1,0:T(8,128)(2,1)S(1)} %copy-done, bf16[1024,384]{1,0:T(8,128)(2,1)S(1)} %collective-permute-done.2, bf16[1024,384]{1,0:T(8,128)(2,1)S(1)} %copy-done.8), kind=kOutput, calls=%fused_computation | convolution fusion | flops 2017394688 | bytes 6160384 | tf_op jit(solution)/shard_map/spc,cd->spd/dot_general | solution.py:445
  59.3 39.5 %all-to-all-done.got_hbm = bf16[16,168,768]{2,1,0:T(8,128)(2,1)} async-done(((bf16[16,168,768]{2,1,0:T(8,128)(2,1)}), bf16[16,168,768]{2,1,0:T(8,128)(2,1)}, u32[]{:S(2)}, u32[]{:S(2)}) %all-to-all-start) | async-done | bytes 4128800 | tf_op jit(solution)/shard_map/all_to_all | solution.py:489
  98.7 13.3 %serve.1 = bf16[128,104,128]{2,1,0:T(8,128)(2,1)} custom-call(bf16[16,168,768]{2,1,0:T(8,128)(2,1)} %all-to-all-done.got_hbm, bf16[2048,768]{1,0:T(8,128)(2,1)} %slab_hbm.1, bf16[32,40,768]{2,1,0:T(8,128)(2,1)} %convert_bitcast_fusion.1.keys_hbm, bf16[32,40,768]{2,1,0:T(8,128)(2,1)} %convert_bitcast_fusion.values_hbm), custom_call_target="tpu_custom_call" | custom-call | flops 8589934592 | bytes 14680064 | tf_op jit(solution)/shard_map/serve/pallas_call | solution.py:315
  112.0 0.0 copy-start.4
  112.0 0.0 copy-start.3
  112.0 0.0 copy-start.6
  112.1 9.2 %all-to-all-start.1 = ((bf16[128,104,128]{2,1,0:T(8,128)(2,1)}), bf16[128,104,128]{2,1,0:T(8,128)(2,1)}, u32[]{:S(2)}, u32[]{:S(2)}) async-start(bf16[128,104,128]{2,1,0:T(8,128)(2,1)} %serve.1), calls=%async_computation.1 | async-start | bytes 6815744 | tf_op jit(solution)/shard_map/all_to_all | solution.py:508
  121.3 0.1 collective-permute-start.3
  121.4 0.1 reshape.22
  121.5 0.1 fusion.7
  121.6 0.0 copy-start.1
  121.6 1.9 collective-permute-done.3
  123.5 1.1 fusion.6
  124.7 2.5 %maximum_select_fusion.w_out = bf16[768,768]{1,0:T(8,128)(2,1)} fusion(bf16[768,384]{1,0:T(8,128)(2,1)} %collective-permute-done.3, bf16[768,384]{1,0:T(8,128)(2,1)S(1)} %copy-done.4, bf16[384,384]{1,0:T(8,128)(2,1)S(1)} %get-tuple-element.5, bf16[384,384]{1,0:T(8,128)(2,1)S(1)} %get-tuple-element.3, bf16[384,384]{1,0:T(8,128)(2,1)S(1)} %get-tuple-element.4, ...), kind=kLoop, calls=%fused_computation.8 | loop fusion | flops 7667712 | bytes 3538945 | tf_op jit(solution)/shard_map/jit(_where)/select_n | solution.py:495
  127.1 73.8 %all-to-all-done.1.back_hbm = bf16[128,104,128]{2,1,0:T(8,128)(2,1)} async-done(((bf16[128,104,128]{2,1,0:T(8,128)(2,1)}), bf16[128,104,128]{2,1,0:T(8,128)(2,1)}, u32[]{:S(2)}, u32[]{:S(2)}) %all-to-all-start.1) | async-done | bytes 3407904 | tf_op jit(solution)/shard_map/all_to_all | solution.py:508
  201.0 6.6 %finish.1 = (f32[4,16]{1,0:T(4,128)}, bf16[4,16,16,768]{3,2,1,0:T(8,128)(2,1)}) custom-call(s32[64]{0:T(128)S(1)} %and_select_fusion.shards, s32[1]{0:T(128)} %bitcast.place, bf16[128,104,128]{2,1,0:T(8,128)(2,1)} %all-to-all-done.1.back_hbm, bf16[4,16,768]{2,1,0:T(8,128)(2,1)S(1)} %copy-done.1, bf16[768,768]{1,0:T(8,128)(2,1)} %maximum_select_fusion.w_out, ...), custom_call_target="tpu_custom_call" | custom-call | flops 1207959552 | bytes 7340032 | tf_op jit(solution)/shard_map/finish/pallas_call | solution.py:408
  (11 shorter events, 0.0 us)
Async XLA Ops:
  0.6 51.6 %copy-start = (bf16[32,40,1024]{2,1,0:T(8,128)(2,1)S(1)}, bf16[32,40,1024]{2,1,0:T(8,128)(2,1)}, u32[]{:S(2)}) copy-start(bf16[32,40,1024]{2,1,0:T(8,128)(2,1)} %param.13) | copy-start | bytes 7864324
  0.6 2.3 %collective-permute-start = (bf16[768,384]{1,0:T(8,128)(2,1)}, bf16[768,384]{1,0:T(8,128)(2,1)S(1)}, u32[]{:S(2)}, u32[]{:S(2)}) collective-permute-start(bf16[768,384]{1,0:T(8,128)(2,1)} %w_own.1), channel_id=1, source_target_pairs={{0,1},{1,0},{2,3},{3,2},{4,5},{5,4},{6,7},{7,6},{8,9},{9,8},{10,11... | collective-permute-start | bytes 1769480 | tf_op jit(solution)/shard_map/ppermute | solution.py:467
  2.9 0.8 copy-start.5
  3.8 0.7 copy-start.2
  42.5 7.2 %copy-start.7 = (bf16[1024,384]{1,0:T(8,128)(2,1)S(1)}, bf16[1024,384]{1,0:T(8,128)(2,1)}, u32[]{:S(2)}) copy-start(bf16[1024,384]{1,0:T(8,128)(2,1)} %param.16) | copy-start | bytes 2359300
  42.5 56.2 %all-to-all-start = ((bf16[16,168,768]{2,1,0:T(8,128)(2,1)}), bf16[16,168,768]{2,1,0:T(8,128)(2,1)}, u32[]{:S(2)}, u32[]{:S(2)}) async-start(bf16[16,168,768]{2,1,0:T(8,128)(2,1)} %request.1), calls=%async_computation | async-start | bytes 8257536 | tf_op jit(solution)/shard_map/all_to_all | solution.py:489
  49.8 6.0 %copy-start.8 = (bf16[1024,384]{1,0:T(8,128)(2,1)S(1)}, bf16[1024,384]{1,0:T(8,128)(2,1)}, u32[]{:S(2)}) copy-start(bf16[1024,384]{1,0:T(8,128)(2,1)} %param.17) | copy-start | bytes 2359300
  49.8 2.5 %collective-permute-start.1 = (bf16[1024,384]{1,0:T(8,128)(2,1)S(1)}, bf16[1024,384]{1,0:T(8,128)(2,1)S(1)}, u32[]{:S(2)}, u32[]{:S(2)}) collective-permute-start(bf16[1024,384]{1,0:T(8,128)(2,1)S(1)} %copy-done.7), channel_id=1, source_target_pairs={{0,1},{1,0},{2,3},{3,2},{4,5},{5,4},{6,7},{7,6},{8,9},{9,8},{10,11... | collective-permute-start | bytes 2359304 | tf_op jit(solution)/shard_map/ppermute | solution.py:491
  49.9 5.9 %collective-permute-start.2 = (bf16[1024,384]{1,0:T(8,128)(2,1)}, bf16[1024,384]{1,0:T(8,128)(2,1)S(1)}, u32[]{:S(2)}, u32[]{:S(2)}) collective-permute-start(bf16[1024,384]{1,0:T(8,128)(2,1)} %param.17), channel_id=1, source_target_pairs={{0,1},{1,0},{2,3},{3,2},{4,5},{5,4},{6,7},{7,6},{8,9},{9,8},{10,11... | collective-permute-start | bytes 2359304 | tf_op jit(solution)/shard_map/ppermute | solution.py:492
  112.0 9.3 %copy-start.4 = (bf16[768,384]{1,0:T(8,128)(2,1)S(1)}, bf16[768,384]{1,0:T(8,128)(2,1)}, u32[]{:S(2)}) copy-start(bf16[768,384]{1,0:T(8,128)(2,1)} %param.18) | copy-start | bytes 1769476
  112.0 9.4 %copy-start.3 = (s32[4,16]{1,0:T(4,128)S(1)}, s32[4,16]{1,0:T(4,128)}, u32[]{:S(2)}) copy-start(s32[4,16]{1,0:T(4,128)} %ids.1) | copy-start | bytes 772
  112.0 9.5 %copy-start.6 = (f32[768]{0:T(1024)S(1)}, f32[768]{0:T(1024)}, u32[]{:S(2)}) copy-start(f32[768]{0:T(1024)} %param.19) | copy-start | bytes 9220
  112.1 88.9 %all-to-all-start.1 = ((bf16[128,104,128]{2,1,0:T(8,128)(2,1)}), bf16[128,104,128]{2,1,0:T(8,128)(2,1)}, u32[]{:S(2)}, u32[]{:S(2)}) async-start(bf16[128,104,128]{2,1,0:T(8,128)(2,1)} %serve.1), calls=%async_computation.1 | async-start | bytes 6815744 | tf_op jit(solution)/shard_map/all_to_all | solution.py:508
  121.3 2.2 %collective-permute-start.3 = (bf16[768,384]{1,0:T(8,128)(2,1)S(1)}, bf16[768,384]{1,0:T(8,128)(2,1)}, u32[]{:S(2)}, u32[]{:S(2)}) collective-permute-start(bf16[768,384]{1,0:T(8,128)(2,1)S(1)} %copy-done.4), channel_id=1, source_target_pairs={{0,1},{1,0},{2,3},{3,2},{4,5},{5,4},{6,7},{7,6},{8,9},{9,8},{10,11... | collective-permute-start | bytes 1769480 | tf_op jit(solution)/shard_map/ppermute | solution.py:493
  121.6 79.4 %copy-start.1 = (bf16[4,16,768]{2,1,0:T(8,128)(2,1)S(1)}, bf16[4,16,768]{2,1,0:T(8,128)(2,1)}, u32[]{:S(2)}) copy-start(bf16[4,16,768]{2,1,0:T(8,128)(2,1)} %text.1) | copy-start | bytes 294916

commit v5 on v4

--- a/solution.py
+++ b/solution.py
@@ -66,7 +66,7 @@
             flops=2 * text.shape[0] * text.shape[1] * width, bytes_accessed=2 << 20, transcendentals=0
         ),
         name="project",
-    )(ids, *[in_hbm(a) for a in operands])
+    )(ids, in_hbm(text), in_hbm(queries), in_hbm(w_own), w_other)
 
 
 def to_scalars(vectors, decoded, table, sem):
@@ -76,23 +76,24 @@
     copy.wait()
 
 
-def request_kernel(place, owners, out, decoded, table, shared, sem, *, grid_x, rows, query_count, top_count):
+def read_codes(owners, decoded, table, sem):
+    depth, height = owners.shape[:2]
+    tile_row = row_of((EXTRA, LANES), 0)
+    found = [jnp.zeros((EXTRA, LANES), jnp.float32) for _ in range(2)]
+    for z in range(depth):
+        code = owners[z, height - EXTRA :, : 2 * LANES].astype(jnp.float32)
+        found = [jnp.where(tile_row == z, code[:, i * LANES : (i + 1) * LANES], found[i]) for i in range(2)]
+    to_scalars(jnp.concatenate(found, axis=0).astype(jnp.int32), decoded, table, sem)
+
+
+def first_request_kernel(place, owners, out, decoded, table, sem, *, grid_x, rows, top_count):
     step = pl.program_id(0)
-    depth, height = owners.shape[:2]
-    texts = height - 2 * EXTRA
-    slot_rows = depth * rows
-    shared_rows = shared.shape[0]
-    tile_row = row_of((EXTRA, LANES), 0)
+    depth = owners.shape[0]
+    columns = out.shape[2]
 
     @pl.when(step == 0)
     def _():
-        found = [jnp.zeros((EXTRA, LANES), jnp.float32) for _ in range(2)]
-        for z in range(depth):
-            code = owners[z, texts + EXTRA :, :].astype(jnp.float32)
-            found = [jnp.where(tile_row == z, code[:, i * LANES : (i + 1) * LANES], found[i]) for i in range(2)]
-        to_scalars(jnp.concatenate(found, axis=0).astype(jnp.int32), decoded, table, sem)
-        picked = [owners[z, texts : texts + EXTRA, :].astype(jnp.float32)[:query_count] for z in range(depth)]
-        shared[...] = jnp.concatenate(picked, axis=0).astype(jnp.bfloat16)
+        read_codes(owners, decoded, table, sem)
 
     lane = row_of((EXTRA, LANES), 1)
     for i in range(out.shape[0]):
@@ -100,40 +101,89 @@
         shard = (lax.div(target, grid_x) * depth + place[0]) * grid_x + lax.rem(target, grid_x)
         code = jnp.full((EXTRA, LANES), -1.0, jnp.float32)
         for z in range(depth):
-            image, listed = table[z, shard], table[EXTRA + z, shard]
-            first = lax.div(jnp.maximum(listed, 0), top_count) * rows
-            out[i, z * rows : (z + 1) * rows, :] = owners[z, pl.ds(pl.multiple_of(first, rows), rows), :]
+            image, entry = table[z, shard], table[EXTRA + z, shard]
+            first = lax.div(jnp.maximum(entry, 0), top_count) * rows
+            out[i, z * rows : (z + 1) * rows, :] = owners[z, pl.ds(pl.multiple_of(first, rows), rows), :columns]
             code = jnp.where(lane == z, image.astype(jnp.float32), code)
-            code = jnp.where(lane == EXTRA + z, listed.astype(jnp.float32), code)
-        out[i, slot_rows : slot_rows + shared_rows, :] = shared[...]
-        out[i, slot_rows + shared_rows :, :LANES] = code.astype(jnp.bfloat16)
-
-
-def make_request(place, owners, grid_y, grid_x, rows, query_count, top_count):
+            code = jnp.where(lane == EXTRA + z, entry.astype(jnp.float32), code)
+        out[i, depth * rows :, :LANES] = code.astype(jnp.bfloat16)
+
+
+def first_request(place, owners, grid_y, grid_x, rows, top_count):
     depth, height, width = owners.shape
-    shared_rows = depth * query_count
-    total = depth * rows + shared_rows + EXTRA
+    columns = width // 2
+    total = depth * rows + EXTRA
+    block = 4
     return pl.pallas_call(
-        functools.partial(
-            request_kernel, grid_x=grid_x, rows=rows, query_count=query_count, top_count=top_count
-        ),
+        functools.partial(first_request_kernel, grid_x=grid_x, rows=rows, top_count=top_count),
         grid_spec=pltpu.PrefetchScalarGridSpec(
             num_scalar_prefetch=1,
-            grid=(grid_y * grid_x // 4,),
+            grid=(grid_y * grid_x // block,),
             in_specs=[pl.BlockSpec(owners.shape, lambda i, *_: (0, 0, 0))],
-            out_specs=pl.BlockSpec((4, total, width), lambda i, *_: (i, 0, 0)),
+            out_specs=pl.BlockSpec((block, total, columns), lambda i, *_: (i, 0, 0)),
             scratch_shapes=[
                 pltpu.VMEM((2 * EXTRA, LANES), jnp.int32),
                 pltpu.SMEM((2 * EXTRA, LANES), jnp.int32),
-                pltpu.VMEM((shared_rows, width), jnp.bfloat16),
                 pltpu.SemaphoreType.DMA,
             ],
         ),
-        out_shape=pltpu.HBM((grid_y * grid_x, total, width), jnp.bfloat16),
+        out_shape=pltpu.HBM((grid_y * grid_x, total, columns), jnp.bfloat16),
         compiler_params=pltpu.CompilerParams(vmem_limit_bytes=VMEM_LIMIT),
-        cost_estimate=pl.CostEstimate(flops=1 << 20, bytes_accessed=6 << 20, transcendentals=0),
-        name="request",
+        cost_estimate=pl.CostEstimate(flops=1 << 20, bytes_accessed=4 << 20, transcendentals=0),
+        name="first_request",
     )(place, in_hbm(owners))
+
+
+def second_request_kernel(place, after, owners, *rest, grid_y, grid_x, rows, query_count, top_count):
+    outs = rest[: grid_y * grid_x]
+    decoded, table, sem = rest[grid_y * grid_x :]
+    depth, height, width = owners.shape
+    columns = width // 2
+    texts = height - 2 * EXTRA
+    read_codes(owners, decoded, table, sem)
+    picked = [owners[z, texts : texts + EXTRA, :].astype(jnp.float32)[:query_count] for z in range(depth)]
+    shared = jnp.concatenate(picked, axis=0).astype(jnp.bfloat16)
+    for k, out in enumerate(outs):
+        y = lax.rem(place[1] + k // grid_x, grid_y)
+        x = lax.rem(place[2] + k % grid_x, grid_x)
+        shard = (y * depth + place[0]) * grid_x + x
+        for z in range(depth):
+            first = lax.div(jnp.maximum(table[EXTRA + z, shard], 0), top_count) * rows
+            out[z * rows : (z + 1) * rows, :] = owners[z, pl.ds(pl.multiple_of(first, rows), rows), columns:]
+        at = depth * rows
+        out[at : at + shared.shape[0], :] = shared[:, :columns]
+        out[at + shared.shape[0] :, :] = shared[:, columns:]
+
+
+def second_request(place, after, owners, grid_y, grid_x, rows, query_count, top_count):
+    depth, height, width = owners.shape
+    total = depth * rows + 2 * depth * query_count
+    count = grid_y * grid_x
+    return pl.pallas_call(
+        functools.partial(
+            second_request_kernel,
+            grid_y=grid_y,
+            grid_x=grid_x,
+            rows=rows,
+            query_count=query_count,
+            top_count=top_count,
+        ),
+        grid_spec=pltpu.PrefetchScalarGridSpec(
+            num_scalar_prefetch=2,
+            grid=(1,),
+            in_specs=[pl.BlockSpec(owners.shape, lambda i, *_: (0, 0, 0))],
+            out_specs=[pl.BlockSpec((total, width // 2), lambda i, *_: (0, 0))] * count,
+            scratch_shapes=[
+                pltpu.VMEM((2 * EXTRA, LANES), jnp.int32),
+                pltpu.SMEM((2 * EXTRA, LANES), jnp.int32),
+                pltpu.SemaphoreType.DMA,
+            ],
+        ),
+        out_shape=[pltpu.HBM((total, width // 2), jnp.bfloat16)] * count,
+        compiler_params=pltpu.CompilerParams(vmem_limit_bytes=VMEM_LIMIT),
+        cost_estimate=pl.CostEstimate(flops=1 << 20, bytes_accessed=4 << 20, transcendentals=0),
+        name="second_request",
+    )(place, after, in_hbm(owners))
 
 
 def index_stats(query, slab, picked, logits):
@@ -165,84 +215,19 @@
     return jnp.where(tile_row < 3, parts, 0.0)
 
 
-def serve_kernel(
-    got_hbm, slab_hbm, keys_hbm, values_hbm, out_hbm,
-    out, got, slab, keys, values, logits, decoded, table, listed, sems, *, grid_x, depth, rows, query_count, top_count, head_size
-):
-    sources = got.shape[0]
-    slots = sources * depth
-    columns = keys.shape[2]
-    slot_rows = depth * rows
-    late = got.shape[1] - slot_rows
-    copies = [
-        pltpu.make_async_copy(source, target, sems.at[i])
-        for i, (source, target) in enumerate(
-            [
-                (got_hbm.at[:, pl.ds(slot_rows, late), :], got.at[:, pl.ds(slot_rows, late), :]),
-                (slab_hbm, slab),
-                (got_hbm.at[:, pl.ds(0, slot_rows), :], got.at[:, pl.ds(0, slot_rows), :]),
-                (keys_hbm, keys),
-                (values_hbm, values),
-            ]
-        )
-    ]
-    for copy in copies:
-        copy.start()
-    shared_rows = depth * query_count
-    body = columns // LANES * rows
-    per_chunk = LANES // query_count
-    lane = row_of((EXTRA, LANES), 1)
-    tile_row = row_of((EXTRA, LANES), 0)
-
-    copies[0].wait()
-    found = [jnp.zeros((EXTRA, LANES), jnp.float32) for _ in range(-(-sources // EXTRA))]
-    for source in range(sources):
-        code = got[source, slot_rows + shared_rows :, :LANES].astype(jnp.float32)
-        found[source // EXTRA] = jnp.where(tile_row == source % EXTRA, code, found[source // EXTRA])
-    found = found[0] if len(found) == 1 else jnp.concatenate(found, axis=0)
-    to_scalars(found.astype(jnp.int32), decoded, table, sems.at[5])
-
+def list_slots(slots, depth, table, listed):
     count = 0
-    chunks = [jnp.full((EXTRA, LANES), -1, jnp.int32) for _ in range(-(-slots // per_chunk))]
     for slot in range(slots):
-        image, entry = table[slot // depth, slot % depth], table[slot // depth, EXTRA + slot % depth]
-        query = lax.div(jnp.maximum(entry, 0), top_count)
-        at = slot % per_chunk * query_count + query
-        chunks[slot // per_chunk] = jnp.where(lane == at, image, chunks[slot // per_chunk])
         listed[count] = slot
-        count = count + jnp.where(image >= 0, 1, 0)
+        count = count + jnp.where(table[slot // depth, slot % depth] >= 0, 1, 0)
     last = listed[jnp.maximum(count - 1, 0)]
     for g in range(UNROLL):
         listed[count + g] = last
-
-    queries = jnp.concatenate([got[source, slot_rows : slot_rows + shared_rows, :] for source in range(sources)], axis=0)
-    missing = len(chunks) * LANES - queries.shape[0]
-    if missing:
-        queries = jnp.concatenate([queries, jnp.zeros((missing, queries.shape[1]), queries.dtype)], axis=0)
-    copies[1].wait()
-    stats = index_stats(queries, slab, jnp.concatenate([chunk[:1] for chunk in chunks], axis=1), logits)
-    for c in range(len(chunks)):
-        tiles = [split_rows(stat[:, c * LANES : (c + 1) * LANES]) for stat in stats]
-        tiles = [tiles[0], pltpu.roll(tiles[1], query_count, 1), pltpu.roll(tiles[2], 2 * query_count, 1)]
-        for slot in range(c * per_chunk, min((c + 1) * per_chunk, slots)):
-            source, z = slot // depth, slot % depth
-            at = slot % per_chunk
-            owner = (source // grid_x * depth + z) * grid_x + source % grid_x
-            place = lane // query_count
-            tile = jnp.where(place == at, tiles[0], jnp.where(place == (at + 1) % per_chunk, tiles[1], tiles[2]))
-            out[owner, body:, :] = tile.astype(jnp.bfloat16)
-
-    stats_out = pltpu.make_async_copy(
-        out.at[:, pl.ds(body, EXTRA), :], out_hbm.at[:, pl.ds(body, EXTRA), :], sems.at[6]
-    )
-    stats_out.start()
-
-    def send(owner):
-        return pltpu.make_async_copy(out.at[owner, pl.ds(0, body), :], out_hbm.at[owner, pl.ds(0, body), :], sems.at[7])
-
-    copies[2].wait()
-    copies[3].wait()
-    copies[4].wait()
+    return count
+
+
+def attend_slots(count, listed, table, got, keys, values, out, send, *, grid_x, depth, rows, head_size):
+    columns = keys.shape[2]
     spans = []
     at = 0
     while at < columns:
@@ -302,19 +287,159 @@
     groups = lax.div(count + UNROLL - 1, UNROLL)
     lax.fori_loop(0, groups, group, 0)
     lax.fori_loop(0, groups, drain, 0)
-    stats_out.wait()
-
-
-def serve(got, slab, keys, values, grid_x, depth, rows, query_count, top_count, head_size):
+
+
+def first_serve_kernel(
+    got_hbm, keys_hbm, values_hbm, out_hbm, decoded, out, got, keys, values, table, listed, sems,
+    *, grid_x, depth, rows, head_size
+):
+    copies = [
+        pltpu.make_async_copy(source, target, sems.at[i])
+        for i, (source, target) in enumerate([(got_hbm, got), (keys_hbm, keys), (values_hbm, values)])
+    ]
+    for copy in copies:
+        copy.start()
+    sources = got.shape[0]
+    tile_row = row_of((EXTRA, LANES), 0)
+    copies[0].wait()
+    found = [jnp.zeros((EXTRA, LANES), jnp.float32) for _ in range(-(-sources // EXTRA))]
+    for source in range(sources):
+        code = got[source, depth * rows :, :LANES].astype(jnp.float32)
+        found[source // EXTRA] = jnp.where(tile_row == source % EXTRA, code, found[source // EXTRA])
+    found = found[0] if len(found) == 1 else jnp.concatenate(found, axis=0)
+    to_scalars(found.astype(jnp.int32), decoded, table, sems.at[3])
+    count = list_slots(sources * depth, depth, table, listed)
+
+    def send(owner):
+        return pltpu.make_async_copy(out.at[owner], out_hbm.at[owner], sems.at[4])
+
+    copies[1].wait()
+    copies[2].wait()
+    attend_slots(
+        count, listed, table, got, keys, values, out, send, grid_x=grid_x, depth=depth, rows=rows, head_size=head_size
+    )
+
+
+def first_serve(got, keys, values, grid_x, depth, rows, head_size):
     sources = got.shape[0]
     slots = sources * depth
     body = keys.shape[2] // LANES * rows
-    lanes = -(-slots * query_count // LANES) * LANES
-    operands = [got, slab, keys, values]
+    operands = [got, keys, values]
     codes = (-(-sources // EXTRA) * EXTRA, LANES)
     return pl.pallas_call(
+        functools.partial(first_serve_kernel, grid_x=grid_x, depth=depth, rows=rows, head_size=head_size),
+        grid=(1,),
+        in_specs=[pl.BlockSpec(memory_space=pltpu.HBM)] * 3,
+        out_specs=[pl.BlockSpec(memory_space=pltpu.HBM), pl.BlockSpec(codes, lambda i: (0, 0))],
+        scratch_shapes=[pltpu.VMEM((slots, body, LANES), jnp.bfloat16)]
+        + [pltpu.VMEM(a.shape, a.dtype) for a in operands]
+        + [
+            pltpu.SMEM(codes, jnp.int32),
+            pltpu.SMEM((slots + UNROLL,), jnp.int32),
+            pltpu.SemaphoreType.DMA((5,)),
+        ],
+        out_shape=[pltpu.HBM((slots, body, LANES), jnp.bfloat16), jax.ShapeDtypeStruct(codes, jnp.int32)],
+        compiler_params=pltpu.CompilerParams(vmem_limit_bytes=VMEM_LIMIT),
+        cost_estimate=pl.CostEstimate(flops=4 << 30, bytes_accessed=6 << 20, transcendentals=1 << 20),
+        name="first_serve",
+    )(*[in_hbm(a) for a in operands])
+
+
+def second_serve_kernel(
+    place, table, *rest, grid_y, grid_x, depth, rows, query_count, top_count, head_size
+):
+    sources = grid_y * grid_x
+    arrived = rest[:sources]
+    slab_hbm, keys_hbm, values_hbm, out_hbm, out, got, slab, keys, values, logits, listed, sems = rest[sources:]
+    slots = sources * depth
+    columns = keys.shape[2]
+    slot_rows = depth * rows
+    shared_rows = depth * query_count
+    body = columns // LANES * rows
+    per_chunk = LANES // query_count
+    late = got.shape[1] - slot_rows
+    lane = row_of((EXTRA, LANES), 1)
+
+    def fetch(k, start, size, sem):
+        y = lax.rem(place[1] + grid_y - k // grid_x, grid_y)
+        x = lax.rem(place[2] + grid_x - k % grid_x, grid_x)
+        return pltpu.make_async_copy(
+            arrived[k].at[pl.ds(start, size), :], got.at[y * grid_x + x, pl.ds(start, size), :], sems.at[sem]
+        )
+
+    early = [fetch(k, slot_rows, late, 0) for k in range(sources)]
+    main = [fetch(k, 0, slot_rows, 1) for k in range(sources)]
+    copies = [
+        pltpu.make_async_copy(source, target, sems.at[2 + i])
+        for i, (source, target) in enumerate([(slab_hbm, slab), (keys_hbm, keys), (values_hbm, values)])
+    ]
+    for copy in early + copies[:1] + main + copies[1:]:
+        copy.start()
+
+    count = list_slots(slots, depth, table, listed)
+    chunks = [jnp.full((EXTRA, LANES), -1, jnp.int32) for _ in range(-(-slots // per_chunk))]
+    for slot in range(slots):
+        image, entry = table[slot // depth, slot % depth], table[slot // depth, EXTRA + slot % depth]
+        query = lax.div(jnp.maximum(entry, 0), top_count)
+        at = slot % per_chunk * query_count + query
+        chunks[slot // per_chunk] = jnp.where(lane == at, image, chunks[slot // per_chunk])
+
+    for copy in early:
+        copy.wait()
+    queries = jnp.concatenate(
+        [
+            jnp.concatenate(
+                [
+                    got[source, slot_rows + i * shared_rows : slot_rows + (i + 1) * shared_rows, :]
+                    for i in range(late // shared_rows)
+                ],
+                axis=1,
+            )
+            for source in range(sources)
+        ],
+        axis=0,
+    )
+    missing = len(chunks) * LANES - queries.shape[0]
+    if missing:
+        queries = jnp.concatenate([queries, jnp.zeros((missing, queries.shape[1]), queries.dtype)], axis=0)
+    copies[0].wait()
+    stats = index_stats(queries, slab, jnp.concatenate([chunk[:1] for chunk in chunks], axis=1), logits)
+    for c in range(len(chunks)):
+        tiles = [split_rows(stat[:, c * LANES : (c + 1) * LANES]) for stat in stats]
+        tiles = [tiles[0], pltpu.roll(tiles[1], query_count, 1), pltpu.roll(tiles[2], 2 * query_count, 1)]
+        for slot in range(c * per_chunk, min((c + 1) * per_chunk, slots)):
+            source, z = slot // depth, slot % depth
+            at = slot % per_chunk
+            owner = (source // grid_x * depth + z) * grid_x + source % grid_x
+            part = lane // query_count
+            tile = jnp.where(part == at, tiles[0], jnp.where(part == (at + 1) % per_chunk, tiles[1], tiles[2]))
+            out[owner, body:, :] = tile.astype(jnp.bfloat16)
+    stats_out = pltpu.make_async_copy(
+        out.at[:, pl.ds(body, EXTRA), :], out_hbm.at[:, pl.ds(body, EXTRA), :], sems.at[5]
+    )
+    stats_out.start()
+
+    def send(owner):
+        return pltpu.make_async_copy(out.at[owner, pl.ds(0, body), :], out_hbm.at[owner, pl.ds(0, body), :], sems.at[6])
+
+    for copy in main + copies[1:]:
+        copy.wait()
+    attend_slots(
+        count, listed, table, got, keys, values, out, send, grid_x=grid_x, depth=depth, rows=rows, head_size=head_size
+    )
+    stats_out.wait()
+
+
+def second_serve(place, table, arrived, slab, keys, values, grid_y, grid_x, depth, rows, query_count, top_count, head_size):
+    sources = grid_y * grid_x
+    slots = sources * depth
+    body = keys.shape[2] // LANES * rows
+    lanes = -(-slots * query_count // LANES) * LANES
+    operands = [*arrived, slab, keys, values]
+    return pl.pallas_call(
         functools.partial(
-            serve_kernel,
+            second_serve_kernel,
+            grid_y=grid_y,
             grid_x=grid_x,
             depth=depth,
             rows=rows,
@@ -322,43 +447,54 @@
             top_count=top_count,
             head_size=head_size,
         ),
-        grid=(1,),
-        in_specs=[pl.BlockSpec(memory_space=pltpu.HBM)] * 4,
-        out_specs=pl.BlockSpec(memory_space=pltpu.HBM),
-        scratch_shapes=[pltpu.VMEM((slots, body + EXTRA, LANES), jnp.bfloat16)]
-        + [pltpu.VMEM(a.shape, a.dtype) for a in operands]
-        + [
-            pltpu.VMEM((slab.shape[0], lanes), jnp.float32),
-            pltpu.VMEM(codes, jnp.int32),
-            pltpu.SMEM(codes, jnp.int32),
-            pltpu.SMEM((slots + UNROLL,), jnp.int32),
-            pltpu.SemaphoreType.DMA((8,)),
-        ],
+        grid_spec=pltpu.PrefetchScalarGridSpec(
+            num_scalar_prefetch=2,
+            grid=(1,),
+            in_specs=[pl.BlockSpec(memory_space=pltpu.HBM)] * len(operands),
+            out_specs=pl.BlockSpec(memory_space=pltpu.HBM),
+            scratch_shapes=[
+                pltpu.VMEM((slots, body + EXTRA, LANES), jnp.bfloat16),
+                pltpu.VMEM((sources, *arrived[0].shape), jnp.bfloat16),
+            ]
+            + [pltpu.VMEM(a.shape, a.dtype) for a in (slab, keys, values)]
+            + [
+                pltpu.VMEM((slab.shape[0], lanes), jnp.float32),
+                pltpu.SMEM((slots + UNROLL,), jnp.int32),
+                pltpu.SemaphoreType.DMA((7,)),
+            ],
+        ),
         out_shape=pltpu.HBM((slots, body + EXTRA, LANES), jnp.bfloat16),
         compiler_params=pltpu.CompilerParams(vmem_limit_bytes=VMEM_LIMIT),
-        cost_estimate=pl.CostEstimate(flops=8 << 30, bytes_accessed=14 << 20, transcendentals=2 << 20),
-        name="serve",
-    )(*[in_hbm(a) for a in operands])
+        cost_estimate=pl.CostEstimate(flops=6 << 30, bytes_accessed=10 << 20, transcendentals=2 << 20),
+        name="second_serve",
+    )(place, table, *[in_hbm(a) for a in operands])
 
 
 def finish_kernel(
-    shards, place, back_hbm, text, w_out, gain, found, out,
+    shards, place, first_hbm, second_hbm, text, w_out, gain, found, out,
     exact, normalizers, gathered, back, sent, sems, *, top_count, query_count, shift
 ):
     step = pl.program_id(0)
     rows = text.shape[1]
     body = back.shape[1]
+    half = body // 2
 
     def fetch(entry, query):
-        return pltpu.make_async_copy(back_hbm.at[shards[entry], pl.ds(0, body), :], back.at[entry], sems.at[query])
+        return [
+            pltpu.make_async_copy(
+                source.at[shards[entry], pl.ds(0, half), :], back.at[entry, pl.ds(i * half, half), :], sems.at[query]
+            )
+            for i, source in enumerate((first_hbm, second_hbm))
+        ]
 
     @pl.when(step == 0)
     def _():
-        stats = pltpu.make_async_copy(back_hbm.at[:, pl.ds(body, EXTRA), :], sent, sems.at[query_count])
+        stats = pltpu.make_async_copy(second_hbm.at[:, pl.ds(half, EXTRA), :], sent, sems.at[query_count])
         stats.start()
         for query in range(query_count):
             for k in range(top_count):
-                fetch(query * top_count + k, query // text.shape[0]).start()
+                for copy in fetch(query * top_count + k, query // text.shape[0]):
+                    copy.start()
         stats.wait()
         parts = sent[...].astype(jnp.float32)
         joined = jnp.sum(jnp.where(row_of(parts.shape, 1) < 3, parts, 0.0), axis=1)
@@ -385,7 +521,8 @@
 
     entries = per_step * top_count
     for k in range(entries):
-        fetch(step * entries + k, step).wait()
+        for copy in fetch(step * entries + k, step):
+            copy.wait()
     for k in range(entries):
         for j in range(body // rows):
             gathered[k * rows : (k + 1) * rows, j * LANES : (j + 1) * LANES] = back[
@@ -401,7 +538,7 @@
     out[...] = normed.astype(jnp.bfloat16)
 
 
-def finish(shards, place, back, text, w_out, gain, top_count, shift):
+def finish(shards, place, first, second, text, w_out, gain, top_count, shift):
     query_count, rows, width = text.shape
     per_step = 2
     full = lambda a: pl.BlockSpec(a.shape, lambda i, *_: (0,) * a.ndim)
@@ -412,6 +549,7 @@
             grid=(query_count // per_step,),
             in_specs=[
                 pl.BlockSpec(memory_space=pltpu.HBM),
+                pl.BlockSpec(memory_space=pltpu.HBM),
                 pl.BlockSpec((per_step, rows, width), lambda i, *_: (i, 0, 0)),
                 full(w_out),
                 full(gain),
@@ -421,11 +559,11 @@
                 pl.BlockSpec((per_step, top_count, rows, width), lambda i, *_: (i, 0, 0, 0)),
             ],
             scratch_shapes=[
-                pltpu.VMEM((back.shape[0], LANES), jnp.float32),
+                pltpu.VMEM((first.shape[0], LANES), jnp.float32),
                 pltpu.VMEM((EXTRA, LANES), jnp.float32),
                 pltpu.VMEM((per_step * top_count * rows, width), jnp.bfloat16),
-                pltpu.VMEM((query_count * top_count, back.shape[1] - EXTRA, LANES), jnp.bfloat16),
-                pltpu.VMEM((back.shape[0], EXTRA, LANES), jnp.bfloat16),
+                pltpu.VMEM((query_count * top_count, 2 * first.shape[1], LANES), jnp.bfloat16),
+                pltpu.VMEM((first.shape[0], EXTRA, LANES), jnp.bfloat16),
                 pltpu.SemaphoreType.DMA((query_count + 1,)),
             ],
         ),
@@ -438,7 +576,7 @@
             flops=2 * query_count * top_count * rows * width * width, bytes_accessed=7 << 20, transcendentals=0
         ),
         name="finish",
-    )(shards, place, in_hbm(back), text, in_hbm(w_out), gain)
+    )(shards, place, in_hbm(first), in_hbm(second), text, in_hbm(w_out), gain)
 
 
 def project_rows(rows_in, weight):
@@ -477,19 +615,30 @@
         slab_count,
     )
     owners = lax.all_gather(sent, "shard", axis=0, tiled=True, axis_index_groups=columns)
-    request = make_request(
-        here_z.reshape(1),
-        owners.reshape(depth, sent.shape[0], model_width),
-        grid_y,
-        grid_x,
-        text_count,
-        query_count,
-        top_count,
-    )
+    owners = owners.reshape(depth, sent.shape[0], model_width)
+    at = jnp.stack([here_z, here_y, here_x])
+    request = first_request(at, owners, grid_y, grid_x, text_count, top_count)
     got = lax.all_to_all(request, "shard", split_axis=0, concat_axis=0, tiled=True, axis_index_groups=planes)
-
-    keys = project_rows(patches, jnp.concatenate([w_key, lax.ppermute(w_key, "rep", swap)], axis=1))
-    values = project_rows(patches, jnp.concatenate([w_value, lax.ppermute(w_value, "rep", swap)], axis=1))
+    context_first, codes = first_serve(
+        got, project_rows(patches, w_key), project_rows(patches, w_value), grid_x, depth, text_count, head_size
+    )
+    back_first = lax.all_to_all(context_first, "shard", split_axis=0, concat_axis=0, tiled=True)
+
+    request = second_request(at, codes, owners, grid_y, grid_x, text_count, query_count, top_count)
+    arrived = [request[0]]
+    for k in range(1, grid_y * grid_x):
+        moves = [
+            (
+                (y * depth + z) * grid_x + x,
+                ((y + k // grid_x) % grid_y * depth + z) * grid_x + (x + k % grid_x) % grid_x,
+            )
+            for y in range(grid_y)
+            for z in range(depth)
+            for x in range(grid_x)
+        ]
+        arrived.append(lax.ppermute(request[k], "shard", moves))
+    keys = project_rows(patches, lax.ppermute(w_key, "rep", swap))
+    values = project_rows(patches, lax.ppermute(w_value, "rep", swap))
     w_out_other = lax.ppermute(w_out, "rep", swap)
     half = model_width // 2
     w_out_whole = jnp.where(
@@ -504,14 +653,17 @@
         ),
     )
 
-    context = serve(got, slab, keys, values, grid_x, depth, text_count, query_count, top_count, head_size)
-    back = lax.all_to_all(context, "shard", split_axis=0, concat_axis=0, tiled=True)
+    context_second = second_serve(
+        at, codes, arrived, slab, keys, values, grid_y, grid_x, depth, text_count, query_count, top_count, head_size
+    )
+    back_second = lax.all_to_all(context_second, "shard", split_axis=0, concat_axis=0, tiled=True)
 
     place = ((here_y * grid_x + here_x) * depth + here_z) % (LANES // query_count)
     retrieval, attended = finish(
         own_anchor,
         place.reshape(1),
-        back,
+        back_first,
+        back_second,
         text_states,
         w_out_whole,
         norm_gain.reshape(1, model_width),

time: 209 us -> 224 us (1.072)
  starting transfers between devices: 17.2 us -> 52.3 us
  waiting for transfers between devices: 119 us -> 87.4 us
  Pallas kernels: 26.6 us -> 35.7 us
  matrix products: 6.97 us -> 10 us
    all_to_all x1 -> x2, waiting for transfers between devices: 73.8 us -> 36.6 us  [the longest x1 36.6 us: on_device(): lax.all_to_all(context_second, 'shard', split_axis=0, concat_axis=0, tile...]
    ppermute x2 -> x17, waiting for transfers between devices: 1.9 us -> 31.5 us  [the longest x15 31.5 us: on_device(): arrived.append(lax.ppermute(request[k], 'shard', moves))]
    all_to_all x1, waiting for transfers between devices: 39.5 us -> 15.3 us  [on_device(): lax.all_to_all(request, 'shard', split_axis=0, concat_axis=0, tiled=True,...]
    ppermute x2 -> x17, starting transfers between devices: 0.59 us -> 23.5 us  [the longest x15 22.9 us: on_device(): arrived.append(lax.ppermute(request[k], 'shard', moves))]
    all_to_all x1 -> x2, starting transfers between devices: 9.24 us -> 21.5 us  [the longest x1 12.7 us: on_device(): lax.all_to_all(context_second, 'shard', split_axis=0, concat_axis=0, tile...]
    pallas_call x2 -> x4, Pallas kernels: 17.8 us -> 27.1 us  [the longest x1 10.8 us: second_serve(): pl.pallas_call(functools.partial(second_serve_kernel, grid_y=grid_y, grid...]
    dot_general x2 -> x4, matrix products: 6.97 us -> 10 us  [project_rows(): jnp.einsum('spc,cd->spd', rows_in, weight, preferred_element_type=jnp.flo...]
  transfers between devices with their start and end apart: 6 -> 22, of which waited for: 5 -> 10; matrix products, arithmetic and copies ran while one was open for 5% -> 6% of each run, Pallas kernels for 0% -> 7%
where the time goes in v5:
time: 224 us; the launch traced here: 223 us
  waiting for transfers between devices  87.4 us (39%)
  starting transfers between devices  52.3 us (23%)
  Pallas kernels  35.7 us (16%)
  blocking collectives  31.3 us (14%)
  matrix products  10 us (4%)
  local copies, waits for them, and re-layouts  2.83 us (1%)
  other arithmetic  2.48 us (1%)
    all_to_all x1, waiting for transfers between devices, on_device(): lax.all_to_all(context_second, 'shard', split_axis=0, concat_axis=0, tile...  36.6 us
    ppermute x15, waiting for transfers between devices, on_device(): arrived.append(lax.ppermute(request[k], 'shard', moves))  31.5 us
    all_gather x1, blocking collectives, on_device(): lax.all_gather(sent, 'shard', axis=0, tiled=True, axis_index_groups=columns)  31.3 us
    ppermute x15, starting transfers between devices, on_device(): arrived.append(lax.ppermute(request[k], 'shard', moves))  22.9 us
    all_to_all x1, waiting for transfers between devices, on_device(): lax.all_to_all(request, 'shard', split_axis=0, concat_axis=0, tiled=True,...  15.3 us
    all_to_all x1, starting transfers between devices, on_device(): lax.all_to_all(context_second, 'shard', split_axis=0, concat_axis=0, tile...  12.7 us
    pallas_call x1, Pallas kernels, second_serve(): pl.pallas_call(functools.partial(second_serve_kernel, grid_y=grid_y, grid...  10.8 us
    dot_general x4, matrix products, project_rows(): jnp.einsum('spc,cd->spd', rows_in, weight, preferred_element_type=jnp.flo...  10 us
  transfers between devices with their start and end apart: 22, of which 10 were waited for; matrix products, arithmetic and copies ran while one was open for 6% of the time, Pallas kernels for 7%

profile of v5, /device:TPU:32, one launch (start us, length us, event | category | flops | bytes accessed | tf_op | source)
XLA Modules:
  0.0 223.2 jit_solution(3641642218353395024)
XLA Ops:
  0.9 2.1 collective-permute-done.w_other
  3.6 2.0 project.1
  5.6 31.3 %all_gather.3 = bf16[640,768]{1,0:T(8,128)(2,1)} all-gather(bf16[80,768]{1,0:T(8,128)(2,1)S(1)} %project.1), channel_id=1, replica_groups={{0,8,16,24,32,40,48,56},{2,10,18,26,34,42,50,58},{4,12,20,28,36,44,52,6..., dimensions={0}, use_global_device_ids=true | all-gather | bytes 1105920 | tf_op jit(solution)/shard_map/all_gather | solution.py:617
  37.0 4.5 %first_request.1 = bf16[16,136,384]{2,1,0:T(8,128)(2,1)} custom-call(s32[3]{0:T(128)S(1)} %pad_add_fusion.place, bf16[8,80,768]{2,1,0:T(8,128)(2,1)} %bitcast.23), custom_call_target="tpu_custom_call" | custom-call | flops 1048576 | bytes 4194304 | tf_op jit(solution)/shard_map/first_request/pallas_call | solution.py:117
  41.5 7.1 %all-to-all-start = ((bf16[16,136,384]{2,1,0:T(8,128)(2,1)}), bf16[16,136,384]{2,1,0:T(8,128)(2,1)}, u32[]{:S(2)}, u32[]{:S(2)}) async-start(bf16[16,136,384]{2,1,0:T(8,128)(2,1)} %first_request.1), calls=%async_computation | async-start | bytes 3342336 | tf_op jit(solution)/shard_map/all_to_all | solution.py:621
  48.6 2.5 %convolution_convert_fusion.3.keys_hbm = bf16[32,40,384]{2,1,0:T(8,128)(2,1)} fusion(bf16[32,40,1024]{2,1,0:T(8,128)(2,1)S(1)} %copy-done, bf16[1024,384]{1,0:T(8,128)(2,1)S(1)} %copy-done.6), kind=kOutput, calls=%fused_computation.3 | convolution fusion | flops 1007124480 | bytes 4390912 | tf_op jit(solution)/shard_map/spc,cd->spd/dot_general | solution.py:583
  51.2 2.5 %convolution_convert_fusion.2.values_hbm = bf16[32,40,384]{2,1,0:T(8,128)(2,1)} fusion(bf16[32,40,1024]{2,1,0:T(8,128)(2,1)S(1)} %copy-done, bf16[1024,384]{1,0:T(8,128)(2,1)S(1)} %copy-done.7), kind=kOutput, calls=%fused_computation.2 | convolution fusion | flops 1007124480 | bytes 4390912 | tf_op jit(solution)/shard_map/spc,cd->spd/dot_general | solution.py:583
  53.7 15.3 %all-to-all-done.got_hbm = bf16[16,136,384]{2,1,0:T(8,128)(2,1)} async-done(((bf16[16,136,384]{2,1,0:T(8,128)(2,1)}), bf16[16,136,384]{2,1,0:T(8,128)(2,1)}, u32[]{:S(2)}, u32[]{:S(2)}) %all-to-all-start) | async-done | bytes 1671200 | tf_op jit(solution)/shard_map/all_to_all | solution.py:621
  69.0 7.2 %first_serve.1 = (bf16[128,48,128]{2,1,0:T(8,128)(2,1)}, s32[16,128]{1,0:T(8,128)S(1)}) custom-call(bf16[16,136,384]{2,1,0:T(8,128)(2,1)} %all-to-all-done.got_hbm, bf16[32,40,384]{2,1,0:T(8,128)(2,1)} %convolution_convert_fusion.3.keys_hbm, bf16[32,40,384]{2,1,0:T(8,128)(2,1)} %convolution_convert_fusion.2.values_hbm), custom_call_target="tpu_custom_call" | custom-call | flops 4294967296 | bytes 6291456 | tf_op jit(solution)/shard_map/first_serve/pallas_call | solution.py:329
  76.2 8.8 %all-to-all-start.1 = ((bf16[128,48,128]{2,1,0:T(8,128)(2,1)}), bf16[128,48,128]{2,1,0:T(8,128)(2,1)}, u32[]{:S(2)}, u32[]{:S(2)}) async-start(bf16[128,48,128]{2,1,0:T(8,128)(2,1)} %get-tuple-element.20), calls=%async_computation.1 | async-start | bytes 3145728 | tf_op jit(solution)/shard_map/all_to_all | solution.py:625
  85.6 4.5 %second_request.1 = (bf16[192,384]{1,0:T(8,128)(2,1)}, bf16[192,384]{1,0:T(8,128)(2,1)}, bf16[192,384]{1,0:T(8,128)(2,1)}, bf16[192,384]{1,0:T(8,128)(2,1)}, bf1...) custom-call(s32[3]{0:T(128)S(1)} %pad_add_fusion.place, ...), custom_call_target="tpu_custom_call" | custom-call | flops 1048576 | bytes 4194304 | tf_op jit(solution)/shard_map/second_request/pallas_call | solution.py:162
  90.1 1.5 collective-permute-start.1
  91.7 2.7 %collective-permute-start.2 = (bf16[192,384]{1,0:T(8,128)(2,1)}, bf16[192,384]{1,0:T(8,128)(2,1)S(1)}, u32[]{:S(2)}, u32[]{:S(2)}) collective-permute-start(bf16[192,384]{1,0:T(8,128)(2,1)} %get-tuple-element.24), channel_id=1, source_target_pairs={{0,4},{2,6},{4,0},{6,2},{8,12},{10,14},{12,8},{14,10},{16,20},{18,... | collective-permute-start | bytes 442376 | tf_op jit(solution)/shard_map/ppermute | solution.py:639
  95.8 1.6 collective-permute-start.4
  97.4 1.7 collective-permute-start.5
  99.1 8.4 %collective-permute-done.1.rest_1_ = bf16[192,384]{1,0:T(8,128)(2,1)S(1)} collective-permute-done((bf16[192,384]{1,0:T(8,128)(2,1)}, bf16[192,384]{1,0:T(8,128)(2,1)S(1)}, u32[]{:S(2)}, u32[]{:S(2)}) %collective-permute-start.1) | collective-permute-done | bytes 147488 | tf_op jit(solution)/shard_map/ppermute | solution.py:639
  107.9 3.5 %collective-permute-start.8 = (bf16[192,384]{1,0:T(8,128)(2,1)}, bf16[192,384]{1,0:T(8,128)(2,1)S(1)}, u32[]{:S(2)}, u32[]{:S(2)}) collective-permute-start(bf16[192,384]{1,0:T(8,128)(2,1)} %get-tuple-element.30), channel_id=1, source_target_pairs={{0,128},{2,130},{4,132},{6,134},{8,136},{10,138},{12,140},{14,142}... | collective-permute-start | bytes 442376 | tf_op jit(solution)/shard_map/ppermute | solution.py:639
  111.4 2.6 %collective-permute-start.9 = (bf16[192,384]{1,0:T(8,128)(2,1)}, bf16[192,384]{1,0:T(8,128)(2,1)S(1)}, u32[]{:S(2)}, u32[]{:S(2)}) collective-permute-start(bf16[192,384]{1,0:T(8,128)(2,1)} %get-tuple-element.31), channel_id=1, source_target_pairs={{0,130},{2,132},{4,134},{6,128},{8,138},{10,140},{12,142},{14,136}... | collective-permute-start | bytes 442376 | tf_op jit(solution)/shard_map/ppermute | solution.py:639
  114.0 2.8 %collective-permute-done.5.rest_5_ = bf16[192,384]{1,0:T(8,128)(2,1)S(1)} collective-permute-done((bf16[192,384]{1,0:T(8,128)(2,1)}, bf16[192,384]{1,0:T(8,128)(2,1)S(1)}, u32[]{:S(2)}, u32[]{:S(2)}) %collective-permute-start.5) | collective-permute-done | bytes 147488 | tf_op jit(solution)/shard_map/ppermute | solution.py:639
  116.9 2.3 %collective-permute-start.10 = (bf16[192,384]{1,0:T(8,128)(2,1)}, bf16[192,384]{1,0:T(8,128)(2,1)S(1)}, u32[]{:S(2)}, u32[]{:S(2)}) collective-permute-start(bf16[192,384]{1,0:T(8,128)(2,1)} %get-tuple-element.32), channel_id=1, source_target_pairs={{0,132},{2,134},{4,128},{6,130},{8,140},{10,142},{12,136},{14,138}... | collective-permute-start | bytes 442376 | tf_op jit(solution)/shard_map/ppermute | solution.py:639
  119.2 2.5 %convolution_convert_fusion.1.rest_17_ = bf16[32,40,384]{2,1,0:T(8,128)(2,1)} fusion(bf16[32,40,1024]{2,1,0:T(8,128)(2,1)S(1)} %copy-done, bf16[1024,384]{1,0:T(8,128)(2,1)S(1)} %collective-permute-done.16), kind=kOutput, calls=%fused_computation.1 | convolution fusion | flops 1007124480 | bytes 4390912 | tf_op jit(solution)/shard_map/spc,cd->spd/dot_general | solution.py:583
  123.6 1.6 collective-permute-start.12
  125.2 10.4 %collective-permute-done.8.rest_8_ = bf16[192,384]{1,0:T(8,128)(2,1)S(1)} collective-permute-done((bf16[192,384]{1,0:T(8,128)(2,1)}, bf16[192,384]{1,0:T(8,128)(2,1)S(1)}, u32[]{:S(2)}, u32[]{:S(2)}) %collective-permute-start.8) | collective-permute-done | bytes 147488 | tf_op jit(solution)/shard_map/ppermute | solution.py:639
  135.7 2.2 %collective-permute-start.14 = (bf16[192,384]{1,0:T(8,128)(2,1)S(1)}, bf16[192,384]{1,0:T(8,128)(2,1)S(1)}, u32[]{:S(2)}, u32[]{:S(2)}) collective-permute-start(bf16[192,384]{1,0:T(8,128)(2,1)S(1)} %copy-done.11), channel_id=1, source_target_pairs={{0,196},{2,198},{4,192},{6,194},{8,204},{10,206},{12,200},{14,202}... | collective-permute-start | bytes 442376 | tf_op jit(solution)/shard_map/ppermute | solution.py:639
  139.3 2.5 %convolution_convert_fusion.rest_18_ = bf16[32,40,384]{2,1,0:T(8,128)(2,1)} fusion(bf16[32,40,1024]{2,1,0:T(8,128)(2,1)S(1)} %copy-done, bf16[1024,384]{1,0:T(8,128)(2,1)S(1)} %collective-permute-done.17), kind=kOutput, calls=%fused_computation | convolution fusion | flops 1007124480 | bytes 4390912 | tf_op jit(solution)/shard_map/spc,cd->spd/dot_general | solution.py:583
  141.8 7.9 %collective-permute-done.13.rest_13_ = bf16[192,384]{1,0:T(8,128)(2,1)S(1)} collective-permute-done((bf16[192,384]{1,0:T(8,128)(2,1)S(1)}, bf16[192,384]{1,0:T(8,128)(2,1)S(1)}, u32[]{:S(2)}, u32[]{:S(2)}) %collective-permute-start.13) | collective-permute-done | bytes 147488 | tf_op jit(solution)/shard_map/ppermute | solution.py:639
  150.6 10.8 %second_serve.1 = bf16[128,56,128]{2,1,0:T(8,128)(2,1)} custom-call(s32[3]{0:T(128)S(1)} %pad_add_fusion.place, s32[16,128]{1,0:T(8,128)S(1)} %get-tuple-element.21.after.table, bf16[192,384]{1,0:T(8,128)(2,1)} %get-tuple-element.22.rest_0_, bf16[192,384]{1,0:T(8,128)(2,1)} %copy-done.8, bf16[192,384]{1,0:T(8,128)(2,1)} %copy-done.10, ...), custom_call_target="tpu_custom_call" | custom-call | flops 6442450944 | bytes 10485760 | tf_op jit(solution)/shard_map/second_serve/pallas_call | solution.py:439
  161.4 12.7 %all-to-all-start.2 = ((bf16[128,56,128]{2,1,0:T(8,128)(2,1)}), bf16[128,56,128]{2,1,0:T(8,128)(2,1)}, u32[]{:S(2)}, u32[]{:S(2)}) async-start(bf16[128,56,128]{2,1,0:T(8,128)(2,1)} %second_serve.1), calls=%async_computation.2 | async-start | bytes 3670016 | tf_op jit(solution)/shard_map/all_to_all | solution.py:659
  174.5 1.9 collective-permute-done.18
  177.5 2.4 %maximum_select_fusion.w_out = bf16[768,768]{1,0:T(8,128)(2,1)} fusion(bf16[768,384]{1,0:T(8,128)(2,1)} %collective-permute-done.18, bf16[768,384]{1,0:T(8,128)(2,1)S(1)} %copy-done.4, bf16[384,384]{1,0:T(8,128)(2,1)S(1)} %get-tuple-element.41, bf16[384,384]{1,0:T(8,128)(2,1)S(1)} %get-tuple-element.39, bf16[384,384]{1,0:T(8,128)(2,1)S(1)} %get-tuple-element.40, ...), kind=kLoop, calls=%fused_computation.4 | loop fusion | flops 7667712 | bytes 3538945 | tf_op jit(solution)/shard_map/jit(_where)/select_n | solution.py:644
  179.9 36.6 %all-to-all-done.2.second_hbm = bf16[128,56,128]{2,1,0:T(8,128)(2,1)} async-done(((bf16[128,56,128]{2,1,0:T(8,128)(2,1)}), bf16[128,56,128]{2,1,0:T(8,128)(2,1)}, u32[]{:S(2)}, u32[]{:S(2)}) %all-to-all-start.2) | async-done | bytes 1835040 | tf_op jit(solution)/shard_map/all_to_all | solution.py:659
  216.5 6.6 %finish.1 = (f32[4,16]{1,0:T(4,128)}, bf16[4,16,16,768]{3,2,1,0:T(8,128)(2,1)}) custom-call(s32[64]{0:T(128)S(1)} %and_select_fusion.shards, s32[1]{0:T(128)} %bitcast.place, bf16[128,48,128]{2,1,0:T(8,128)(2,1)} %all-to-all-done.1.first_hbm, bf16[128,56,128]{2,1,0:T(8,128)(2,1)} %all-to-all-done.2.second_hbm, bf16[4,16,768]{2,1,0:T(8,128)(2,1)S(1)} %copy-done.1, ...), custom_call_target="tpu_custom_call" | custom-call | flops 1207959552 | bytes 7340032 | tf_op jit(solution)/shard_map/finish/pallas_call | solution.py:545
  (86 shorter events, 8.8 us)
Async XLA Ops:
  0.6 48.0 %copy-start = (bf16[32,40,1024]{2,1,0:T(8,128)(2,1)S(1)}, bf16[32,40,1024]{2,1,0:T(8,128)(2,1)}, u32[]{:S(2)}) copy-start(bf16[32,40,1024]{2,1,0:T(8,128)(2,1)} %param.13) | copy-start | bytes 7864324
  0.6 2.3 %collective-permute-start = (bf16[768,384]{1,0:T(8,128)(2,1)}, bf16[768,384]{1,0:T(8,128)(2,1)S(1)}, u32[]{:S(2)}, u32[]{:S(2)}) collective-permute-start(bf16[768,384]{1,0:T(8,128)(2,1)} %w_own.1), channel_id=1, source_target_pairs={{0,1},{1,0},{2,3},{3,2},{4,5},{5,4},{6,7},{7,6},{8,9},{9,8},{10,11... | collective-permute-start | bytes 1769480 | tf_op jit(solution)/shard_map/ppermute | solution.py:605
  41.5 27.5 %all-to-all-start = ((bf16[16,136,384]{2,1,0:T(8,128)(2,1)}), bf16[16,136,384]{2,1,0:T(8,128)(2,1)}, u32[]{:S(2)}, u32[]{:S(2)}) async-start(bf16[16,136,384]{2,1,0:T(8,128)(2,1)} %first_request.1), calls=%async_computation | async-start | bytes 3342336 | tf_op jit(solution)/shard_map/all_to_all | solution.py:621
  76.2 85.2 %all-to-all-start.1 = ((bf16[128,48,128]{2,1,0:T(8,128)(2,1)}), bf16[128,48,128]{2,1,0:T(8,128)(2,1)}, u32[]{:S(2)}, u32[]{:S(2)}) async-start(bf16[128,48,128]{2,1,0:T(8,128)(2,1)} %get-tuple-element.20), calls=%async_computation.1 | async-start | bytes 3145728 | tf_op jit(solution)/shard_map/all_to_all | solution.py:625
  85.0 10.8 %collective-permute-start.16 = (bf16[1024,384]{1,0:T(8,128)(2,1)S(1)}, bf16[1024,384]{1,0:T(8,128)(2,1)S(1)}, u32[]{:S(2)}, u32[]{:S(2)}) collective-permute-start(bf16[1024,384]{1,0:T(8,128)(2,1)S(1)} %copy-done.6), channel_id=1, source_target_pairs={{0,1},{1,0},{2,3},{3,2},{4,5},{5,4},{6,7},{7,6},{8,9},{9,8},{10,11... | collective-permute-start | bytes 2359304 | tf_op jit(solution)/shard_map/ppermute | solution.py:640
  85.1 12.3 %collective-permute-start.17 = (bf16[1024,384]{1,0:T(8,128)(2,1)}, bf16[1024,384]{1,0:T(8,128)(2,1)S(1)}, u32[]{:S(2)}, u32[]{:S(2)}) collective-permute-start(bf16[1024,384]{1,0:T(8,128)(2,1)} %param.17), channel_id=1, source_target_pairs={{0,1},{1,0},{2,3},{3,2},{4,5},{5,4},{6,7},{7,6},{8,9},{9,8},{10,11... | collective-permute-start | bytes 2359304 | tf_op jit(solution)/shard_map/ppermute | solution.py:641
  90.1 17.4 %collective-permute-start.1 = (bf16[192,384]{1,0:T(8,128)(2,1)}, bf16[192,384]{1,0:T(8,128)(2,1)S(1)}, u32[]{:S(2)}, u32[]{:S(2)}) collective-permute-start(bf16[192,384]{1,0:T(8,128)(2,1)} %get-tuple-element.23), channel_id=1, source_target_pairs={{0,2},{2,4},{4,6},{6,0},{8,10},{10,12},{12,14},{14,8},{16,18},{18,... | collective-permute-start | bytes 442376 | tf_op jit(solution)/shard_map/ppermute | solution.py:639
  91.7 16.1 %collective-permute-start.2 = (bf16[192,384]{1,0:T(8,128)(2,1)}, bf16[192,384]{1,0:T(8,128)(2,1)S(1)}, u32[]{:S(2)}, u32[]{:S(2)}) collective-permute-start(bf16[192,384]{1,0:T(8,128)(2,1)} %get-tuple-element.24), channel_id=1, source_target_pairs={{0,4},{2,6},{4,0},{6,2},{8,12},{10,14},{12,8},{14,10},{16,20},{18,... | collective-permute-start | bytes 442376 | tf_op jit(solution)/shard_map/ppermute | solution.py:639
  94.4 13.5 %collective-permute-start.3 = (bf16[192,384]{1,0:T(8,128)(2,1)}, bf16[192,384]{1,0:T(8,128)(2,1)S(1)}, u32[]{:S(2)}, u32[]{:S(2)}) collective-permute-start(bf16[192,384]{1,0:T(8,128)(2,1)} %get-tuple-element.25), channel_id=1, source_target_pairs={{0,6},{2,0},{4,2},{6,4},{8,14},{10,8},{12,10},{14,12},{16,22},{18,... | collective-permute-start | bytes 442376 | tf_op jit(solution)/shard_map/ppermute | solution.py:639
  95.8 15.6 %collective-permute-start.4 = (bf16[192,384]{1,0:T(8,128)(2,1)}, bf16[192,384]{1,0:T(8,128)(2,1)S(1)}, u32[]{:S(2)}, u32[]{:S(2)}) collective-permute-start(bf16[192,384]{1,0:T(8,128)(2,1)} %get-tuple-element.26), channel_id=1, source_target_pairs={{0,64},{2,66},{4,68},{6,70},{8,72},{10,74},{12,76},{14,78},{16,80}... | collective-permute-start | bytes 442376 | tf_op jit(solution)/shard_map/ppermute | solution.py:639
  97.4 19.4 %collective-permute-start.5 = (bf16[192,384]{1,0:T(8,128)(2,1)}, bf16[192,384]{1,0:T(8,128)(2,1)S(1)}, u32[]{:S(2)}, u32[]{:S(2)}) collective-permute-start(bf16[192,384]{1,0:T(8,128)(2,1)} %get-tuple-element.27), channel_id=1, source_target_pairs={{0,66},{2,68},{4,70},{6,64},{8,74},{10,76},{12,78},{14,72},{16,82}... | collective-permute-start | bytes 442376 | tf_op jit(solution)/shard_map/ppermute | solution.py:639
  107.5 14.2 %copy-start.8 = (bf16[192,384]{1,0:T(8,128)(2,1)}, bf16[192,384]{1,0:T(8,128)(2,1)S(1)}, u32[]{:S(2)}) copy-start(bf16[192,384]{1,0:T(8,128)(2,1)S(1)} %collective-permute-done.1.rest_1_) | copy-start | bytes 442372
  107.5 15.7 %collective-permute-start.6 = (bf16[192,384]{1,0:T(8,128)(2,1)}, bf16[192,384]{1,0:T(8,128)(2,1)S(1)}, u32[]{:S(2)}, u32[]{:S(2)}) collective-permute-start(bf16[192,384]{1,0:T(8,128)(2,1)} %get-tuple-element.28), channel_id=1, source_target_pairs={{0,68},{2,70},{4,64},{6,66},{8,76},{10,78},{12,72},{14,74},{16,84}... | collective-permute-start | bytes 442376 | tf_op jit(solution)/shard_map/ppermute | solution.py:639
  107.8 13.9 %copy-start.10 = (bf16[192,384]{1,0:T(8,128)(2,1)}, bf16[192,384]{1,0:T(8,128)(2,1)S(1)}, u32[]{:S(2)}) copy-start(bf16[192,384]{1,0:T(8,128)(2,1)S(1)} %collective-permute-done.2.rest_2_) | copy-start | bytes 442372
  107.8 15.8 %collective-permute-start.7 = (bf16[192,384]{1,0:T(8,128)(2,1)}, bf16[192,384]{1,0:T(8,128)(2,1)S(1)}, u32[]{:S(2)}, u32[]{:S(2)}) collective-permute-start(bf16[192,384]{1,0:T(8,128)(2,1)} %get-tuple-element.29), channel_id=1, source_target_pairs={{0,70},{2,64},{4,66},{6,68},{8,78},{10,72},{12,74},{14,76},{16,86}... | collective-permute-start | bytes 442376 | tf_op jit(solution)/shard_map/ppermute | solution.py:639
  107.9 13.9 %copy-start.12 = (bf16[192,384]{1,0:T(8,128)(2,1)}, bf16[192,384]{1,0:T(8,128)(2,1)S(1)}, u32[]{:S(2)}) copy-start(bf16[192,384]{1,0:T(8,128)(2,1)S(1)} %collective-permute-done.3.rest_3_) | copy-start | bytes 442372
  107.9 27.8 %collective-permute-start.8 = (bf16[192,384]{1,0:T(8,128)(2,1)}, bf16[192,384]{1,0:T(8,128)(2,1)S(1)}, u32[]{:S(2)}, u32[]{:S(2)}) collective-permute-start(bf16[192,384]{1,0:T(8,128)(2,1)} %get-tuple-element.30), channel_id=1, source_target_pairs={{0,128},{2,130},{4,132},{6,134},{8,136},{10,138},{12,140},{14,142}... | collective-permute-start | bytes 442376 | tf_op jit(solution)/shard_map/ppermute | solution.py:639
  111.4 24.3 %collective-permute-start.9 = (bf16[192,384]{1,0:T(8,128)(2,1)}, bf16[192,384]{1,0:T(8,128)(2,1)S(1)}, u32[]{:S(2)}, u32[]{:S(2)}) collective-permute-start(bf16[192,384]{1,0:T(8,128)(2,1)} %get-tuple-element.31), channel_id=1, source_target_pairs={{0,130},{2,132},{4,134},{6,128},{8,138},{10,140},{12,142},{14,136}... | collective-permute-start | bytes 442376 | tf_op jit(solution)/shard_map/ppermute | solution.py:639
  116.9 18.8 %copy-start.13 = (bf16[192,384]{1,0:T(8,128)(2,1)S(1)}, bf16[192,384]{1,0:T(8,128)(2,1)}, u32[]{:S(2)}) copy-start(bf16[192,384]{1,0:T(8,128)(2,1)} %get-tuple-element.35) | copy-start | bytes 442372
  116.9 18.8 %copy-start.11 = (bf16[192,384]{1,0:T(8,128)(2,1)S(1)}, bf16[192,384]{1,0:T(8,128)(2,1)}, u32[]{:S(2)}) copy-start(bf16[192,384]{1,0:T(8,128)(2,1)} %get-tuple-element.36) | copy-start | bytes 442372
  116.9 21.1 %copy-start.9 = (bf16[192,384]{1,0:T(8,128)(2,1)S(1)}, bf16[192,384]{1,0:T(8,128)(2,1)}, u32[]{:S(2)}) copy-start(bf16[192,384]{1,0:T(8,128)(2,1)} %get-tuple-element.37) | copy-start | bytes 442372
  116.9 21.0 %collective-permute-start.10 = (bf16[192,384]{1,0:T(8,128)(2,1)}, bf16[192,384]{1,0:T(8,128)(2,1)S(1)}, u32[]{:S(2)}, u32[]{:S(2)}) collective-permute-start(bf16[192,384]{1,0:T(8,128)(2,1)} %get-tuple-element.32), channel_id=1, source_target_pairs={{0,132},{2,134},{4,128},{6,130},{8,140},{10,142},{12,136},{14,138}... | collective-permute-start | bytes 442376 | tf_op jit(solution)/shard_map/ppermute | solution.py:639
  123.2 18.5 %copy-start.18 = (bf16[192,384]{1,0:T(8,128)(2,1)}, bf16[192,384]{1,0:T(8,128)(2,1)S(1)}, u32[]{:S(2)}) copy-start(bf16[192,384]{1,0:T(8,128)(2,1)S(1)} %collective-permute-done.6.rest_6_) | copy-start | bytes 442372
  123.2 18.6 %collective-permute-start.11 = (bf16[192,384]{1,0:T(8,128)(2,1)S(1)}, bf16[192,384]{1,0:T(8,128)(2,1)S(1)}, u32[]{:S(2)}, u32[]{:S(2)}) collective-permute-start(bf16[192,384]{1,0:T(8,128)(2,1)S(1)} %copy-done.16), channel_id=1, source_target_pairs={{0,134},{2,128},{4,130},{6,132},{8,142},{10,136},{12,138},{14,140}... | collective-permute-start | bytes 442376 | tf_op jit(solution)/shard_map/ppermute | solution.py:639
  123.6 18.2 %copy-start.19 = (bf16[192,384]{1,0:T(8,128)(2,1)}, bf16[192,384]{1,0:T(8,128)(2,1)S(1)}, u32[]{:S(2)}) copy-start(bf16[192,384]{1,0:T(8,128)(2,1)S(1)} %collective-permute-done.7.rest_7_) | copy-start | bytes 442372
  123.6 18.2 %collective-permute-start.12 = (bf16[192,384]{1,0:T(8,128)(2,1)S(1)}, bf16[192,384]{1,0:T(8,128)(2,1)S(1)}, u32[]{:S(2)}, u32[]{:S(2)}) collective-permute-start(bf16[192,384]{1,0:T(8,128)(2,1)S(1)} %copy-done.14), channel_id=1, source_target_pairs={{0,192},{2,194},{4,196},{6,198},{8,200},{10,202},{12,204},{14,206}... | collective-permute-start | bytes 442376 | tf_op jit(solution)/shard_map/ppermute | solution.py:639
  135.6 14.1 %collective-permute-start.13 = (bf16[192,384]{1,0:T(8,128)(2,1)S(1)}, bf16[192,384]{1,0:T(8,128)(2,1)S(1)}, u32[]{:S(2)}, u32[]{:S(2)}) collective-permute-start(bf16[192,384]{1,0:T(8,128)(2,1)S(1)} %copy-done.13), channel_id=1, source_target_pairs={{0,194},{2,196},{4,198},{6,192},{8,202},{10,204},{12,206},{14,200}... | collective-permute-start | bytes 442376 | tf_op jit(solution)/shard_map/ppermute | solution.py:639
  135.7 14.1 %collective-permute-start.14 = (bf16[192,384]{1,0:T(8,128)(2,1)S(1)}, bf16[192,384]{1,0:T(8,128)(2,1)S(1)}, u32[]{:S(2)}, u32[]{:S(2)}) collective-permute-start(bf16[192,384]{1,0:T(8,128)(2,1)S(1)} %copy-done.11), channel_id=1, source_target_pairs={{0,196},{2,198},{4,192},{6,194},{8,204},{10,206},{12,200},{14,202}... | collective-permute-start | bytes 442376 | tf_op jit(solution)/shard_map/ppermute | solution.py:639
  137.9 11.9 %collective-permute-start.15 = (bf16[192,384]{1,0:T(8,128)(2,1)S(1)}, bf16[192,384]{1,0:T(8,128)(2,1)S(1)}, u32[]{:S(2)}, u32[]{:S(2)}) collective-permute-start(bf16[192,384]{1,0:T(8,128)(2,1)S(1)} %copy-done.9), channel_id=1, source_target_pairs={{0,198},{2,192},{4,194},{6,196},{8,206},{10,200},{12,202},{14,204}... | collective-permute-start | bytes 442376 | tf_op jit(solution)/shard_map/ppermute | solution.py:639
  161.4 55.0 %all-to-all-start.2 = ((bf16[128,56,128]{2,1,0:T(8,128)(2,1)}), bf16[128,56,128]{2,1,0:T(8,128)(2,1)}, u32[]{:S(2)}, u32[]{:S(2)}) async-start(bf16[128,56,128]{2,1,0:T(8,128)(2,1)} %second_serve.1), calls=%async_computation.2 | async-start | bytes 3670016 | tf_op jit(solution)/shard_map/all_to_all | solution.py:659
  174.2 2.2 collective-permute-start.18
  174.5 42.0 %copy-start.1 = (bf16[4,16,768]{2,1,0:T(8,128)(2,1)S(1)}, bf16[4,16,768]{2,1,0:T(8,128)(2,1)}, u32[]{:S(2)}) copy-start(bf16[4,16,768]{2,1,0:T(8,128)(2,1)} %text.1) | copy-start | bytes 294916
  (18 other events, 116.1 us)

commit v6 on v4

--- a/solution.py
+++ b/solution.py
@@ -14,12 +14,24 @@
 LANES = 128
 EXTRA = 8
 UNROLL = 16
+PAIR = 2
 GRIDS = {128: (4, 8, 4), 8: (2, 2, 2)}
 VMEM_LIMIT = 48 * 1024 * 1024
 
 
 def row_of(shape, dim):
     return lax.broadcasted_iota(jnp.int32, shape, dim)
+
+
+def split_source(source, grid_y, grid_x):
+    if isinstance(source, int):
+        return source // (grid_y * grid_x), source // grid_x % grid_y, source % grid_x
+    return lax.div(source, grid_y * grid_x), lax.rem(lax.div(source, grid_x), grid_y), lax.rem(source, grid_x)
+
+
+def owner_of(source, k, grid_y, grid_x, owned):
+    in_pair, y, x = split_source(source, grid_y, grid_x)
+    return (y * owned * PAIR + k * PAIR + in_pair) * grid_x + x
 
 
 def in_hbm(array):
@@ -66,7 +78,7 @@
             flops=2 * text.shape[0] * text.shape[1] * width, bytes_accessed=2 << 20, transcendentals=0
         ),
         name="project",
-    )(ids, *[in_hbm(a) for a in operands])
+    )(ids, in_hbm(text), in_hbm(queries), in_hbm(w_own), w_other)
 
 
 def to_scalars(vectors, decoded, table, sem):
@@ -76,7 +88,9 @@
     copy.wait()
 
 
-def request_kernel(place, owners, out, decoded, table, shared, sem, *, grid_x, rows, query_count, top_count):
+def request_kernel(
+    place, owners, out, decoded, table, shared, sem, *, grid_y, grid_x, rows, query_count, top_count
+):
     step = pl.program_id(0)
     depth, height = owners.shape[:2]
     texts = height - 2 * EXTRA
@@ -97,7 +111,8 @@
     lane = row_of((EXTRA, LANES), 1)
     for i in range(out.shape[0]):
         target = step * out.shape[0] + i
-        shard = (lax.div(target, grid_x) * depth + place[0]) * grid_x + lax.rem(target, grid_x)
+        in_pair, y, x = split_source(target, grid_y, grid_x)
+        shard = (y * depth * PAIR + place[0] + in_pair) * grid_x + x
         code = jnp.full((EXTRA, LANES), -1.0, jnp.float32)
         for z in range(depth):
             image, listed = table[z, shard], table[EXTRA + z, shard]
@@ -113,15 +128,22 @@
     depth, height, width = owners.shape
     shared_rows = depth * query_count
     total = depth * rows + shared_rows + EXTRA
+    targets = PAIR * grid_y * grid_x
+    block = min(8, targets)
     return pl.pallas_call(
         functools.partial(
-            request_kernel, grid_x=grid_x, rows=rows, query_count=query_count, top_count=top_count
+            request_kernel,
+            grid_y=grid_y,
+            grid_x=grid_x,
+            rows=rows,
+            query_count=query_count,
+            top_count=top_count,
         ),
         grid_spec=pltpu.PrefetchScalarGridSpec(
             num_scalar_prefetch=1,
-            grid=(grid_y * grid_x // 4,),
+            grid=(targets // block,),
             in_specs=[pl.BlockSpec(owners.shape, lambda i, *_: (0, 0, 0))],
-            out_specs=pl.BlockSpec((4, total, width), lambda i, *_: (i, 0, 0)),
+            out_specs=pl.BlockSpec((block, total, width), lambda i, *_: (i, 0, 0)),
             scratch_shapes=[
                 pltpu.VMEM((2 * EXTRA, LANES), jnp.int32),
                 pltpu.SMEM((2 * EXTRA, LANES), jnp.int32),
@@ -129,7 +151,7 @@
                 pltpu.SemaphoreType.DMA,
             ],
         ),
-        out_shape=pltpu.HBM((grid_y * grid_x, total, width), jnp.bfloat16),
+        out_shape=pltpu.HBM((targets, total, width), jnp.bfloat16),
         compiler_params=pltpu.CompilerParams(vmem_limit_bytes=VMEM_LIMIT),
         cost_estimate=pl.CostEstimate(flops=1 << 20, bytes_accessed=6 << 20, transcendentals=0),
         name="request",
@@ -167,7 +189,7 @@
 
 def serve_kernel(
     got_hbm, slab_hbm, keys_hbm, values_hbm, out_hbm,
-    out, got, slab, keys, values, logits, decoded, table, listed, sems, *, grid_x, depth, rows, query_count, top_count, head_size
+    out, got, slab, keys, values, logits, decoded, table, listed, sems, *, grid_y, grid_x, depth, rows, query_count, top_count, head_size
 ):
     sources = got.shape[0]
     slots = sources * depth
@@ -227,7 +249,7 @@
         for slot in range(c * per_chunk, min((c + 1) * per_chunk, slots)):
             source, z = slot // depth, slot % depth
             at = slot % per_chunk
-            owner = (source // grid_x * depth + z) * grid_x + source % grid_x
+            owner = owner_of(source, z, grid_y, grid_x, depth)
             place = lane // query_count
             tile = jnp.where(place == at, tiles[0], jnp.where(place == (at + 1) % per_chunk, tiles[1], tiles[2]))
             out[owner, body:, :] = tile.astype(jnp.bfloat16)
@@ -255,9 +277,7 @@
         chosen = [listed[index * UNROLL + g] for g in range(UNROLL)]
         places = [(lax.div(slot, depth), lax.rem(slot, depth)) for slot in chosen]
         images = [table[source, z] for source, z in places]
-        owners = [
-            (lax.div(source, grid_x) * depth + z) * grid_x + lax.rem(source, grid_x) for source, z in places
-        ]
+        owners = [owner_of(source, z, grid_y, grid_x, depth) for source, z in places]
         work = [(g, span) for g in range(UNROLL) for span in spans]
         scores = []
         for g, (at, width, masks) in work:
@@ -305,7 +325,7 @@
     stats_out.wait()
 
 
-def serve(got, slab, keys, values, grid_x, depth, rows, query_count, top_count, head_size):
+def serve(got, slab, keys, values, grid_y, grid_x, depth, rows, query_count, top_count, head_size):
     sources = got.shape[0]
     slots = sources * depth
     body = keys.shape[2] // LANES * rows
@@ -315,6 +335,7 @@
     return pl.pallas_call(
         functools.partial(
             serve_kernel,
+            grid_y=grid_y,
             grid_x=grid_x,
             depth=depth,
             rows=rows,
@@ -457,11 +478,21 @@
     text_count, model_width = text_states.shape[1:]
     head_size = model_width // HEADS
     here_x, here_z, here_y = shard_here % grid_x, shard_here // grid_x % depth, shard_here // (grid_x * depth)
+    owned = depth // PAIR
     columns = [
-        [(y * depth + z) * grid_x + x for z in range(depth)] for y in range(grid_y) for x in range(grid_x)
+        [(y * depth + k * PAIR + in_pair) * grid_x + x for k in range(owned)]
+        for y in range(grid_y)
+        for x in range(grid_x)
+        for in_pair in range(PAIR)
     ]
-    planes = [
-        [(y * depth + z) * grid_x + x for y in range(grid_y) for x in range(grid_x)] for z in range(depth)
+    pairs = [
+        [
+            (y * depth + k * PAIR + in_pair) * grid_x + x
+            for in_pair in range(PAIR)
+            for y in range(grid_y)
+            for x in range(grid_x)
+        ]
+        for k in range(owned)
     ]
     swap = [(0, 1), (1, 0)]
     w_query_other = lax.ppermute(w_query, "rep", swap)
@@ -478,15 +509,15 @@
     )
     owners = lax.all_gather(sent, "shard", axis=0, tiled=True, axis_index_groups=columns)
     request = make_request(
-        here_z.reshape(1),
-        owners.reshape(depth, sent.shape[0], model_width),
+        (here_z // PAIR * PAIR).reshape(1),
+        owners.reshape(owned, sent.shape[0], model_width),
         grid_y,
         grid_x,
         text_count,
         query_count,
         top_count,
     )
-    got = lax.all_to_all(request, "shard", split_axis=0, concat_axis=0, tiled=True, axis_index_groups=planes)
+    got = lax.all_to_all(request, "shard", split_axis=0, concat_axis=0, tiled=True, axis_index_groups=pairs)
 
     keys = project_rows(patches, jnp.concatenate([w_key, lax.ppermute(w_key, "rep", swap)], axis=1))
     values = project_rows(patches, jnp.concatenate([w_value, lax.ppermute(w_value, "rep", swap)], axis=1))
@@ -504,10 +535,13 @@
         ),
     )
 
-    context = serve(got, slab, keys, values, grid_x, depth, text_count, query_count, top_count, head_size)
+    context = serve(
+        got, slab, keys, values, grid_y, grid_x, owned, text_count, query_count, top_count, head_size
+    )
     back = lax.all_to_all(context, "shard", split_axis=0, concat_axis=0, tiled=True)
 
-    place = ((here_y * grid_x + here_x) * depth + here_z) % (LANES // query_count)
+    source = (here_z % PAIR * grid_y + here_y) * grid_x + here_x
+    place = (source * owned + here_z // PAIR) % (LANES // query_count)
     retrieval, attended = finish(
         own_anchor,
         place.reshape(1),

time: 209 us -> 200 us (0.957)
  blocking collectives: 31.3 us -> 19.8 us
  starting transfers between devices: 17.2 us -> 19.3 us
    all_gather x1, blocking collectives: 31.3 us -> 19.8 us  [on_device(): lax.all_gather(sent, 'shard', axis=0, tiled=True, axis_index_groups=columns)]
where the time goes in v6:
time: 200 us; the launch traced here: 199 us
  waiting for transfers between devices  120 us (60%)
  Pallas kernels  26.6 us (13%)
  blocking collectives  19.8 us (10%)
  starting transfers between devices  19.3 us (10%)
  matrix products  7.04 us (4%)
  other arithmetic  2.49 us (1%)
    all_to_all x1, waiting for transfers between devices, on_device(): lax.all_to_all(context, 'shard', split_axis=0, concat_axis=0, tiled=True)  73 us
    all_to_all x1, waiting for transfers between devices, on_device(): lax.all_to_all(request, 'shard', split_axis=0, concat_axis=0, tiled=True,...  41.5 us
    all_gather x1, blocking collectives, on_device(): lax.all_gather(sent, 'shard', axis=0, tiled=True, axis_index_groups=columns)  19.8 us
    pallas_call x1, Pallas kernels, serve(): pl.pallas_call(functools.partial(serve_kernel, grid_y=grid_y, grid_x=grid...  13.3 us
    all_to_all x1, starting transfers between devices, on_device(): lax.all_to_all(context, 'shard', split_axis=0, concat_axis=0, tiled=True)  9.7 us
    all_to_all x1, starting transfers between devices, on_device(): lax.all_to_all(request, 'shard', split_axis=0, concat_axis=0, tiled=True,...  8.82 us
    dot_general x2, matrix products, project_rows(): jnp.einsum('spc,cd->spd', rows_in, weight, preferred_element_type=jnp.flo...  7.04 us
    pallas_call x1, Pallas kernels, finish(): pl.pallas_call(functools.partial(finish_kernel, top_count=top_count, quer...  6.6 us
  transfers between devices with their start and end apart: 6, of which 5 were waited for; matrix products, arithmetic and copies ran while one was open for 5% of the time, Pallas kernels for 0%

profile of v6, /device:TPU:32, one launch (start us, length us, event | category | flops | bytes accessed | tf_op | source)
XLA Modules:
  0.0 198.7 jit_solution(11187905459457972350)
XLA Ops:
  0.6 0.0 copy-start
  0.6 0.1 collective-permute-start
  0.8 2.1 %collective-permute-done.w_other = bf16[768,384]{1,0:T(8,128)(2,1)S(1)} collective-permute-done((bf16[768,384]{1,0:T(8,128)(2,1)}, bf16[768,384]{1,0:T(8,128)(2,1)S(1)}, u32[]{:S(2)}, u32[]{:S(2)}) %collective-permute-start) | collective-permute-done | bytes 589856 | tf_op jit(solution)/shard_map/ppermute | solution.py:498
  2.9 0.7 copy-done.2
  3.6 2.0 %project.1 = bf16[80,768]{1,0:T(8,128)(2,1)S(1)} custom-call(s32[4,16]{1,0:T(4,128)S(1)} %copy-done.2, bf16[64,768]{1,0:T(8,128)(2,1)} %bitcast.16, bf16[4,768]{1,0:T(4,128)(2,1)} %queries.1, bf16[768,384]{1,0:T(8,128)(2,1)} %w_own.1, bf16[768,384]{1,0:T(8,128)(2,1)S(1)} %collective-permute-done.w_other), custom_call_target="tpu_custom_call" | custom-call | flops 75497472 | bytes 2097152 | tf_op jit(solution)/shard_map/project/pallas_call | solution.py:67
  5.6 19.8 %all_gather.3 = bf16[320,768]{1,0:T(8,128)(2,1)} all-gather(bf16[80,768]{1,0:T(8,128)(2,1)S(1)} %project.1), channel_id=1, replica_groups={{0,16,32,48},{8,24,40,56},{2,18,34,50},{10,26,42,58},{4,20,36,52},{12,2..., dimensions={0}, use_global_device_ids=true | all-gather | bytes 614400 | tf_op jit(solution)/shard_map/all_gather | solution.py:510
  25.5 4.6 %request.1 = bf16[32,88,768]{2,1,0:T(8,128)(2,1)} custom-call(s32[1]{0:T(128)} %bitcast.1.place, bf16[4,80,768]{2,1,0:T(8,128)(2,1)} %bitcast.17), custom_call_target="tpu_custom_call" | custom-call | flops 1048576 | bytes 6291456 | tf_op jit(solution)/shard_map/request/pallas_call | solution.py:133
  30.1 0.0 copy-start.6
  30.1 8.8 %all-to-all-start = ((bf16[32,88,768]{2,1,0:T(8,128)(2,1)}), bf16[32,88,768]{2,1,0:T(8,128)(2,1)}, u32[]{:S(2)}, u32[]{:S(2)}) async-start(bf16[32,88,768]{2,1,0:T(8,128)(2,1)} %request.1), calls=%async_computation | async-start | bytes 8650752 | tf_op jit(solution)/shard_map/all_to_all | solution.py:520
  38.9 0.0 copy-start.7
  39.0 0.1 collective-permute-start.1
  39.1 0.5 collective-permute-start.2
  39.6 1.9 collective-permute-done.1
  41.4 3.5 %convert_bitcast_fusion.1.keys_hbm = bf16[32,40,768]{2,1,0:T(8,128)(2,1)} fusion(bf16[32,40,1024]{2,1,0:T(8,128)(2,1)S(1)} %copy-done, bf16[1024,384]{1,0:T(8,128)(2,1)S(1)} %collective-permute-done.1, bf16[1024,384]{1,0:T(8,128)(2,1)S(1)} %copy-done.6), kind=kOutput, calls=%fused_computation.1 | convolution fusion | flops 2017394688 | bytes 6160384 | tf_op jit(solution)/shard_map/spc,cd->spd/dot_general | solution.py:466
  45.0 0.0 collective-permute-done.2
  45.0 0.0 copy-done.7
  45.0 3.5 %convert_bitcast_fusion.values_hbm = bf16[32,40,768]{2,1,0:T(8,128)(2,1)} fusion(bf16[32,40,1024]{2,1,0:T(8,128)(2,1)S(1)} %copy-done, bf16[1024,384]{1,0:T(8,128)(2,1)S(1)} %collective-permute-done.2, bf16[1024,384]{1,0:T(8,128)(2,1)S(1)} %copy-done.7), kind=kOutput, calls=%fused_computation | convolution fusion | flops 2017394688 | bytes 6160384 | tf_op jit(solution)/shard_map/spc,cd->spd/dot_general | solution.py:466
  48.5 41.5 %all-to-all-done.got_hbm = bf16[32,88,768]{2,1,0:T(8,128)(2,1)} async-done(((bf16[32,88,768]{2,1,0:T(8,128)(2,1)}), bf16[32,88,768]{2,1,0:T(8,128)(2,1)}, u32[]{:S(2)}, u32[]{:S(2)}) %all-to-all-start) | async-done | bytes 4325408 | tf_op jit(solution)/shard_map/all_to_all | solution.py:520
  90.0 13.3 %serve.1 = bf16[128,104,128]{2,1,0:T(8,128)(2,1)} custom-call(bf16[32,88,768]{2,1,0:T(8,128)(2,1)} %all-to-all-done.got_hbm, bf16[2048,768]{1,0:T(8,128)(2,1)} %slab_hbm.1, bf16[32,40,768]{2,1,0:T(8,128)(2,1)} %convert_bitcast_fusion.1.keys_hbm, bf16[32,40,768]{2,1,0:T(8,128)(2,1)} %convert_bitcast_fusion.values_hbm), custom_call_target="tpu_custom_call" | custom-call | flops 8589934592 | bytes 14680064 | tf_op jit(solution)/shard_map/serve/pallas_call | solution.py:335
  103.4 0.0 copy-start.4
  103.4 0.0 copy-start.3
  103.4 0.0 copy-start.5
  103.4 9.7 %all-to-all-start.1 = ((bf16[128,104,128]{2,1,0:T(8,128)(2,1)}), bf16[128,104,128]{2,1,0:T(8,128)(2,1)}, u32[]{:S(2)}, u32[]{:S(2)}) async-start(bf16[128,104,128]{2,1,0:T(8,128)(2,1)} %serve.1), calls=%async_computation.1 | async-start | bytes 6815744 | tf_op jit(solution)/shard_map/all_to_all | solution.py:541
  113.1 0.1 collective-permute-start.3
  113.2 0.1 reshape.22
  113.3 0.1 fusion.7
  113.4 0.0 copy-start.1
  113.4 1.9 collective-permute-done.3
  115.3 1.1 fusion.6
  116.4 2.5 %maximum_select_fusion.w_out = bf16[768,768]{1,0:T(8,128)(2,1)} fusion(bf16[768,384]{1,0:T(8,128)(2,1)} %collective-permute-done.3, bf16[768,384]{1,0:T(8,128)(2,1)S(1)} %copy-done.4, bf16[384,384]{1,0:T(8,128)(2,1)S(1)} %get-tuple-element.5, bf16[384,384]{1,0:T(8,128)(2,1)S(1)} %get-tuple-element.3, bf16[384,384]{1,0:T(8,128)(2,1)S(1)} %get-tuple-element.4, ...), kind=kLoop, calls=%fused_computation.8 | loop fusion | flops 7667712 | bytes 3538945 | tf_op jit(solution)/shard_map/jit(_where)/select_n | solution.py:526
  118.9 73.0 %all-to-all-done.1.back_hbm = bf16[128,104,128]{2,1,0:T(8,128)(2,1)} async-done(((bf16[128,104,128]{2,1,0:T(8,128)(2,1)}), bf16[128,104,128]{2,1,0:T(8,128)(2,1)}, u32[]{:S(2)}, u32[]{:S(2)}) %all-to-all-start.1) | async-done | bytes 3407904 | tf_op jit(solution)/shard_map/all_to_all | solution.py:541
  191.9 6.6 %finish.1 = (f32[4,16]{1,0:T(4,128)}, bf16[4,16,16,768]{3,2,1,0:T(8,128)(2,1)}) custom-call(s32[64]{0:T(128)S(1)} %and_select_fusion.shards, s32[1]{0:T(128)} %bitcast.place, bf16[128,104,128]{2,1,0:T(8,128)(2,1)} %all-to-all-done.1.back_hbm, bf16[4,16,768]{2,1,0:T(8,128)(2,1)S(1)} %copy-done.1, bf16[768,768]{1,0:T(8,128)(2,1)} %maximum_select_fusion.w_out, ...), custom_call_target="tpu_custom_call" | custom-call | flops 1207959552 | bytes 7340032 | tf_op jit(solution)/shard_map/finish/pallas_call | solution.py:429
  (9 shorter events, 0.0 us)
Async XLA Ops:
  0.6 40.8 %copy-start = (bf16[32,40,1024]{2,1,0:T(8,128)(2,1)S(1)}, bf16[32,40,1024]{2,1,0:T(8,128)(2,1)}, u32[]{:S(2)}) copy-start(bf16[32,40,1024]{2,1,0:T(8,128)(2,1)} %param.13) | copy-start | bytes 7864324
  0.6 2.3 %collective-permute-start = (bf16[768,384]{1,0:T(8,128)(2,1)}, bf16[768,384]{1,0:T(8,128)(2,1)S(1)}, u32[]{:S(2)}, u32[]{:S(2)}) collective-permute-start(bf16[768,384]{1,0:T(8,128)(2,1)} %w_own.1), channel_id=1, source_target_pairs={{0,1},{1,0},{2,3},{3,2},{4,5},{5,4},{6,7},{7,6},{8,9},{9,8},{10,11... | collective-permute-start | bytes 1769480 | tf_op jit(solution)/shard_map/ppermute | solution.py:498
  2.9 0.7 copy-start.2
  30.1 8.8 %copy-start.6 = (bf16[1024,384]{1,0:T(8,128)(2,1)S(1)}, bf16[1024,384]{1,0:T(8,128)(2,1)}, u32[]{:S(2)}) copy-start(bf16[1024,384]{1,0:T(8,128)(2,1)} %param.16) | copy-start | bytes 2359300
  30.1 59.9 %all-to-all-start = ((bf16[32,88,768]{2,1,0:T(8,128)(2,1)}), bf16[32,88,768]{2,1,0:T(8,128)(2,1)}, u32[]{:S(2)}, u32[]{:S(2)}) async-start(bf16[32,88,768]{2,1,0:T(8,128)(2,1)} %request.1), calls=%async_computation | async-start | bytes 8650752 | tf_op jit(solution)/shard_map/all_to_all | solution.py:520
  38.9 6.1 %copy-start.7 = (bf16[1024,384]{1,0:T(8,128)(2,1)S(1)}, bf16[1024,384]{1,0:T(8,128)(2,1)}, u32[]{:S(2)}) copy-start(bf16[1024,384]{1,0:T(8,128)(2,1)} %param.17) | copy-start | bytes 2359300
  39.0 2.5 %collective-permute-start.1 = (bf16[1024,384]{1,0:T(8,128)(2,1)S(1)}, bf16[1024,384]{1,0:T(8,128)(2,1)S(1)}, u32[]{:S(2)}, u32[]{:S(2)}) collective-permute-start(bf16[1024,384]{1,0:T(8,128)(2,1)S(1)} %copy-done.6), channel_id=1, source_target_pairs={{0,1},{1,0},{2,3},{3,2},{4,5},{5,4},{6,7},{7,6},{8,9},{9,8},{10,11... | collective-permute-start | bytes 2359304 | tf_op jit(solution)/shard_map/ppermute | solution.py:522
  39.1 5.9 %collective-permute-start.2 = (bf16[1024,384]{1,0:T(8,128)(2,1)}, bf16[1024,384]{1,0:T(8,128)(2,1)S(1)}, u32[]{:S(2)}, u32[]{:S(2)}) collective-permute-start(bf16[1024,384]{1,0:T(8,128)(2,1)} %param.17), channel_id=1, source_target_pairs={{0,1},{1,0},{2,3},{3,2},{4,5},{5,4},{6,7},{7,6},{8,9},{9,8},{10,11... | collective-permute-start | bytes 2359304 | tf_op jit(solution)/shard_map/ppermute | solution.py:523
  103.4 9.7 %copy-start.4 = (bf16[768,384]{1,0:T(8,128)(2,1)S(1)}, bf16[768,384]{1,0:T(8,128)(2,1)}, u32[]{:S(2)}) copy-start(bf16[768,384]{1,0:T(8,128)(2,1)} %param.18) | copy-start | bytes 1769476
  103.4 9.8 %copy-start.3 = (s32[4,16]{1,0:T(4,128)S(1)}, s32[4,16]{1,0:T(4,128)}, u32[]{:S(2)}) copy-start(s32[4,16]{1,0:T(4,128)} %ids.1) | copy-start | bytes 772
  103.4 9.9 %copy-start.5 = (f32[768]{0:T(1024)S(1)}, f32[768]{0:T(1024)}, u32[]{:S(2)}) copy-start(f32[768]{0:T(1024)} %param.19) | copy-start | bytes 9220
  103.4 88.5 %all-to-all-start.1 = ((bf16[128,104,128]{2,1,0:T(8,128)(2,1)}), bf16[128,104,128]{2,1,0:T(8,128)(2,1)}, u32[]{:S(2)}, u32[]{:S(2)}) async-start(bf16[128,104,128]{2,1,0:T(8,128)(2,1)} %serve.1), calls=%async_computation.1 | async-start | bytes 6815744 | tf_op jit(solution)/shard_map/all_to_all | solution.py:541
  113.1 2.2 %collective-permute-start.3 = (bf16[768,384]{1,0:T(8,128)(2,1)S(1)}, bf16[768,384]{1,0:T(8,128)(2,1)}, u32[]{:S(2)}, u32[]{:S(2)}) collective-permute-start(bf16[768,384]{1,0:T(8,128)(2,1)S(1)} %copy-done.4), channel_id=1, source_target_pairs={{0,1},{1,0},{2,3},{3,2},{4,5},{5,4},{6,7},{7,6},{8,9},{9,8},{10,11... | collective-permute-start | bytes 1769480 | tf_op jit(solution)/shard_map/ppermute | solution.py:524
  113.4 78.5 %copy-start.1 = (bf16[4,16,768]{2,1,0:T(8,128)(2,1)S(1)}, bf16[4,16,768]{2,1,0:T(8,128)(2,1)}, u32[]{:S(2)}) copy-start(bf16[4,16,768]{2,1,0:T(8,128)(2,1)} %text.1) | copy-start | bytes 294916

commit v7 on v6

--- a/solution.py
+++ b/solution.py
@@ -38,9 +38,8 @@
     return pltpu.with_memory_space_constraint(array, pltpu.HBM)
 
 
-def project_kernel(ids, text, queries, w_own, w_other, out, *, slab_count):
+def pack_kernel(ids, text, queries, out, *, slab_count):
     rows = text.shape[0]
-    half = w_own.shape[1]
     count, width = queries.shape
     lane = row_of((EXTRA, LANES), 1)
     image = jnp.full((EXTRA, LANES), -1, jnp.int32)
@@ -56,29 +55,23 @@
     code = [image.astype(jnp.float32), listed.astype(jnp.float32)]
     code.append(jnp.zeros((EXTRA, width - 2 * LANES), jnp.float32))
     pieces.append(jnp.concatenate(code, axis=1))
+    out[:rows, :] = text[...]
     out[rows:, :] = jnp.concatenate(pieces, axis=0).astype(jnp.bfloat16)
-    out[:rows, :half] = jnp.dot(text[...], w_own[...], preferred_element_type=jnp.float32).astype(jnp.bfloat16)
-    out[:rows, half:] = jnp.dot(text[...], w_other[...], preferred_element_type=jnp.float32).astype(jnp.bfloat16)
-
-
-def project(ids, text, queries, w_own, w_other, slab_count):
-    width = w_own.shape[1] + w_other.shape[1]
-    operands = [text, queries, w_own, w_other]
+
+
+def pack(ids, text, queries, slab_count):
+    rows, width = text.shape
     return pl.pallas_call(
-        functools.partial(project_kernel, slab_count=slab_count),
-        grid_spec=pltpu.PrefetchScalarGridSpec(
-            num_scalar_prefetch=1,
-            grid=(1,),
-            in_specs=[pl.BlockSpec(a.shape, lambda i, *_: (0, 0)) for a in operands],
-            out_specs=pl.BlockSpec((text.shape[0] + 2 * EXTRA, width), lambda i, *_: (0, 0)),
-        ),
-        out_shape=jax.ShapeDtypeStruct((text.shape[0] + 2 * EXTRA, width), jnp.bfloat16),
+        functools.partial(pack_kernel, slab_count=slab_count),
+        grid=(1,),
+        in_specs=[pl.BlockSpec(memory_space=pltpu.SMEM)]
+        + [pl.BlockSpec(a.shape, lambda i: (0, 0)) for a in (text, queries)],
+        out_specs=pl.BlockSpec((rows + 2 * EXTRA, width), lambda i: (0, 0)),
+        out_shape=jax.ShapeDtypeStruct((rows + 2 * EXTRA, width), jnp.bfloat16),
         compiler_params=pltpu.CompilerParams(vmem_limit_bytes=VMEM_LIMIT),
-        cost_estimate=pl.CostEstimate(
-            flops=2 * text.shape[0] * text.shape[1] * width, bytes_accessed=2 << 20, transcendentals=0
-        ),
-        name="project",
-    )(ids, in_hbm(text), in_hbm(queries), in_hbm(w_own), w_other)
+        cost_estimate=pl.CostEstimate(flops=1 << 20, bytes_accessed=1 << 18, transcendentals=0),
+        name="pack",
+    )(ids, in_hbm(text), in_hbm(queries))
 
 
 def to_scalars(vectors, decoded, table, sem):
@@ -89,24 +82,38 @@
 
 
 def request_kernel(
-    place, owners, out, decoded, table, shared, sem, *, grid_y, grid_x, rows, query_count, top_count
+    place, owners, w_own, w_other, out, decoded, table, projected, shared, sem,
+    *, grid_y, grid_x, rows, query_count, top_count
 ):
     step = pl.program_id(0)
-    depth, height = owners.shape[:2]
+    depth, height, width = owners.shape
     texts = height - 2 * EXTRA
-    slot_rows = depth * rows
-    shared_rows = shared.shape[0]
+    body = projected.shape[1]
     tile_row = row_of((EXTRA, LANES), 0)
 
     @pl.when(step == 0)
     def _():
         found = [jnp.zeros((EXTRA, LANES), jnp.float32) for _ in range(2)]
         for z in range(depth):
-            code = owners[z, texts + EXTRA :, :].astype(jnp.float32)
+            code = owners[z, texts + EXTRA :, : 2 * LANES].astype(jnp.float32)
             found = [jnp.where(tile_row == z, code[:, i * LANES : (i + 1) * LANES], found[i]) for i in range(2)]
-        to_scalars(jnp.concatenate(found, axis=0).astype(jnp.int32), decoded, table, sem)
+        decoded[...] = jnp.concatenate(found, axis=0).astype(jnp.int32)
+        copy = pltpu.make_async_copy(decoded, table, sem)
+        copy.start()
+        states = owners[:, :texts, :].reshape(depth * texts, width)
+        at = 0
+        for weight in (w_own, w_other):
+            half = jnp.dot(states, weight[...], preferred_element_type=jnp.float32).astype(jnp.bfloat16)
+            for c in range(half.shape[1] // LANES):
+                for t in range(depth * query_count):
+                    projected[t, at : at + rows, :] = half[t * rows : (t + 1) * rows, c * LANES : (c + 1) * LANES]
+                at += rows
         picked = [owners[z, texts : texts + EXTRA, :].astype(jnp.float32)[:query_count] for z in range(depth)]
-        shared[...] = jnp.concatenate(picked, axis=0).astype(jnp.bfloat16)
+        picked = jnp.concatenate(picked, axis=0).astype(jnp.bfloat16)
+        for c in range(width // LANES):
+            size = depth * query_count
+            shared[c * size : (c + 1) * size, :] = picked[:, c * LANES : (c + 1) * LANES]
+        copy.wait()
 
     lane = row_of((EXTRA, LANES), 1)
     for i in range(out.shape[0]):
@@ -116,20 +123,22 @@
         code = jnp.full((EXTRA, LANES), -1.0, jnp.float32)
         for z in range(depth):
             image, listed = table[z, shard], table[EXTRA + z, shard]
-            first = lax.div(jnp.maximum(listed, 0), top_count) * rows
-            out[i, z * rows : (z + 1) * rows, :] = owners[z, pl.ds(pl.multiple_of(first, rows), rows), :]
+            query = lax.div(jnp.maximum(listed, 0), top_count)
+            out[i, z * body : (z + 1) * body, :] = projected[z * query_count + query]
             code = jnp.where(lane == z, image.astype(jnp.float32), code)
             code = jnp.where(lane == EXTRA + z, listed.astype(jnp.float32), code)
-        out[i, slot_rows : slot_rows + shared_rows, :] = shared[...]
-        out[i, slot_rows + shared_rows :, :LANES] = code.astype(jnp.bfloat16)
-
-
-def make_request(place, owners, grid_y, grid_x, rows, query_count, top_count):
+        out[i, depth * body : depth * body + shared.shape[0], :] = shared[...]
+        out[i, depth * body + shared.shape[0] :, :] = code.astype(jnp.bfloat16)
+
+
+def make_request(place, owners, w_own, w_other, grid_y, grid_x, rows, query_count, top_count):
     depth, height, width = owners.shape
-    shared_rows = depth * query_count
-    total = depth * rows + shared_rows + EXTRA
+    body = width // LANES * rows
+    shared_rows = depth * query_count * (width // LANES)
+    total = depth * body + shared_rows + EXTRA
     targets = PAIR * grid_y * grid_x
     block = min(8, targets)
+    whole = lambda a: pl.BlockSpec(a.shape, lambda i, *_: (0,) * a.ndim)
     return pl.pallas_call(
         functools.partial(
             request_kernel,
@@ -142,20 +151,21 @@
         grid_spec=pltpu.PrefetchScalarGridSpec(
             num_scalar_prefetch=1,
             grid=(targets // block,),
-            in_specs=[pl.BlockSpec(owners.shape, lambda i, *_: (0, 0, 0))],
-            out_specs=pl.BlockSpec((block, total, width), lambda i, *_: (i, 0, 0)),
+            in_specs=[whole(owners), whole(w_own), whole(w_other)],
+            out_specs=pl.BlockSpec((block, total, LANES), lambda i, *_: (i, 0, 0)),
             scratch_shapes=[
                 pltpu.VMEM((2 * EXTRA, LANES), jnp.int32),
                 pltpu.SMEM((2 * EXTRA, LANES), jnp.int32),
-                pltpu.VMEM((shared_rows, width), jnp.bfloat16),
+                pltpu.VMEM((depth * query_count, body, LANES), jnp.bfloat16),
+                pltpu.VMEM((shared_rows, LANES), jnp.bfloat16),
                 pltpu.SemaphoreType.DMA,
             ],
         ),
-        out_shape=pltpu.HBM((targets, total, width), jnp.bfloat16),
+        out_shape=pltpu.HBM((targets, total, LANES), jnp.bfloat16),
         compiler_params=pltpu.CompilerParams(vmem_limit_bytes=VMEM_LIMIT),
-        cost_estimate=pl.CostEstimate(flops=1 << 20, bytes_accessed=6 << 20, transcendentals=0),
+        cost_estimate=pl.CostEstimate(flops=1 << 29, bytes_accessed=6 << 20, transcendentals=0),
         name="request",
-    )(place, in_hbm(owners))
+    )(place, in_hbm(owners), in_hbm(w_own), in_hbm(w_other))
 
 
 def index_stats(query, slab, picked, logits):
@@ -194,7 +204,8 @@
     sources = got.shape[0]
     slots = sources * depth
     columns = keys.shape[2]
-    slot_rows = depth * rows
+    body = columns // LANES * rows
+    slot_rows = depth * body
     late = got.shape[1] - slot_rows
     copies = [
         pltpu.make_async_copy(source, target, sems.at[i])
@@ -210,8 +221,8 @@
     ]
     for copy in copies:
         copy.start()
-    shared_rows = depth * query_count
-    body = columns // LANES * rows
+    size = depth * query_count
+    shared_rows = size * (columns // LANES)
     per_chunk = LANES // query_count
     lane = row_of((EXTRA, LANES), 1)
     tile_row = row_of((EXTRA, LANES), 0)
@@ -237,7 +248,19 @@
     for g in range(UNROLL):
         listed[count + g] = last
 
-    queries = jnp.concatenate([got[source, slot_rows : slot_rows + shared_rows, :] for source in range(sources)], axis=0)
+    queries = jnp.concatenate(
+        [
+            jnp.concatenate(
+                [
+                    got[source, slot_rows + c * size : slot_rows + (c + 1) * size, :]
+                    for c in range(columns // LANES)
+                ],
+                axis=1,
+            )
+            for source in range(sources)
+        ],
+        axis=0,
+    )
     missing = len(chunks) * LANES - queries.shape[0]
     if missing:
         queries = jnp.concatenate([queries, jnp.zeros((missing, queries.shape[1]), queries.dtype)], axis=0)
@@ -282,7 +305,11 @@
         scores = []
         for g, (at, width, masks) in work:
             source, z = places[g]
-            query = got[source, pl.ds(pl.multiple_of(z * rows, rows), rows), at : at + width]
+            pieces = [
+                got[source, pl.ds(pl.multiple_of(z * body + c * rows, rows), rows), :]
+                for c in range(at // LANES, (at + width) // LANES)
+            ]
+            query = pieces[0] if len(pieces) == 1 else jnp.concatenate(pieces, axis=1)
             spread = jnp.concatenate([query * mask.astype(query.dtype) for mask in masks], axis=0)
             scores.append(
                 lax.dot_general(
@@ -363,103 +390,118 @@
 
 
 def finish_kernel(
-    shards, place, back_hbm, text, w_out, gain, found, out,
-    exact, normalizers, gathered, back, sent, sems, *, top_count, query_count, shift
+    shards, place, back_hbm, text_hbm, w_out_hbm, gain_hbm, found, out_hbm,
+    exact, gathered, back, sent, text, w_out, gain, out, sems, *, top_count, query_count, chunks, shift
 ):
-    step = pl.program_id(0)
-    rows = text.shape[1]
+    rows, width = text.shape[1:]
     body = back.shape[1]
-
-    def fetch(entry, query):
-        return pltpu.make_async_copy(back_hbm.at[shards[entry], pl.ds(0, body), :], back.at[entry], sems.at[query])
-
-    @pl.when(step == 0)
-    def _():
-        stats = pltpu.make_async_copy(back_hbm.at[:, pl.ds(body, EXTRA), :], sent, sems.at[query_count])
-        stats.start()
-        for query in range(query_count):
-            for k in range(top_count):
-                fetch(query * top_count + k, query // text.shape[0]).start()
-        stats.wait()
-        parts = sent[...].astype(jnp.float32)
-        joined = jnp.sum(jnp.where(row_of(parts.shape, 1) < 3, parts, 0.0), axis=1)
-        joined = pltpu.roll(joined, lax.rem(LANES - place[0] * query_count, LANES), 1)
-        exact[...] = joined
-        peak = jnp.max(joined, axis=0, keepdims=True)
-        scaled = jnp.exp(joined - peak) * pltpu.roll(joined, LANES - query_count, 1)
-        total = jnp.sum(scaled, axis=0, keepdims=True)
-        total = jnp.where(row_of(total.shape, 1) < query_count, total, 1.0)
-        normalizers[...] = jnp.broadcast_to(peak + jnp.log(total), normalizers.shape)
-
-    per_step = text.shape[0]
-    for i in range(per_step):
-        query = step * per_step + i
-        picked = jnp.concatenate(
-            [exact[pl.ds(shards[query * top_count + k], 1), :] for k in range(top_count)], axis=0
+    entries = query_count * top_count // chunks
+    queries = query_count // chunks
+
+    def fetch(entry, chunk):
+        return pltpu.make_async_copy(back_hbm.at[shards[entry], pl.ds(0, body), :], back.at[entry], sems.at[chunk])
+
+    loads = [
+        pltpu.make_async_copy(source, target, sems.at[chunks + i])
+        for i, (source, target) in enumerate(
+            [
+                (back_hbm.at[:, pl.ds(body, EXTRA), :], sent),
+                (w_out_hbm, w_out),
+                (text_hbm, text),
+                (gain_hbm, gain),
+            ]
         )
+    ]
+    for load in loads:
+        load.start()
+    for chunk in range(chunks):
+        for entry in range(chunk * entries, (chunk + 1) * entries):
+            fetch(entry, chunk).start()
+
+    loads[0].wait()
+    parts = sent[...].astype(jnp.float32)
+    joined = jnp.sum(jnp.where(row_of(parts.shape, 1) < 3, parts, 0.0), axis=1)
+    joined = pltpu.roll(joined, lax.rem(LANES - place[0] * query_count, LANES), 1)
+    exact[...] = joined
+    peak = jnp.max(joined, axis=0, keepdims=True)
+    scaled = jnp.exp(joined - peak) * pltpu.roll(joined, LANES - query_count, 1)
+    total = jnp.sum(scaled, axis=0, keepdims=True)
+    total = jnp.where(row_of(total.shape, 1) < query_count, total, 1.0)
+    normalizers = peak + jnp.log(total)
+    for query in range(query_count):
+        picked = jnp.concatenate([exact[pl.ds(shards[query * top_count + k], 1), :] for k in range(top_count)], axis=0)
         lane = row_of(picked.shape, 1)
         candidate = jnp.sum(jnp.where(lane == 2 * query_count + query, picked, 0.0), axis=1, keepdims=True)
-        normalizer = jnp.sum(jnp.where(lane[:1] == query, normalizers[:1, :], 0.0), axis=1, keepdims=True)
-        result = candidate - normalizer + shift
+        result = candidate - normalizers[:, query : query + 1] + shift
         result = jnp.sum(jnp.where(lane == row_of(picked.shape, 0), result, 0.0), axis=0, keepdims=True)
-        found[pl.ds(query, 1), :] = result[:, :top_count]
-
-    entries = per_step * top_count
-    for k in range(entries):
-        fetch(step * entries + k, step).wait()
-    for k in range(entries):
-        for j in range(body // rows):
-            gathered[k * rows : (k + 1) * rows, j * LANES : (j + 1) * LANES] = back[
-                step * entries + k, j * rows : (j + 1) * rows, :
-            ]
-    mixed = jnp.dot(gathered[...], w_out[...], preferred_element_type=jnp.float32)
-    width = mixed.shape[1]
-    summed = mixed.reshape(per_step, top_count, rows, width) + text[...].astype(jnp.float32).reshape(per_step, 1, rows, width)
-    mean = jnp.mean(summed, axis=-1, keepdims=True)
-    centred = summed - mean
-    variance = jnp.mean(centred * centred, axis=-1, keepdims=True)
-    normed = centred * lax.rsqrt(variance + EPSILON) * gain[...].reshape(1, 1, 1, width)
-    out[...] = normed.astype(jnp.bfloat16)
+        found[query : query + 1, :] = result[:, :top_count]
+
+    for load in loads[1:]:
+        load.wait()
+    stores = []
+    for chunk in range(chunks):
+        first = chunk * queries
+        for entry in range(chunk * entries, (chunk + 1) * entries):
+            fetch(entry, chunk).wait()
+        for k in range(entries):
+            for j in range(body // rows):
+                gathered[chunk, k * rows : (k + 1) * rows, j * LANES : (j + 1) * LANES] = back[
+                    chunk * entries + k, j * rows : (j + 1) * rows, :
+                ]
+        mixed = jnp.dot(gathered[chunk], w_out[...], preferred_element_type=jnp.float32)
+        states = text[first : first + queries].astype(jnp.float32).reshape(queries, 1, rows, width)
+        summed = mixed.reshape(queries, top_count, rows, width) + states
+        mean = jnp.mean(summed, axis=-1, keepdims=True)
+        centred = summed - mean
+        variance = jnp.mean(centred * centred, axis=-1, keepdims=True)
+        normed = centred * lax.rsqrt(variance + EPSILON) * gain[...].reshape(1, 1, 1, width)
+        out[first : first + queries] = normed.astype(jnp.bfloat16)
+        store = pltpu.make_async_copy(
+            out.at[pl.ds(first, queries)], out_hbm.at[pl.ds(first, queries)], sems.at[chunks + 4 + chunk]
+        )
+        store.start()
+        stores.append(store)
+    for store in stores:
+        store.wait()
 
 
 def finish(shards, place, back, text, w_out, gain, top_count, shift):
     query_count, rows, width = text.shape
-    per_step = 2
-    full = lambda a: pl.BlockSpec(a.shape, lambda i, *_: (0,) * a.ndim)
+    chunks = 2
+    body = back.shape[1] - EXTRA
+    entries = query_count * top_count
     return pl.pallas_call(
-        functools.partial(finish_kernel, top_count=top_count, query_count=query_count, shift=shift),
+        functools.partial(finish_kernel, top_count=top_count, query_count=query_count, chunks=chunks, shift=shift),
         grid_spec=pltpu.PrefetchScalarGridSpec(
             num_scalar_prefetch=2,
-            grid=(query_count // per_step,),
-            in_specs=[
-                pl.BlockSpec(memory_space=pltpu.HBM),
-                pl.BlockSpec((per_step, rows, width), lambda i, *_: (i, 0, 0)),
-                full(w_out),
-                full(gain),
-            ],
+            grid=(1,),
+            in_specs=[pl.BlockSpec(memory_space=pltpu.HBM)] * 4,
             out_specs=[
                 pl.BlockSpec((query_count, top_count), lambda i, *_: (0, 0)),
-                pl.BlockSpec((per_step, top_count, rows, width), lambda i, *_: (i, 0, 0, 0)),
+                pl.BlockSpec(memory_space=pltpu.HBM),
             ],
             scratch_shapes=[
                 pltpu.VMEM((back.shape[0], LANES), jnp.float32),
-                pltpu.VMEM((EXTRA, LANES), jnp.float32),
-                pltpu.VMEM((per_step * top_count * rows, width), jnp.bfloat16),
-                pltpu.VMEM((query_count * top_count, back.shape[1] - EXTRA, LANES), jnp.bfloat16),
+                pltpu.VMEM((chunks, entries // chunks * rows, width), jnp.bfloat16),
+                pltpu.VMEM((entries, body, LANES), jnp.bfloat16),
                 pltpu.VMEM((back.shape[0], EXTRA, LANES), jnp.bfloat16),
-                pltpu.SemaphoreType.DMA((query_count + 1,)),
+                pltpu.VMEM(text.shape, text.dtype),
+                pltpu.VMEM(w_out.shape, w_out.dtype),
+                pltpu.VMEM(gain.shape, gain.dtype),
+                pltpu.VMEM((query_count, top_count, rows, width), jnp.bfloat16),
+                pltpu.SemaphoreType.DMA((2 * chunks + 4,)),
             ],
         ),
         out_shape=[
             jax.ShapeDtypeStruct((query_count, top_count), jnp.float32),
-            jax.ShapeDtypeStruct((query_count, top_count, rows, width), jnp.bfloat16),
+            pltpu.HBM((query_count, top_count, rows, width), jnp.bfloat16),
         ],
         compiler_params=pltpu.CompilerParams(vmem_limit_bytes=VMEM_LIMIT),
         cost_estimate=pl.CostEstimate(
-            flops=2 * query_count * top_count * rows * width * width, bytes_accessed=7 << 20, transcendentals=0
+            flops=2 * entries * rows * width * width, bytes_accessed=7 << 20, transcendentals=0
         ),
         name="finish",
-    )(shards, place, in_hbm(back), text, in_hbm(w_out), gain)
+    )(shards, place, in_hbm(back), in_hbm(text), in_hbm(w_out), in_hbm(gain))
 
 
 def project_rows(rows_in, weight):
@@ -496,21 +538,15 @@
     ]
     swap = [(0, 1), (1, 0)]
     w_query_other = lax.ppermute(w_query, "rep", swap)
-
     own_list = cand_ids.reshape(list_length)
     own_anchor = own_list // slab_count
-    sent = project(
-        cand_ids,
-        text_states.reshape(query_count * text_count, model_width),
-        queries,
-        w_query,
-        w_query_other,
-        slab_count,
-    )
+    sent = pack(cand_ids, text_states.reshape(query_count * text_count, model_width), queries, slab_count)
     owners = lax.all_gather(sent, "shard", axis=0, tiled=True, axis_index_groups=columns)
     request = make_request(
         (here_z // PAIR * PAIR).reshape(1),
         owners.reshape(owned, sent.shape[0], model_width),
+        w_query,
+        w_query_other,
         grid_y,
         grid_x,
         text_count,

time: 200 us -> 194 us (0.970)
  waiting for transfers between devices: 120 us -> 114 us
  Pallas kernels: 26.6 us -> 24.5 us
    all_to_all x1, waiting for transfers between devices: 41.5 us -> 37.2 us  [on_device(): lax.all_to_all(request, 'shard', split_axis=0, concat_axis=0, tiled=True,...]
    ppermute x1, waiting for transfers between devices: 2.15 us -> 0.01 us  [on_device(): w_query_other = lax.ppermute(w_query, 'rep', swap)]
  transfers between devices with their start and end apart: 6 -> 6, of which waited for: 5 -> 4; matrix products, arithmetic and copies ran while one was open for 5% -> 6% of each run, Pallas kernels for 0% -> 1%
where the time goes in v7:
time: 194 us
  waiting for transfers between devices  114 us (59%)
  Pallas kernels  24.5 us (13%)
  starting transfers between devices  21 us (11%)
  blocking collectives  20 us (10%)
  matrix products  7.03 us (4%)
  local copies, waits for them, and re-layouts  3.53 us (2%)
  other arithmetic  2.51 us (1%)
    all_to_all x1, waiting for transfers between devices, on_device(): lax.all_to_all(context, 'shard', split_axis=0, concat_axis=0, tiled=True)  74 us
    all_to_all x1, waiting for transfers between devices, on_device(): lax.all_to_all(request, 'shard', split_axis=0, concat_axis=0, tiled=True,...  37.2 us
    all_gather x1, blocking collectives, on_device(): lax.all_gather(sent, 'shard', axis=0, tiled=True, axis_index_groups=columns)  20 us
    pallas_call x1, Pallas kernels, serve(): pl.pallas_call(functools.partial(serve_kernel, grid_y=grid_y, grid_x=grid...  11.8 us
    all_to_all x1, starting transfers between devices, on_device(): lax.all_to_all(context, 'shard', split_axis=0, concat_axis=0, tiled=True)  11.5 us
    all_to_all x1, starting transfers between devices, on_device(): lax.all_to_all(request, 'shard', split_axis=0, concat_axis=0, tiled=True,...  8.74 us
    dot_general x2, matrix products, project_rows(): jnp.einsum('spc,cd->spd', rows_in, weight, preferred_element_type=jnp.flo...  7.03 us
    pallas_call x1, Pallas kernels, finish(): pl.pallas_call(functools.partial(finish_kernel, top_count=top_count, quer...  6.33 us
  transfers between devices with their start and end apart: 6, of which 4 were waited for; matrix products, arithmetic and copies ran while one was open for 6% of the time, Pallas kernels for 1%

profile of v7, /device:TPU:32, one launch (start us, length us, event | category | flops | bytes accessed | tf_op | source)
XLA Modules:
  0.0 194.1 jit_solution(3496439725036211509)
XLA Ops:
  0.6 0.0 copy-start
  0.6 0.1 collective-permute-start
  0.8 0.0 copy-start.1
  0.8 0.8 copy-done.1
  1.6 1.1 pack.1
  2.8 20.0 %all_gather.3 = bf16[320,768]{1,0:T(8,128)(2,1)} all-gather(bf16[80,768]{1,0:T(8,128)(2,1)S(1)} %pack.1), channel_id=1, replica_groups={{0,16,32,48},{8,24,40,56},{2,18,34,50},{10,26,42,58},{4,20,36,52},{12,2..., dimensions={0}, use_global_device_ids=true | all-gather | bytes 614400 | tf_op jit(solution)/shard_map/all_gather | solution.py:544
  22.8 0.0 collective-permute-done.w_other
  22.8 0.8 copy-done.4
  23.6 5.2 %request.1 = bf16[32,488,128]{2,1,0:T(8,128)(2,1)} custom-call(s32[1]{0:T(128)} %bitcast.1.place, bf16[4,80,768]{2,1,0:T(8,128)(2,1)} %bitcast.16, bf16[768,384]{1,0:T(8,128)(2,1)} %w_own.1, bf16[768,384]{1,0:T(8,128)(2,1)} %copy-done.4), custom_call_target="tpu_custom_call" | custom-call | flops 536870912 | bytes 6291456 | tf_op jit(solution)/shard_map/request/pallas_call | solution.py:142
  28.8 0.0 copy-start.6
  28.8 8.7 %all-to-all-start = ((bf16[32,488,128]{2,1,0:T(8,128)(2,1)}), bf16[32,488,128]{2,1,0:T(8,128)(2,1)}, u32[]{:S(2)}, u32[]{:S(2)}) async-start(bf16[32,488,128]{2,1,0:T(8,128)(2,1)} %request.1), calls=%async_computation | async-start | bytes 7995392 | tf_op jit(solution)/shard_map/all_to_all | solution.py:556
  37.6 0.0 copy-start.7
  37.6 0.1 collective-permute-start.1
  37.7 0.5 collective-permute-start.2
  38.2 1.9 collective-permute-done.1
  40.1 3.6 %convert_bitcast_fusion.1.keys_hbm = bf16[32,40,768]{2,1,0:T(8,128)(2,1)} fusion(bf16[32,40,1024]{2,1,0:T(8,128)(2,1)S(1)} %copy-done, bf16[1024,384]{1,0:T(8,128)(2,1)S(1)} %collective-permute-done.1, bf16[1024,384]{1,0:T(8,128)(2,1)S(1)} %copy-done.6), kind=kOutput, calls=%fused_computation.1 | convolution fusion | flops 2017394688 | bytes 6160384 | tf_op jit(solution)/shard_map/spc,cd->spd/dot_general | solution.py:508
  43.6 3.5 %convert_bitcast_fusion.values_hbm = bf16[32,40,768]{2,1,0:T(8,128)(2,1)} fusion(bf16[32,40,1024]{2,1,0:T(8,128)(2,1)S(1)} %copy-done, bf16[1024,384]{1,0:T(8,128)(2,1)S(1)} %collective-permute-done.2, bf16[1024,384]{1,0:T(8,128)(2,1)S(1)} %copy-done.7), kind=kOutput, calls=%fused_computation | convolution fusion | flops 2017394688 | bytes 6160384 | tf_op jit(solution)/shard_map/spc,cd->spd/dot_general | solution.py:508
  47.1 37.2 %all-to-all-done.got_hbm = bf16[32,488,128]{2,1,0:T(8,128)(2,1)} async-done(((bf16[32,488,128]{2,1,0:T(8,128)(2,1)}), bf16[32,488,128]{2,1,0:T(8,128)(2,1)}, u32[]{:S(2)}, u32[]{:S(2)}) %all-to-all-start) | async-done | bytes 3997728 | tf_op jit(solution)/shard_map/all_to_all | solution.py:556
  84.4 11.8 %serve.1 = bf16[128,104,128]{2,1,0:T(8,128)(2,1)} custom-call(bf16[32,488,128]{2,1,0:T(8,128)(2,1)} %all-to-all-done.got_hbm, bf16[2048,768]{1,0:T(8,128)(2,1)} %slab_hbm.1, bf16[32,40,768]{2,1,0:T(8,128)(2,1)} %convert_bitcast_fusion.1.keys_hbm, bf16[32,40,768]{2,1,0:T(8,128)(2,1)} %convert_bitcast_fusion.values_hbm), custom_call_target="tpu_custom_call" | custom-call | flops 8589934592 | bytes 14680064 | tf_op jit(solution)/shard_map/serve/pallas_call | solution.py:362
  96.2 0.0 copy-start.3
  96.2 0.0 copy-start.2
  96.2 0.0 copy-start.5
  96.2 11.5 %all-to-all-start.1 = ((bf16[128,104,128]{2,1,0:T(8,128)(2,1)}), bf16[128,104,128]{2,1,0:T(8,128)(2,1)}, u32[]{:S(2)}, u32[]{:S(2)}) async-start(bf16[128,104,128]{2,1,0:T(8,128)(2,1)} %serve.1), calls=%async_computation.1 | async-start | bytes 6815744 | tf_op jit(solution)/shard_map/all_to_all | solution.py:577
  107.8 0.1 collective-permute-start.3
  107.9 0.1 reshape.22
  108.0 0.6 reshape.27.gain_hbm
  108.6 0.1 fusion.7
  108.6 1.4 collective-permute-done.3
  110.0 1.1 fusion.6
  111.1 2.5 %maximum_select_fusion.w_out_hbm = bf16[768,768]{1,0:T(8,128)(2,1)} fusion(bf16[768,384]{1,0:T(8,128)(2,1)} %collective-permute-done.3, bf16[768,384]{1,0:T(8,128)(2,1)S(1)} %copy-done.3, bf16[384,384]{1,0:T(8,128)(2,1)S(1)} %get-tuple-element.5, bf16[384,384]{1,0:T(8,128)(2,1)S(1)} %get-tuple-element.3, bf16[384,384]{1,0:T(8,128)(2,1)S(1)} %get-tuple-element.4, ...), kind=kLoop, calls=%fused_computation.8 | loop fusion | flops 7667712 | bytes 3538945 | tf_op jit(solution)/shard_map/jit(_where)/select_n | solution.py:562
  113.6 74.0 %all-to-all-done.1.back_hbm = bf16[128,104,128]{2,1,0:T(8,128)(2,1)} async-done(((bf16[128,104,128]{2,1,0:T(8,128)(2,1)}), bf16[128,104,128]{2,1,0:T(8,128)(2,1)}, u32[]{:S(2)}, u32[]{:S(2)}) %all-to-all-start.1) | async-done | bytes 3407904 | tf_op jit(solution)/shard_map/all_to_all | solution.py:577
  187.6 6.3 %finish.1 = (f32[4,16]{1,0:T(4,128)}, bf16[4,16,16,768]{3,2,1,0:T(8,128)(2,1)}) custom-call(s32[64]{0:T(128)S(1)} %and_select_fusion.shards, s32[1]{0:T(128)} %bitcast.place, bf16[128,104,128]{2,1,0:T(8,128)(2,1)} %all-to-all-done.1.back_hbm, bf16[4,16,768]{2,1,0:T(8,128)(2,1)} %text_hbm.1, bf16[768,768]{1,0:T(8,128)(2,1)} %maximum_select_fusion.w_out_hbm, ...), custom_call_target="tpu_custom_call" | custom-call | flops 1207959552 | bytes 7340032 | tf_op jit(solution)/shard_map/finish/pallas_call | solution.py:473
  (9 shorter events, 0.0 us)
Async XLA Ops:
  0.6 39.5 %copy-start = (bf16[32,40,1024]{2,1,0:T(8,128)(2,1)S(1)}, bf16[32,40,1024]{2,1,0:T(8,128)(2,1)}, u32[]{:S(2)}) copy-start(bf16[32,40,1024]{2,1,0:T(8,128)(2,1)} %param.13) | copy-start | bytes 7864324
  0.6 22.1 %collective-permute-start = (bf16[768,384]{1,0:T(8,128)(2,1)}, bf16[768,384]{1,0:T(8,128)(2,1)S(1)}, u32[]{:S(2)}, u32[]{:S(2)}) collective-permute-start(bf16[768,384]{1,0:T(8,128)(2,1)} %w_own.1), channel_id=1, source_target_pairs={{0,1},{1,0},{2,3},{3,2},{4,5},{5,4},{6,7},{7,6},{8,9},{9,8},{10,11... | collective-permute-start | bytes 1769480 | tf_op jit(solution)/shard_map/ppermute | solution.py:540
  0.8 0.8 copy-start.1
  22.8 0.8 copy-start.4
  28.8 8.8 %copy-start.6 = (bf16[1024,384]{1,0:T(8,128)(2,1)S(1)}, bf16[1024,384]{1,0:T(8,128)(2,1)}, u32[]{:S(2)}) copy-start(bf16[1024,384]{1,0:T(8,128)(2,1)} %param.16) | copy-start | bytes 2359300
  28.8 55.5 %all-to-all-start = ((bf16[32,488,128]{2,1,0:T(8,128)(2,1)}), bf16[32,488,128]{2,1,0:T(8,128)(2,1)}, u32[]{:S(2)}, u32[]{:S(2)}) async-start(bf16[32,488,128]{2,1,0:T(8,128)(2,1)} %request.1), calls=%async_computation | async-start | bytes 7995392 | tf_op jit(solution)/shard_map/all_to_all | solution.py:556
  37.6 6.1 %copy-start.7 = (bf16[1024,384]{1,0:T(8,128)(2,1)S(1)}, bf16[1024,384]{1,0:T(8,128)(2,1)}, u32[]{:S(2)}) copy-start(bf16[1024,384]{1,0:T(8,128)(2,1)} %param.17) | copy-start | bytes 2359300
  37.6 2.5 %collective-permute-start.1 = (bf16[1024,384]{1,0:T(8,128)(2,1)S(1)}, bf16[1024,384]{1,0:T(8,128)(2,1)S(1)}, u32[]{:S(2)}, u32[]{:S(2)}) collective-permute-start(bf16[1024,384]{1,0:T(8,128)(2,1)S(1)} %copy-done.6), channel_id=1, source_target_pairs={{0,1},{1,0},{2,3},{3,2},{4,5},{5,4},{6,7},{7,6},{8,9},{9,8},{10,11... | collective-permute-start | bytes 2359304 | tf_op jit(solution)/shard_map/ppermute | solution.py:558
  37.7 6.0 %collective-permute-start.2 = (bf16[1024,384]{1,0:T(8,128)(2,1)}, bf16[1024,384]{1,0:T(8,128)(2,1)S(1)}, u32[]{:S(2)}, u32[]{:S(2)}) collective-permute-start(bf16[1024,384]{1,0:T(8,128)(2,1)} %param.17), channel_id=1, source_target_pairs={{0,1},{1,0},{2,3},{3,2},{4,5},{5,4},{6,7},{7,6},{8,9},{9,8},{10,11... | collective-permute-start | bytes 2359304 | tf_op jit(solution)/shard_map/ppermute | solution.py:559
  96.2 11.6 %copy-start.3 = (bf16[768,384]{1,0:T(8,128)(2,1)S(1)}, bf16[768,384]{1,0:T(8,128)(2,1)}, u32[]{:S(2)}) copy-start(bf16[768,384]{1,0:T(8,128)(2,1)} %param.18) | copy-start | bytes 1769476
  96.2 11.7 %copy-start.2 = (s32[4,16]{1,0:T(4,128)S(1)}, s32[4,16]{1,0:T(4,128)}, u32[]{:S(2)}) copy-start(s32[4,16]{1,0:T(4,128)} %ids.1) | copy-start | bytes 772
  96.2 11.7 %copy-start.5 = (f32[768]{0:T(1024)S(1)}, f32[768]{0:T(1024)}, u32[]{:S(2)}) copy-start(f32[768]{0:T(1024)} %param.19) | copy-start | bytes 9220
  96.2 91.4 %all-to-all-start.1 = ((bf16[128,104,128]{2,1,0:T(8,128)(2,1)}), bf16[128,104,128]{2,1,0:T(8,128)(2,1)}, u32[]{:S(2)}, u32[]{:S(2)}) async-start(bf16[128,104,128]{2,1,0:T(8,128)(2,1)} %serve.1), calls=%async_computation.1 | async-start | bytes 6815744 | tf_op jit(solution)/shard_map/all_to_all | solution.py:577
  107.8 2.2 %collective-permute-start.3 = (bf16[768,384]{1,0:T(8,128)(2,1)S(1)}, bf16[768,384]{1,0:T(8,128)(2,1)}, u32[]{:S(2)}, u32[]{:S(2)}) collective-permute-start(bf16[768,384]{1,0:T(8,128)(2,1)S(1)} %copy-done.3), channel_id=1, source_target_pairs={{0,1},{1,0},{2,3},{3,2},{4,5},{5,4},{6,7},{7,6},{8,9},{9,8},{10,11... | collective-permute-start | bytes 1769480 | tf_op jit(solution)/shard_map/ppermute | solution.py:560

commit v8 on v7

--- a/solution.py
+++ b/solution.py
@@ -38,40 +38,52 @@
     return pltpu.with_memory_space_constraint(array, pltpu.HBM)
 
 
-def pack_kernel(ids, text, queries, out, *, slab_count):
-    rows = text.shape[0]
+def pack_kernel(ids_hbm, text_hbm, queries_hbm, out, ids, queries, sems, *, slab_count):
+    rows = text_hbm.shape[0]
+    copies = [
+        pltpu.make_async_copy(ids_hbm, ids, sems.at[0]),
+        pltpu.make_async_copy(queries_hbm, queries, sems.at[1]),
+        pltpu.make_async_copy(text_hbm, out.at[pl.ds(0, rows), :], sems.at[2]),
+    ]
+    for copy in copies:
+        copy.start()
     count, width = queries.shape
     lane = row_of((EXTRA, LANES), 1)
     image = jnp.full((EXTRA, LANES), -1, jnp.int32)
     listed = image
+    copies[0].wait()
     for entry in range(ids.shape[0] * ids.shape[1]):
         row = ids[entry // ids.shape[1], entry % ids.shape[1]]
         here = lane == lax.div(row, slab_count)
         image = jnp.where(here, lax.rem(row, slab_count), image)
         listed = jnp.where(here, entry, listed)
+    copies[1].wait()
     pieces = [queries[...].astype(jnp.float32)]
     if count < EXTRA:
         pieces.append(jnp.zeros((EXTRA - count, width), jnp.float32))
     code = [image.astype(jnp.float32), listed.astype(jnp.float32)]
     code.append(jnp.zeros((EXTRA, width - 2 * LANES), jnp.float32))
     pieces.append(jnp.concatenate(code, axis=1))
-    out[:rows, :] = text[...]
     out[rows:, :] = jnp.concatenate(pieces, axis=0).astype(jnp.bfloat16)
+    copies[2].wait()
 
 
 def pack(ids, text, queries, slab_count):
     rows, width = text.shape
     return pl.pallas_call(
         functools.partial(pack_kernel, slab_count=slab_count),
-        grid=(1,),
-        in_specs=[pl.BlockSpec(memory_space=pltpu.SMEM)]
-        + [pl.BlockSpec(a.shape, lambda i: (0, 0)) for a in (text, queries)],
-        out_specs=pl.BlockSpec((rows + 2 * EXTRA, width), lambda i: (0, 0)),
+        in_specs=[pl.BlockSpec(memory_space=pltpu.HBM)] * 3,
+        out_specs=pl.BlockSpec(memory_space=pltpu.VMEM),
+        scratch_shapes=[
+            pltpu.SMEM(ids.shape, ids.dtype),
+            pltpu.VMEM(queries.shape, queries.dtype),
+            pltpu.SemaphoreType.DMA((3,)),
+        ],
         out_shape=jax.ShapeDtypeStruct((rows + 2 * EXTRA, width), jnp.bfloat16),
         compiler_params=pltpu.CompilerParams(vmem_limit_bytes=VMEM_LIMIT),
         cost_estimate=pl.CostEstimate(flops=1 << 20, bytes_accessed=1 << 18, transcendentals=0),
         name="pack",
-    )(ids, in_hbm(text), in_hbm(queries))
+    )(in_hbm(ids), in_hbm(text), in_hbm(queries))
 
 
 def to_scalars(vectors, decoded, table, sem):
@@ -82,34 +94,44 @@
 
 
 def request_kernel(
-    place, owners, w_own, w_other, out, decoded, table, projected, shared, sem,
-    *, grid_y, grid_x, rows, query_count, top_count
+    place, w_own, w_other, *rest, depth, grid_y, grid_x, rows, query_count, top_count
 ):
+    owners = rest[:depth]
+    out, decoded, table, projected, shared, sem = rest[depth:]
     step = pl.program_id(0)
-    depth, height, width = owners.shape
+    height, width = owners[0].shape
     texts = height - 2 * EXTRA
     body = projected.shape[1]
     tile_row = row_of((EXTRA, LANES), 0)
 
     @pl.when(step == 0)
     def _():
+        places = [lax.rem(place[1] + depth - o, depth) for o in range(depth)]
         found = [jnp.zeros((EXTRA, LANES), jnp.float32) for _ in range(2)]
-        for z in range(depth):
-            code = owners[z, texts + EXTRA :, : 2 * LANES].astype(jnp.float32)
-            found = [jnp.where(tile_row == z, code[:, i * LANES : (i + 1) * LANES], found[i]) for i in range(2)]
+        for o in range(depth):
+            code = owners[o][texts + EXTRA :, : 2 * LANES].astype(jnp.float32)
+            found = [jnp.where(tile_row == places[o], code[:, i * LANES : (i + 1) * LANES], found[i]) for i in range(2)]
         decoded[...] = jnp.concatenate(found, axis=0).astype(jnp.int32)
         copy = pltpu.make_async_copy(decoded, table, sem)
         copy.start()
-        states = owners[:, :texts, :].reshape(depth * texts, width)
+        states = jnp.concatenate([owner[:texts, :] for owner in owners], axis=0)
         at = 0
         for weight in (w_own, w_other):
             half = jnp.dot(states, weight[...], preferred_element_type=jnp.float32).astype(jnp.bfloat16)
             for c in range(half.shape[1] // LANES):
-                for t in range(depth * query_count):
-                    projected[t, at : at + rows, :] = half[t * rows : (t + 1) * rows, c * LANES : (c + 1) * LANES]
+                for o in range(depth):
+                    for q in range(query_count):
+                        t = o * query_count + q
+                        projected[places[o] * query_count + q, at : at + rows, :] = half[
+                            t * rows : (t + 1) * rows, c * LANES : (c + 1) * LANES
+                        ]
                 at += rows
-        picked = [owners[z, texts : texts + EXTRA, :].astype(jnp.float32)[:query_count] for z in range(depth)]
-        picked = jnp.concatenate(picked, axis=0).astype(jnp.bfloat16)
+        picked = jnp.zeros((depth * query_count, width), jnp.float32)
+        for o in range(depth):
+            part = owners[o][texts : texts + EXTRA, :].astype(jnp.float32)[:query_count]
+            spread = jnp.concatenate([part] * depth, axis=0)
+            picked = jnp.where(row_of(picked.shape, 0) // query_count == places[o], spread, picked)
+        picked = picked.astype(jnp.bfloat16)
         for c in range(width // LANES):
             size = depth * query_count
             shared[c * size : (c + 1) * size, :] = picked[:, c * LANES : (c + 1) * LANES]
@@ -132,7 +154,8 @@
 
 
 def make_request(place, owners, w_own, w_other, grid_y, grid_x, rows, query_count, top_count):
-    depth, height, width = owners.shape
+    depth = len(owners)
+    width = owners[0].shape[1]
     body = width // LANES * rows
     shared_rows = depth * query_count * (width // LANES)
     total = depth * body + shared_rows + EXTRA
@@ -142,6 +165,7 @@
     return pl.pallas_call(
         functools.partial(
             request_kernel,
+            depth=depth,
             grid_y=grid_y,
             grid_x=grid_x,
             rows=rows,
@@ -151,7 +175,7 @@
         grid_spec=pltpu.PrefetchScalarGridSpec(
             num_scalar_prefetch=1,
             grid=(targets // block,),
-            in_specs=[whole(owners), whole(w_own), whole(w_other)],
+            in_specs=[whole(w_own), whole(w_other)] + [whole(owner) for owner in owners],
             out_specs=pl.BlockSpec((block, total, LANES), lambda i, *_: (i, 0, 0)),
             scratch_shapes=[
                 pltpu.VMEM((2 * EXTRA, LANES), jnp.int32),
@@ -165,7 +189,7 @@
         compiler_params=pltpu.CompilerParams(vmem_limit_bytes=VMEM_LIMIT),
         cost_estimate=pl.CostEstimate(flops=1 << 29, bytes_accessed=6 << 20, transcendentals=0),
         name="request",
-    )(place, in_hbm(owners), in_hbm(w_own), in_hbm(w_other))
+    )(place, in_hbm(w_own), w_other, *owners)
 
 
 def index_stats(query, slab, picked, logits):
@@ -521,12 +545,6 @@
     head_size = model_width // HEADS
     here_x, here_z, here_y = shard_here % grid_x, shard_here // grid_x % depth, shard_here // (grid_x * depth)
     owned = depth // PAIR
-    columns = [
-        [(y * depth + k * PAIR + in_pair) * grid_x + x for k in range(owned)]
-        for y in range(grid_y)
-        for x in range(grid_x)
-        for in_pair in range(PAIR)
-    ]
     pairs = [
         [
             (y * depth + k * PAIR + in_pair) * grid_x + x
@@ -541,10 +559,21 @@
     own_list = cand_ids.reshape(list_length)
     own_anchor = own_list // slab_count
     sent = pack(cand_ids, text_states.reshape(query_count * text_count, model_width), queries, slab_count)
-    owners = lax.all_gather(sent, "shard", axis=0, tiled=True, axis_index_groups=columns)
+    owners = [sent]
+    for o in range(1, owned):
+        moves = [
+            (
+                (y * depth + z) * grid_x + x,
+                (y * depth + (z + o * PAIR) % depth) * grid_x + x,
+            )
+            for y in range(grid_y)
+            for z in range(depth)
+            for x in range(grid_x)
+        ]
+        owners.append(lax.ppermute(sent, "shard", moves))
     request = make_request(
-        (here_z // PAIR * PAIR).reshape(1),
-        owners.reshape(owned, sent.shape[0], model_width),
+        jnp.stack([here_z // PAIR * PAIR, here_z // PAIR]),
+        owners,
         w_query,
         w_query_other,
         grid_y,

time: 194 us -> 198 us (1.021)
  blocking collectives: 20 us -> 0 us
  waiting for transfers between devices: 114 us -> 127 us
  starting transfers between devices: 21 us -> 32.9 us
    all_gather x1 -> x0, blocking collectives: 20 us -> none  [on_device(): lax.all_gather(sent, 'shard', axis=0, tiled=True, axis_index_groups=columns)]
    ppermute x0 -> x3, starting transfers between devices: none -> 10.5 us  [on_device(): owners.append(lax.ppermute(sent, 'shard', moves))]
    all_to_all x1, waiting for transfers between devices: 37.2 us -> 44.3 us  [on_device(): lax.all_to_all(request, 'shard', split_axis=0, concat_axis=0, tiled=True,...]
    ppermute x0 -> x3, waiting for transfers between devices: none -> 6.99 us  [on_device(): owners.append(lax.ppermute(sent, 'shard', moves))]
    all_to_all x1, starting transfers between devices: 8.74 us -> 10.8 us  [on_device(): lax.all_to_all(request, 'shard', split_axis=0, concat_axis=0, tiled=True,...]
  transfers between devices with their start and end apart: 6 -> 9, of which waited for: 4 -> 7; matrix products, arithmetic and copies ran while one was open for 6% -> 6% of each run, Pallas kernels for 1% -> 1%
where the time goes in v8:
time: 198 us; the launch traced here: 197 us
  waiting for transfers between devices  127 us (64%)
  starting transfers between devices  32.9 us (17%)
  Pallas kernels  24.7 us (12%)
  matrix products  7.03 us (4%)
  other arithmetic  2.5 us (1%)
    all_to_all x1, waiting for transfers between devices, on_device(): lax.all_to_all(context, 'shard', split_axis=0, concat_axis=0, tiled=True)  72.7 us
    all_to_all x1, waiting for transfers between devices, on_device(): lax.all_to_all(request, 'shard', split_axis=0, concat_axis=0, tiled=True,...  44.3 us
    pallas_call x1, Pallas kernels, serve(): pl.pallas_call(functools.partial(serve_kernel, grid_y=grid_y, grid_x=grid...  11.7 us
    all_to_all x1, starting transfers between devices, on_device(): lax.all_to_all(request, 'shard', split_axis=0, concat_axis=0, tiled=True,...  10.8 us
    all_to_all x1, starting transfers between devices, on_device(): lax.all_to_all(context, 'shard', split_axis=0, concat_axis=0, tiled=True)  10.6 us
    ppermute x3, starting transfers between devices, on_device(): owners.append(lax.ppermute(sent, 'shard', moves))  10.5 us
    dot_general x2, matrix products, project_rows(): jnp.einsum('spc,cd->spd', rows_in, weight, preferred_element_type=jnp.flo...  7.03 us
    ppermute x3, waiting for transfers between devices, on_device(): owners.append(lax.ppermute(sent, 'shard', moves))  6.99 us
  transfers between devices with their start and end apart: 9, of which 7 were waited for; matrix products, arithmetic and copies ran while one was open for 6% of the time, Pallas kernels for 1%

profile of v8, /device:TPU:32, one launch (start us, length us, event | category | flops | bytes accessed | tf_op | source)
XLA Modules:
  0.0 197.0 jit_solution(11465994680534751714)
XLA Ops:
  0.6 0.0 copy-start
  0.6 0.1 collective-permute-start
  0.7 1.1 pack.1.rest_0_
  1.8 3.3 %collective-permute-start.1 = (bf16[80,768]{1,0:T(8,128)(2,1)S(1)}, bf16[80,768]{1,0:T(8,128)(2,1)S(1)}, u32[]{:S(2)}, u32[]{:S(2)}) collective-permute-start(bf16[80,768]{1,0:T(8,128)(2,1)S(1)} %pack.1.rest_0_), channel_id=1, source_target_pairs={{0,16},{2,18},{4,20},{6,22},{8,24},{10,26},{12,28},{14,30},{16,32}... | collective-permute-start | bytes 368648 | tf_op jit(solution)/shard_map/ppermute | solution.py:573
  5.2 4.5 %collective-permute-start.2 = (bf16[80,768]{1,0:T(8,128)(2,1)S(1)}, bf16[80,768]{1,0:T(8,128)(2,1)}, u32[]{:S(2)}, u32[]{:S(2)}) collective-permute-start(bf16[80,768]{1,0:T(8,128)(2,1)S(1)} %pack.1.rest_0_), channel_id=1, source_target_pairs={{0,32},{2,34},{4,36},{6,38},{8,40},{10,42},{12,44},{14,46},{16,48}... | collective-permute-start | bytes 368648 | tf_op jit(solution)/shard_map/ppermute | solution.py:573
  9.7 2.7 %collective-permute-start.3 = (bf16[80,768]{1,0:T(8,128)(2,1)S(1)}, bf16[80,768]{1,0:T(8,128)(2,1)}, u32[]{:S(2)}, u32[]{:S(2)}) collective-permute-start(bf16[80,768]{1,0:T(8,128)(2,1)S(1)} %pack.1.rest_0_), channel_id=1, source_target_pairs={{0,48},{2,50},{4,52},{6,54},{8,56},{10,58},{12,60},{14,62},{16,0},... | collective-permute-start | bytes 368648 | tf_op jit(solution)/shard_map/ppermute | solution.py:573
  12.3 0.1 pad_add_fusion.place
  12.4 1.9 collective-permute-done.1.rest_1_
  14.3 3.0 %collective-permute-done.2.rest_2_ = bf16[80,768]{1,0:T(8,128)(2,1)} collective-permute-done((bf16[80,768]{1,0:T(8,128)(2,1)S(1)}, bf16[80,768]{1,0:T(8,128)(2,1)}, u32[]{:S(2)}, u32[]{:S(2)}) %collective-permute-start.2) | collective-permute-done | bytes 122912 | tf_op jit(solution)/shard_map/ppermute | solution.py:573
  17.3 2.1 %collective-permute-done.3.rest_3_ = bf16[80,768]{1,0:T(8,128)(2,1)} collective-permute-done((bf16[80,768]{1,0:T(8,128)(2,1)S(1)}, bf16[80,768]{1,0:T(8,128)(2,1)}, u32[]{:S(2)}, u32[]{:S(2)}) %collective-permute-start.3) | collective-permute-done | bytes 122912 | tf_op jit(solution)/shard_map/ppermute | solution.py:573
  19.4 5.6 %request.1 = bf16[32,488,128]{2,1,0:T(8,128)(2,1)} custom-call(s32[2]{0:T(128)S(1)} %pad_add_fusion.place, bf16[768,384]{1,0:T(8,128)(2,1)} %w_own.1, bf16[768,384]{1,0:T(8,128)(2,1)S(1)} %collective-permute-done.w_other, bf16[80,768]{1,0:T(8,128)(2,1)S(1)} %pack.1.rest_0_, bf16[80,768]{1,0:T(8,128)(2,1)S(1)} %collective-permute-done.1.rest_1_, ...), custom_call_target="tpu_custom_call" | custom-call | flops 536870912 | bytes 6291456 | tf_op jit(solution)/shard_map/request/pallas_call | solution.py:165
  25.0 10.8 %all-to-all-start = ((bf16[32,488,128]{2,1,0:T(8,128)(2,1)}), bf16[32,488,128]{2,1,0:T(8,128)(2,1)}, u32[]{:S(2)}, u32[]{:S(2)}) async-start(bf16[32,488,128]{2,1,0:T(8,128)(2,1)} %request.1), calls=%async_computation | async-start | bytes 7995392 | tf_op jit(solution)/shard_map/all_to_all | solution.py:585
  35.8 0.0 copy-start.5
  35.8 0.1 collective-permute-start.4
  35.9 0.5 collective-permute-start.5
  36.4 1.8 collective-permute-done.4
  38.2 3.6 %convert_bitcast_fusion.1.keys_hbm = bf16[32,40,768]{2,1,0:T(8,128)(2,1)} fusion(bf16[32,40,1024]{2,1,0:T(8,128)(2,1)S(1)} %copy-done, bf16[1024,384]{1,0:T(8,128)(2,1)S(1)} %collective-permute-done.4, bf16[1024,384]{1,0:T(8,128)(2,1)S(1)} %copy-done.4), kind=kOutput, calls=%fused_computation.1 | convolution fusion | flops 2017394688 | bytes 6160384 | tf_op jit(solution)/shard_map/spc,cd->spd/dot_general | solution.py:532
  41.8 3.5 %convert_bitcast_fusion.values_hbm = bf16[32,40,768]{2,1,0:T(8,128)(2,1)} fusion(bf16[32,40,1024]{2,1,0:T(8,128)(2,1)S(1)} %copy-done, bf16[1024,384]{1,0:T(8,128)(2,1)S(1)} %collective-permute-done.5, bf16[1024,384]{1,0:T(8,128)(2,1)S(1)} %copy-done.5), kind=kOutput, calls=%fused_computation | convolution fusion | flops 2017394688 | bytes 6160384 | tf_op jit(solution)/shard_map/spc,cd->spd/dot_general | solution.py:532
  45.2 44.3 %all-to-all-done.got_hbm = bf16[32,488,128]{2,1,0:T(8,128)(2,1)} async-done(((bf16[32,488,128]{2,1,0:T(8,128)(2,1)}), bf16[32,488,128]{2,1,0:T(8,128)(2,1)}, u32[]{:S(2)}, u32[]{:S(2)}) %all-to-all-start) | async-done | bytes 3997728 | tf_op jit(solution)/shard_map/all_to_all | solution.py:585
  89.5 11.7 %serve.1 = bf16[128,104,128]{2,1,0:T(8,128)(2,1)} custom-call(bf16[32,488,128]{2,1,0:T(8,128)(2,1)} %all-to-all-done.got_hbm, bf16[2048,768]{1,0:T(8,128)(2,1)} %slab_hbm.1, bf16[32,40,768]{2,1,0:T(8,128)(2,1)} %convert_bitcast_fusion.1.keys_hbm, bf16[32,40,768]{2,1,0:T(8,128)(2,1)} %convert_bitcast_fusion.values_hbm), custom_call_target="tpu_custom_call" | custom-call | flops 8589934592 | bytes 14680064 | tf_op jit(solution)/shard_map/serve/pallas_call | solution.py:386
  101.2 0.0 copy-start.1
  101.2 0.0 copy-start.2
  101.3 10.6 %all-to-all-start.1 = ((bf16[128,104,128]{2,1,0:T(8,128)(2,1)}), bf16[128,104,128]{2,1,0:T(8,128)(2,1)}, u32[]{:S(2)}, u32[]{:S(2)}) async-start(bf16[128,104,128]{2,1,0:T(8,128)(2,1)} %serve.1), calls=%async_computation.1 | async-start | bytes 6815744 | tf_op jit(solution)/shard_map/all_to_all | solution.py:606
  111.9 0.3 collective-permute-start.6
  112.2 0.1 reshape.16
  112.3 0.6 reshape.19.gain_hbm
  112.9 0.1 fusion.7
  113.0 1.4 collective-permute-done.6
  114.3 1.1 fusion.6
  115.4 2.4 %maximum_select_fusion.w_out_hbm = bf16[768,768]{1,0:T(8,128)(2,1)} fusion(bf16[768,384]{1,0:T(8,128)(2,1)} %collective-permute-done.6, bf16[768,384]{1,0:T(8,128)(2,1)S(1)} %copy-done.1, bf16[384,384]{1,0:T(8,128)(2,1)S(1)} %get-tuple-element.5, bf16[384,384]{1,0:T(8,128)(2,1)S(1)} %get-tuple-element.3, bf16[384,384]{1,0:T(8,128)(2,1)S(1)} %get-tuple-element.4, ...), kind=kLoop, calls=%fused_computation.8 | loop fusion | flops 7667712 | bytes 3538945 | tf_op jit(solution)/shard_map/jit(_where)/select_n | solution.py:591
  117.9 72.7 %all-to-all-done.1.back_hbm = bf16[128,104,128]{2,1,0:T(8,128)(2,1)} async-done(((bf16[128,104,128]{2,1,0:T(8,128)(2,1)}), bf16[128,104,128]{2,1,0:T(8,128)(2,1)}, u32[]{:S(2)}, u32[]{:S(2)}) %all-to-all-start.1) | async-done | bytes 3407904 | tf_op jit(solution)/shard_map/all_to_all | solution.py:606
  190.6 6.3 %finish.1 = (f32[4,16]{1,0:T(4,128)}, bf16[4,16,16,768]{3,2,1,0:T(8,128)(2,1)}) custom-call(s32[64]{0:T(128)S(1)} %and_select_fusion.shards, s32[1]{0:T(128)} %bitcast.place, bf16[128,104,128]{2,1,0:T(8,128)(2,1)} %all-to-all-done.1.back_hbm, bf16[4,16,768]{2,1,0:T(8,128)(2,1)} %text_hbm.1, bf16[768,768]{1,0:T(8,128)(2,1)} %maximum_select_fusion.w_out_hbm, ...), custom_call_target="tpu_custom_call" | custom-call | flops 1207959552 | bytes 7340032 | tf_op jit(solution)/shard_map/finish/pallas_call | solution.py:497
  (11 shorter events, 0.0 us)
Async XLA Ops:
  0.6 37.6 %copy-start = (bf16[32,40,1024]{2,1,0:T(8,128)(2,1)S(1)}, bf16[32,40,1024]{2,1,0:T(8,128)(2,1)}, u32[]{:S(2)}) copy-start(bf16[32,40,1024]{2,1,0:T(8,128)(2,1)} %param.13) | copy-start | bytes 7864324
  0.6 18.8 %collective-permute-start = (bf16[768,384]{1,0:T(8,128)(2,1)}, bf16[768,384]{1,0:T(8,128)(2,1)S(1)}, u32[]{:S(2)}, u32[]{:S(2)}) collective-permute-start(bf16[768,384]{1,0:T(8,128)(2,1)} %w_own.1), channel_id=1, source_target_pairs={{0,1},{1,0},{2,3},{3,2},{4,5},{5,4},{6,7},{7,6},{8,9},{9,8},{10,11... | collective-permute-start | bytes 1769480 | tf_op jit(solution)/shard_map/ppermute | solution.py:558
  1.8 12.5 %collective-permute-start.1 = (bf16[80,768]{1,0:T(8,128)(2,1)S(1)}, bf16[80,768]{1,0:T(8,128)(2,1)S(1)}, u32[]{:S(2)}, u32[]{:S(2)}) collective-permute-start(bf16[80,768]{1,0:T(8,128)(2,1)S(1)} %pack.1.rest_0_), channel_id=1, source_target_pairs={{0,16},{2,18},{4,20},{6,22},{8,24},{10,26},{12,28},{14,30},{16,32}... | collective-permute-start | bytes 368648 | tf_op jit(solution)/shard_map/ppermute | solution.py:573
  5.2 12.1 %collective-permute-start.2 = (bf16[80,768]{1,0:T(8,128)(2,1)S(1)}, bf16[80,768]{1,0:T(8,128)(2,1)}, u32[]{:S(2)}, u32[]{:S(2)}) collective-permute-start(bf16[80,768]{1,0:T(8,128)(2,1)S(1)} %pack.1.rest_0_), channel_id=1, source_target_pairs={{0,32},{2,34},{4,36},{6,38},{8,40},{10,42},{12,44},{14,46},{16,48}... | collective-permute-start | bytes 368648 | tf_op jit(solution)/shard_map/ppermute | solution.py:573
  9.7 9.7 %collective-permute-start.3 = (bf16[80,768]{1,0:T(8,128)(2,1)S(1)}, bf16[80,768]{1,0:T(8,128)(2,1)}, u32[]{:S(2)}, u32[]{:S(2)}) collective-permute-start(bf16[80,768]{1,0:T(8,128)(2,1)S(1)} %pack.1.rest_0_), channel_id=1, source_target_pairs={{0,48},{2,50},{4,52},{6,54},{8,56},{10,58},{12,60},{14,62},{16,0},... | collective-permute-start | bytes 368648 | tf_op jit(solution)/shard_map/ppermute | solution.py:573
  25.0 10.8 %copy-start.4 = (bf16[1024,384]{1,0:T(8,128)(2,1)S(1)}, bf16[1024,384]{1,0:T(8,128)(2,1)}, u32[]{:S(2)}) copy-start(bf16[1024,384]{1,0:T(8,128)(2,1)} %param.16) | copy-start | bytes 2359300
  25.0 64.5 %all-to-all-start = ((bf16[32,488,128]{2,1,0:T(8,128)(2,1)}), bf16[32,488,128]{2,1,0:T(8,128)(2,1)}, u32[]{:S(2)}, u32[]{:S(2)}) async-start(bf16[32,488,128]{2,1,0:T(8,128)(2,1)} %request.1), calls=%async_computation | async-start | bytes 7995392 | tf_op jit(solution)/shard_map/all_to_all | solution.py:585
  35.8 5.9 %copy-start.5 = (bf16[1024,384]{1,0:T(8,128)(2,1)S(1)}, bf16[1024,384]{1,0:T(8,128)(2,1)}, u32[]{:S(2)}) copy-start(bf16[1024,384]{1,0:T(8,128)(2,1)} %param.17) | copy-start | bytes 2359300
  35.8 2.4 %collective-permute-start.4 = (bf16[1024,384]{1,0:T(8,128)(2,1)S(1)}, bf16[1024,384]{1,0:T(8,128)(2,1)S(1)}, u32[]{:S(2)}, u32[]{:S(2)}) collective-permute-start(bf16[1024,384]{1,0:T(8,128)(2,1)S(1)} %copy-done.4), channel_id=1, source_target_pairs={{0,1},{1,0},{2,3},{3,2},{4,5},{5,4},{6,7},{7,6},{8,9},{9,8},{10,11... | collective-permute-start | bytes 2359304 | tf_op jit(solution)/shard_map/ppermute | solution.py:587
  35.9 5.8 %collective-permute-start.5 = (bf16[1024,384]{1,0:T(8,128)(2,1)}, bf16[1024,384]{1,0:T(8,128)(2,1)S(1)}, u32[]{:S(2)}, u32[]{:S(2)}) collective-permute-start(bf16[1024,384]{1,0:T(8,128)(2,1)} %param.17), channel_id=1, source_target_pairs={{0,1},{1,0},{2,3},{3,2},{4,5},{5,4},{6,7},{7,6},{8,9},{9,8},{10,11... | collective-permute-start | bytes 2359304 | tf_op jit(solution)/shard_map/ppermute | solution.py:588
  101.2 10.6 %copy-start.1 = (bf16[768,384]{1,0:T(8,128)(2,1)S(1)}, bf16[768,384]{1,0:T(8,128)(2,1)}, u32[]{:S(2)}) copy-start(bf16[768,384]{1,0:T(8,128)(2,1)} %param.18) | copy-start | bytes 1769476
  101.2 11.0 %copy-start.2 = (s32[4,16]{1,0:T(4,128)S(1)}, s32[4,16]{1,0:T(4,128)}, u32[]{:S(2)}) copy-start(s32[4,16]{1,0:T(4,128)} %ids_hbm.1) | copy-start | bytes 772
  101.3 11.0 %copy-start.3 = (f32[768]{0:T(1024)S(1)}, f32[768]{0:T(1024)}, u32[]{:S(2)}) copy-start(f32[768]{0:T(1024)} %param.19) | copy-start | bytes 9220
  101.3 89.3 %all-to-all-start.1 = ((bf16[128,104,128]{2,1,0:T(8,128)(2,1)}), bf16[128,104,128]{2,1,0:T(8,128)(2,1)}, u32[]{:S(2)}, u32[]{:S(2)}) async-start(bf16[128,104,128]{2,1,0:T(8,128)(2,1)} %serve.1), calls=%async_computation.1 | async-start | bytes 6815744 | tf_op jit(solution)/shard_map/all_to_all | solution.py:606
  111.9 2.4 %collective-permute-start.6 = (bf16[768,384]{1,0:T(8,128)(2,1)S(1)}, bf16[768,384]{1,0:T(8,128)(2,1)}, u32[]{:S(2)}, u32[]{:S(2)}) collective-permute-start(bf16[768,384]{1,0:T(8,128)(2,1)S(1)} %copy-done.1), channel_id=1, source_target_pairs={{0,1},{1,0},{2,3},{3,2},{4,5},{5,4},{6,7},{7,6},{8,9},{9,8},{10,11... | collective-permute-start | bytes 1769480 | tf_op jit(solution)/shard_map/ppermute | solution.py:589

commit v9 on v7

--- a/solution.py
+++ b/solution.py
@@ -38,40 +38,52 @@
     return pltpu.with_memory_space_constraint(array, pltpu.HBM)
 
 
-def pack_kernel(ids, text, queries, out, *, slab_count):
-    rows = text.shape[0]
+def pack_kernel(ids_hbm, text_hbm, queries_hbm, out, ids, queries, sems, *, slab_count):
+    rows = text_hbm.shape[0]
+    copies = [
+        pltpu.make_async_copy(ids_hbm, ids, sems.at[0]),
+        pltpu.make_async_copy(queries_hbm, queries, sems.at[1]),
+        pltpu.make_async_copy(text_hbm, out.at[pl.ds(0, rows), :], sems.at[2]),
+    ]
+    for copy in copies:
+        copy.start()
     count, width = queries.shape
     lane = row_of((EXTRA, LANES), 1)
     image = jnp.full((EXTRA, LANES), -1, jnp.int32)
     listed = image
+    copies[0].wait()
     for entry in range(ids.shape[0] * ids.shape[1]):
         row = ids[entry // ids.shape[1], entry % ids.shape[1]]
         here = lane == lax.div(row, slab_count)
         image = jnp.where(here, lax.rem(row, slab_count), image)
         listed = jnp.where(here, entry, listed)
+    copies[1].wait()
     pieces = [queries[...].astype(jnp.float32)]
     if count < EXTRA:
         pieces.append(jnp.zeros((EXTRA - count, width), jnp.float32))
     code = [image.astype(jnp.float32), listed.astype(jnp.float32)]
     code.append(jnp.zeros((EXTRA, width - 2 * LANES), jnp.float32))
     pieces.append(jnp.concatenate(code, axis=1))
-    out[:rows, :] = text[...]
     out[rows:, :] = jnp.concatenate(pieces, axis=0).astype(jnp.bfloat16)
+    copies[2].wait()
 
 
 def pack(ids, text, queries, slab_count):
     rows, width = text.shape
     return pl.pallas_call(
         functools.partial(pack_kernel, slab_count=slab_count),
-        grid=(1,),
-        in_specs=[pl.BlockSpec(memory_space=pltpu.SMEM)]
-        + [pl.BlockSpec(a.shape, lambda i: (0, 0)) for a in (text, queries)],
-        out_specs=pl.BlockSpec((rows + 2 * EXTRA, width), lambda i: (0, 0)),
+        in_specs=[pl.BlockSpec(memory_space=pltpu.HBM)] * 3,
+        out_specs=pl.BlockSpec(memory_space=pltpu.VMEM),
+        scratch_shapes=[
+            pltpu.SMEM(ids.shape, ids.dtype),
+            pltpu.VMEM(queries.shape, queries.dtype),
+            pltpu.SemaphoreType.DMA((3,)),
+        ],
         out_shape=jax.ShapeDtypeStruct((rows + 2 * EXTRA, width), jnp.bfloat16),
         compiler_params=pltpu.CompilerParams(vmem_limit_bytes=VMEM_LIMIT),
         cost_estimate=pl.CostEstimate(flops=1 << 20, bytes_accessed=1 << 18, transcendentals=0),
         name="pack",
-    )(ids, in_hbm(text), in_hbm(queries))
+    )(in_hbm(ids), in_hbm(text), in_hbm(queries))
 
 
 def to_scalars(vectors, decoded, table, sem):
@@ -165,7 +177,7 @@
         compiler_params=pltpu.CompilerParams(vmem_limit_bytes=VMEM_LIMIT),
         cost_estimate=pl.CostEstimate(flops=1 << 29, bytes_accessed=6 << 20, transcendentals=0),
         name="request",
-    )(place, in_hbm(owners), in_hbm(w_own), in_hbm(w_other))
+    )(place, in_hbm(owners), in_hbm(w_own), w_other)
 
 
 def index_stats(query, slab, picked, logits):

time: 194 us -> 193 us (level)
  no operation moved by 1% of the time
where the time goes in v9:
time: 193 us; the launch traced here: 191 us
  waiting for transfers between devices  113 us (59%)
  Pallas kernels  25.9 us (13%)
  starting transfers between devices  20.1 us (10%)
  blocking collectives  20.1 us (10%)
  matrix products  7.02 us (4%)
  other arithmetic  2.5 us (1%)
    all_to_all x1, waiting for transfers between devices, on_device(): lax.all_to_all(context, 'shard', split_axis=0, concat_axis=0, tiled=True)  72.4 us
    all_to_all x1, waiting for transfers between devices, on_device(): lax.all_to_all(request, 'shard', split_axis=0, concat_axis=0, tiled=True,...  37.2 us
    all_gather x1, blocking collectives, on_device(): lax.all_gather(sent, 'shard', axis=0, tiled=True, axis_index_groups=columns)  20.1 us
    pallas_call x1, Pallas kernels, serve(): pl.pallas_call(functools.partial(serve_kernel, grid_y=grid_y, grid_x=grid...  13.5 us
    all_to_all x1, starting transfers between devices, on_device(): lax.all_to_all(context, 'shard', split_axis=0, concat_axis=0, tiled=True)  10.6 us
    all_to_all x1, starting transfers between devices, on_device(): lax.all_to_all(request, 'shard', split_axis=0, concat_axis=0, tiled=True,...  8.75 us
    dot_general x2, matrix products, project_rows(): jnp.einsum('spc,cd->spd', rows_in, weight, preferred_element_type=jnp.flo...  7.02 us
    pallas_call x1, Pallas kernels, finish(): pl.pallas_call(functools.partial(finish_kernel, top_count=top_count, quer...  6.3 us
  transfers between devices with their start and end apart: 6, of which 4 were waited for; matrix products, arithmetic and copies ran while one was open for 6% of the time, Pallas kernels for 1%

profile of v9, /device:TPU:32, one launch (start us, length us, event | category | flops | bytes accessed | tf_op | source)
XLA Modules:
  0.0 191.4 jit_solution(13517461267861938182)
XLA Ops:
  0.6 0.0 copy-start
  0.6 0.1 collective-permute-start
  0.8 1.1 pack.1
  1.9 20.1 %all_gather.3 = bf16[320,768]{1,0:T(8,128)(2,1)} all-gather(bf16[80,768]{1,0:T(8,128)(2,1)S(1)} %pack.1), channel_id=1, replica_groups={{0,16,32,48},{8,24,40,56},{2,18,34,50},{10,26,42,58},{4,20,36,52},{12,2..., dimensions={0}, use_global_device_ids=true | all-gather | bytes 614400 | tf_op jit(solution)/shard_map/all_gather | solution.py:556
  22.0 0.0 collective-permute-done.w_other
  22.0 5.1 %request.1 = bf16[32,488,128]{2,1,0:T(8,128)(2,1)} custom-call(s32[1]{0:T(128)} %bitcast.1.place, bf16[4,80,768]{2,1,0:T(8,128)(2,1)} %bitcast.16, bf16[768,384]{1,0:T(8,128)(2,1)} %w_own.1, bf16[768,384]{1,0:T(8,128)(2,1)S(1)} %collective-permute-done.w_other), custom_call_target="tpu_custom_call" | custom-call | flops 536870912 | bytes 6291456 | tf_op jit(solution)/shard_map/request/pallas_call | solution.py:154
  27.0 0.0 copy-start.4
  27.0 8.7 %all-to-all-start = ((bf16[32,488,128]{2,1,0:T(8,128)(2,1)}), bf16[32,488,128]{2,1,0:T(8,128)(2,1)}, u32[]{:S(2)}, u32[]{:S(2)}) async-start(bf16[32,488,128]{2,1,0:T(8,128)(2,1)} %request.1), calls=%async_computation | async-start | bytes 7995392 | tf_op jit(solution)/shard_map/all_to_all | solution.py:568
  35.8 0.0 copy-start.5
  35.8 0.1 collective-permute-start.1
  35.9 0.5 collective-permute-start.2
  36.4 1.9 collective-permute-done.1
  38.3 3.6 %convert_bitcast_fusion.1.keys_hbm = bf16[32,40,768]{2,1,0:T(8,128)(2,1)} fusion(bf16[32,40,1024]{2,1,0:T(8,128)(2,1)S(1)} %copy-done, bf16[1024,384]{1,0:T(8,128)(2,1)S(1)} %collective-permute-done.1, bf16[1024,384]{1,0:T(8,128)(2,1)S(1)} %copy-done.4), kind=kOutput, calls=%fused_computation.1 | convolution fusion | flops 2017394688 | bytes 6160384 | tf_op jit(solution)/shard_map/spc,cd->spd/dot_general | solution.py:520
  41.9 0.0 collective-permute-done.2
  41.9 3.5 %convert_bitcast_fusion.values_hbm = bf16[32,40,768]{2,1,0:T(8,128)(2,1)} fusion(bf16[32,40,1024]{2,1,0:T(8,128)(2,1)S(1)} %copy-done, bf16[1024,384]{1,0:T(8,128)(2,1)S(1)} %collective-permute-done.2, bf16[1024,384]{1,0:T(8,128)(2,1)S(1)} %copy-done.5), kind=kOutput, calls=%fused_computation | convolution fusion | flops 2017394688 | bytes 6160384 | tf_op jit(solution)/shard_map/spc,cd->spd/dot_general | solution.py:520
  45.3 37.2 %all-to-all-done.got_hbm = bf16[32,488,128]{2,1,0:T(8,128)(2,1)} async-done(((bf16[32,488,128]{2,1,0:T(8,128)(2,1)}), bf16[32,488,128]{2,1,0:T(8,128)(2,1)}, u32[]{:S(2)}, u32[]{:S(2)}) %all-to-all-start) | async-done | bytes 3997728 | tf_op jit(solution)/shard_map/all_to_all | solution.py:568
  82.5 13.5 %serve.1 = bf16[128,104,128]{2,1,0:T(8,128)(2,1)} custom-call(bf16[32,488,128]{2,1,0:T(8,128)(2,1)} %all-to-all-done.got_hbm, bf16[2048,768]{1,0:T(8,128)(2,1)} %slab_hbm.1, bf16[32,40,768]{2,1,0:T(8,128)(2,1)} %convert_bitcast_fusion.1.keys_hbm, bf16[32,40,768]{2,1,0:T(8,128)(2,1)} %convert_bitcast_fusion.values_hbm), custom_call_target="tpu_custom_call" | custom-call | flops 8589934592 | bytes 14680064 | tf_op jit(solution)/shard_map/serve/pallas_call | solution.py:374
  96.0 0.0 copy-start.1
  96.0 0.0 copy-start.2
  96.0 0.0 copy-start.3
  96.0 10.6 %all-to-all-start.1 = ((bf16[128,104,128]{2,1,0:T(8,128)(2,1)}), bf16[128,104,128]{2,1,0:T(8,128)(2,1)}, u32[]{:S(2)}, u32[]{:S(2)}) async-start(bf16[128,104,128]{2,1,0:T(8,128)(2,1)} %serve.1), calls=%async_computation.1 | async-start | bytes 6815744 | tf_op jit(solution)/shard_map/all_to_all | solution.py:589
  106.7 0.0 copy-done.1
  106.7 0.1 collective-permute-start.3
  106.8 0.0 copy-done.2
  106.8 0.1 reshape.22
  106.9 0.6 reshape.27.gain_hbm
  107.5 0.1 fusion.7
  107.5 1.4 collective-permute-done.3
  108.9 1.1 fusion.6
  110.0 2.5 %maximum_select_fusion.w_out_hbm = bf16[768,768]{1,0:T(8,128)(2,1)} fusion(bf16[768,384]{1,0:T(8,128)(2,1)} %collective-permute-done.3, bf16[768,384]{1,0:T(8,128)(2,1)S(1)} %copy-done.1, bf16[384,384]{1,0:T(8,128)(2,1)S(1)} %get-tuple-element.5, bf16[384,384]{1,0:T(8,128)(2,1)S(1)} %get-tuple-element.3, bf16[384,384]{1,0:T(8,128)(2,1)S(1)} %get-tuple-element.4, ...), kind=kLoop, calls=%fused_computation.8 | loop fusion | flops 7667712 | bytes 3538945 | tf_op jit(solution)/shard_map/jit(_where)/select_n | solution.py:574
  112.5 72.4 %all-to-all-done.1.back_hbm = bf16[128,104,128]{2,1,0:T(8,128)(2,1)} async-done(((bf16[128,104,128]{2,1,0:T(8,128)(2,1)}), bf16[128,104,128]{2,1,0:T(8,128)(2,1)}, u32[]{:S(2)}, u32[]{:S(2)}) %all-to-all-start.1) | async-done | bytes 3407904 | tf_op jit(solution)/shard_map/all_to_all | solution.py:589
  184.9 6.3 %finish.1 = (f32[4,16]{1,0:T(4,128)}, bf16[4,16,16,768]{3,2,1,0:T(8,128)(2,1)}) custom-call(s32[64]{0:T(128)S(1)} %and_select_fusion.shards, s32[1]{0:T(128)} %bitcast.place, bf16[128,104,128]{2,1,0:T(8,128)(2,1)} %all-to-all-done.1.back_hbm, bf16[4,16,768]{2,1,0:T(8,128)(2,1)} %text_hbm.1, bf16[768,768]{1,0:T(8,128)(2,1)} %maximum_select_fusion.w_out_hbm, ...), custom_call_target="tpu_custom_call" | custom-call | flops 1207959552 | bytes 7340032 | tf_op jit(solution)/shard_map/finish/pallas_call | solution.py:485
  (5 shorter events, 0.0 us)
Async XLA Ops:
  0.6 37.7 %copy-start = (bf16[32,40,1024]{2,1,0:T(8,128)(2,1)S(1)}, bf16[32,40,1024]{2,1,0:T(8,128)(2,1)}, u32[]{:S(2)}) copy-start(bf16[32,40,1024]{2,1,0:T(8,128)(2,1)} %param.13) | copy-start | bytes 7864324
  0.6 21.3 %collective-permute-start = (bf16[768,384]{1,0:T(8,128)(2,1)}, bf16[768,384]{1,0:T(8,128)(2,1)S(1)}, u32[]{:S(2)}, u32[]{:S(2)}) collective-permute-start(bf16[768,384]{1,0:T(8,128)(2,1)} %w_own.1), channel_id=1, source_target_pairs={{0,1},{1,0},{2,3},{3,2},{4,5},{5,4},{6,7},{7,6},{8,9},{9,8},{10,11... | collective-permute-start | bytes 1769480 | tf_op jit(solution)/shard_map/ppermute | solution.py:552
  27.0 8.8 %copy-start.4 = (bf16[1024,384]{1,0:T(8,128)(2,1)S(1)}, bf16[1024,384]{1,0:T(8,128)(2,1)}, u32[]{:S(2)}) copy-start(bf16[1024,384]{1,0:T(8,128)(2,1)} %param.16) | copy-start | bytes 2359300
  27.0 55.5 %all-to-all-start = ((bf16[32,488,128]{2,1,0:T(8,128)(2,1)}), bf16[32,488,128]{2,1,0:T(8,128)(2,1)}, u32[]{:S(2)}, u32[]{:S(2)}) async-start(bf16[32,488,128]{2,1,0:T(8,128)(2,1)} %request.1), calls=%async_computation | async-start | bytes 7995392 | tf_op jit(solution)/shard_map/all_to_all | solution.py:568
  35.8 6.1 %copy-start.5 = (bf16[1024,384]{1,0:T(8,128)(2,1)S(1)}, bf16[1024,384]{1,0:T(8,128)(2,1)}, u32[]{:S(2)}) copy-start(bf16[1024,384]{1,0:T(8,128)(2,1)} %param.17) | copy-start | bytes 2359300
  35.8 2.5 %collective-permute-start.1 = (bf16[1024,384]{1,0:T(8,128)(2,1)S(1)}, bf16[1024,384]{1,0:T(8,128)(2,1)S(1)}, u32[]{:S(2)}, u32[]{:S(2)}) collective-permute-start(bf16[1024,384]{1,0:T(8,128)(2,1)S(1)} %copy-done.4), channel_id=1, source_target_pairs={{0,1},{1,0},{2,3},{3,2},{4,5},{5,4},{6,7},{7,6},{8,9},{9,8},{10,11... | collective-permute-start | bytes 2359304 | tf_op jit(solution)/shard_map/ppermute | solution.py:570
  35.9 5.9 %collective-permute-start.2 = (bf16[1024,384]{1,0:T(8,128)(2,1)}, bf16[1024,384]{1,0:T(8,128)(2,1)S(1)}, u32[]{:S(2)}, u32[]{:S(2)}) collective-permute-start(bf16[1024,384]{1,0:T(8,128)(2,1)} %param.17), channel_id=1, source_target_pairs={{0,1},{1,0},{2,3},{3,2},{4,5},{5,4},{6,7},{7,6},{8,9},{9,8},{10,11... | collective-permute-start | bytes 2359304 | tf_op jit(solution)/shard_map/ppermute | solution.py:571
  96.0 10.7 %copy-start.1 = (bf16[768,384]{1,0:T(8,128)(2,1)S(1)}, bf16[768,384]{1,0:T(8,128)(2,1)}, u32[]{:S(2)}) copy-start(bf16[768,384]{1,0:T(8,128)(2,1)} %param.18) | copy-start | bytes 1769476
  96.0 10.8 %copy-start.2 = (s32[4,16]{1,0:T(4,128)S(1)}, s32[4,16]{1,0:T(4,128)}, u32[]{:S(2)}) copy-start(s32[4,16]{1,0:T(4,128)} %ids_hbm.1) | copy-start | bytes 772
  96.0 10.8 %copy-start.3 = (f32[768]{0:T(1024)S(1)}, f32[768]{0:T(1024)}, u32[]{:S(2)}) copy-start(f32[768]{0:T(1024)} %param.19) | copy-start | bytes 9220
  96.0 88.9 %all-to-all-start.1 = ((bf16[128,104,128]{2,1,0:T(8,128)(2,1)}), bf16[128,104,128]{2,1,0:T(8,128)(2,1)}, u32[]{:S(2)}, u32[]{:S(2)}) async-start(bf16[128,104,128]{2,1,0:T(8,128)(2,1)} %serve.1), calls=%async_computation.1 | async-start | bytes 6815744 | tf_op jit(solution)/shard_map/all_to_all | solution.py:589
  106.7 2.2 %collective-permute-start.3 = (bf16[768,384]{1,0:T(8,128)(2,1)S(1)}, bf16[768,384]{1,0:T(8,128)(2,1)}, u32[]{:S(2)}, u32[]{:S(2)}) collective-permute-start(bf16[768,384]{1,0:T(8,128)(2,1)S(1)} %copy-done.1), channel_id=1, source_target_pairs={{0,1},{1,0},{2,3},{3,2},{4,5},{5,4},{6,7},{7,6},{8,9},{9,8},{10,11... | collective-permute-start | bytes 1769480 | tf_op jit(solution)/shard_map/ppermute | solution.py:572

commit v10 on v9

--- a/solution.py
+++ b/solution.py
@@ -16,7 +16,7 @@
 UNROLL = 16
 PAIR = 2
 GRIDS = {128: (4, 8, 4), 8: (2, 2, 2)}
-VMEM_LIMIT = 48 * 1024 * 1024
+VMEM_LIMIT = 40 * 1024 * 1024
 
 
 def row_of(shape, dim):
@@ -32,6 +32,10 @@
 def owner_of(source, k, grid_y, grid_x, owned):
     in_pair, y, x = split_source(source, grid_y, grid_x)
     return (y * owned * PAIR + k * PAIR + in_pair) * grid_x + x
+
+
+def in_vmem(array):
+    return pltpu.with_memory_space_constraint(array, pltpu.VMEM)
 
 
 def in_hbm(array):
@@ -210,25 +214,18 @@
 
 
 def serve_kernel(
-    got_hbm, slab_hbm, keys_hbm, values_hbm, out_hbm,
-    out, got, slab, keys, values, logits, decoded, table, listed, sems, *, grid_y, grid_x, depth, rows, query_count, top_count, head_size
+    got, slab_hbm, keys_hbm, values_hbm, out_hbm,
+    out, slab, keys, values, logits, decoded, table, listed, sems, *, grid_y, grid_x, depth, rows, query_count, top_count, head_size
 ):
     sources = got.shape[0]
     slots = sources * depth
     columns = keys.shape[2]
     body = columns // LANES * rows
     slot_rows = depth * body
-    late = got.shape[1] - slot_rows
     copies = [
         pltpu.make_async_copy(source, target, sems.at[i])
         for i, (source, target) in enumerate(
-            [
-                (got_hbm.at[:, pl.ds(slot_rows, late), :], got.at[:, pl.ds(slot_rows, late), :]),
-                (slab_hbm, slab),
-                (got_hbm.at[:, pl.ds(0, slot_rows), :], got.at[:, pl.ds(0, slot_rows), :]),
-                (keys_hbm, keys),
-                (values_hbm, values),
-            ]
+            [(slab_hbm, slab), (keys_hbm, keys), (values_hbm, values)]
         )
     ]
     for copy in copies:
@@ -239,7 +236,6 @@
     lane = row_of((EXTRA, LANES), 1)
     tile_row = row_of((EXTRA, LANES), 0)
 
-    copies[0].wait()
     found = [jnp.zeros((EXTRA, LANES), jnp.float32) for _ in range(-(-sources // EXTRA))]
     for source in range(sources):
         code = got[source, slot_rows + shared_rows :, :LANES].astype(jnp.float32)
@@ -276,7 +272,7 @@
     missing = len(chunks) * LANES - queries.shape[0]
     if missing:
         queries = jnp.concatenate([queries, jnp.zeros((missing, queries.shape[1]), queries.dtype)], axis=0)
-    copies[1].wait()
+    copies[0].wait()
     stats = index_stats(queries, slab, jnp.concatenate([chunk[:1] for chunk in chunks], axis=1), logits)
     for c in range(len(chunks)):
         tiles = [split_rows(stat[:, c * LANES : (c + 1) * LANES]) for stat in stats]
@@ -297,9 +293,8 @@
     def send(owner):
         return pltpu.make_async_copy(out.at[owner, pl.ds(0, body), :], out_hbm.at[owner, pl.ds(0, body), :], sems.at[7])
 
+    copies[1].wait()
     copies[2].wait()
-    copies[3].wait()
-    copies[4].wait()
     spans = []
     at = 0
     while at < columns:
@@ -335,15 +330,16 @@
         highest = [jnp.max(score, axis=-1, keepdims=True) for score in scores]
         powers = [jnp.exp(score - top) for score, top in zip(scores, highest)]
         totals = [jnp.sum(power, axis=-1, keepdims=True) for power in powers]
-        weights = [(power / total).astype(jnp.bfloat16) for power, total in zip(powers, totals)]
+        inverses = [1.0 / total for total in totals]
+        weights = [(power * inverse).astype(jnp.bfloat16) for power, inverse in zip(powers, inverses)]
         mixed = [
             jnp.dot(weight, values[images[g], :, at : at + width], preferred_element_type=jnp.float32)
             for weight, (g, (at, width, _)) in zip(weights, work)
         ]
         for mix, (g, (at, width, masks)) in zip(mixed, work):
-            context = mix[:rows] * masks[0]
+            context = mix[:rows]
             for h in range(1, len(masks)):
-                context = context + mix[h * rows : (h + 1) * rows] * masks[h]
+                context = jnp.where(masks[h] > 0.5, mix[h * rows : (h + 1) * rows], context)
             context = context.astype(jnp.bfloat16)
             for c in range(width // LANES):
                 out[owners[g], (at // LANES + c) * rows : (at // LANES + c + 1) * rows, :] = context[
@@ -383,10 +379,10 @@
             head_size=head_size,
         ),
         grid=(1,),
-        in_specs=[pl.BlockSpec(memory_space=pltpu.HBM)] * 4,
+        in_specs=[pl.BlockSpec(memory_space=pltpu.VMEM)] + [pl.BlockSpec(memory_space=pltpu.HBM)] * 3,
         out_specs=pl.BlockSpec(memory_space=pltpu.HBM),
         scratch_shapes=[pltpu.VMEM((slots, body + EXTRA, LANES), jnp.bfloat16)]
-        + [pltpu.VMEM(a.shape, a.dtype) for a in operands]
+        + [pltpu.VMEM(a.shape, a.dtype) for a in operands[1:]]
         + [
             pltpu.VMEM((slab.shape[0], lanes), jnp.float32),
             pltpu.VMEM(codes, jnp.int32),
@@ -398,40 +394,25 @@
         compiler_params=pltpu.CompilerParams(vmem_limit_bytes=VMEM_LIMIT),
         cost_estimate=pl.CostEstimate(flops=8 << 30, bytes_accessed=14 << 20, transcendentals=2 << 20),
         name="serve",
-    )(*[in_hbm(a) for a in operands])
+    )(in_vmem(got), *[in_hbm(a) for a in operands[1:]])
 
 
 def finish_kernel(
-    shards, place, back_hbm, text_hbm, w_out_hbm, gain_hbm, found, out_hbm,
-    exact, gathered, back, sent, text, w_out, gain, out, sems, *, top_count, query_count, chunks, shift
+    shards, place, back, text_hbm, w_out_hbm, gain_hbm, found, out_hbm,
+    exact, gathered, text, w_out, gain, out, sems, *, top_count, query_count, chunks, shift
 ):
     rows, width = text.shape[1:]
-    body = back.shape[1]
+    body = back.shape[1] - EXTRA
     entries = query_count * top_count // chunks
     queries = query_count // chunks
 
-    def fetch(entry, chunk):
-        return pltpu.make_async_copy(back_hbm.at[shards[entry], pl.ds(0, body), :], back.at[entry], sems.at[chunk])
-
     loads = [
-        pltpu.make_async_copy(source, target, sems.at[chunks + i])
-        for i, (source, target) in enumerate(
-            [
-                (back_hbm.at[:, pl.ds(body, EXTRA), :], sent),
-                (w_out_hbm, w_out),
-                (text_hbm, text),
-                (gain_hbm, gain),
-            ]
-        )
+        pltpu.make_async_copy(source, target, sems.at[i])
+        for i, (source, target) in enumerate([(w_out_hbm, w_out), (text_hbm, text), (gain_hbm, gain)])
     ]
     for load in loads:
         load.start()
-    for chunk in range(chunks):
-        for entry in range(chunk * entries, (chunk + 1) * entries):
-            fetch(entry, chunk).start()
-
-    loads[0].wait()
-    parts = sent[...].astype(jnp.float32)
+    parts = back[:, body:, :].astype(jnp.float32)
     joined = jnp.sum(jnp.where(row_of(parts.shape, 1) < 3, parts, 0.0), axis=1)
     joined = pltpu.roll(joined, lax.rem(LANES - place[0] * query_count, LANES), 1)
     exact[...] = joined
@@ -448,17 +429,16 @@
         result = jnp.sum(jnp.where(lane == row_of(picked.shape, 0), result, 0.0), axis=0, keepdims=True)
         found[query : query + 1, :] = result[:, :top_count]
 
-    for load in loads[1:]:
+    for load in loads:
         load.wait()
     stores = []
     for chunk in range(chunks):
         first = chunk * queries
-        for entry in range(chunk * entries, (chunk + 1) * entries):
-            fetch(entry, chunk).wait()
         for k in range(entries):
+            shard = shards[chunk * entries + k]
             for j in range(body // rows):
                 gathered[chunk, k * rows : (k + 1) * rows, j * LANES : (j + 1) * LANES] = back[
-                    chunk * entries + k, j * rows : (j + 1) * rows, :
+                    shard, j * rows : (j + 1) * rows, :
                 ]
         mixed = jnp.dot(gathered[chunk], w_out[...], preferred_element_type=jnp.float32)
         states = text[first : first + queries].astype(jnp.float32).reshape(queries, 1, rows, width)
@@ -469,7 +449,7 @@
         normed = centred * lax.rsqrt(variance + EPSILON) * gain[...].reshape(1, 1, 1, width)
         out[first : first + queries] = normed.astype(jnp.bfloat16)
         store = pltpu.make_async_copy(
-            out.at[pl.ds(first, queries)], out_hbm.at[pl.ds(first, queries)], sems.at[chunks + 4 + chunk]
+            out.at[pl.ds(first, queries)], out_hbm.at[pl.ds(first, queries)], sems.at[3 + chunk]
         )
         store.start()
         stores.append(store)
@@ -487,7 +467,7 @@
         grid_spec=pltpu.PrefetchScalarGridSpec(
             num_scalar_prefetch=2,
             grid=(1,),
-            in_specs=[pl.BlockSpec(memory_space=pltpu.HBM)] * 4,
+            in_specs=[pl.BlockSpec(memory_space=pltpu.VMEM)] + [pl.BlockSpec(memory_space=pltpu.HBM)] * 3,
             out_specs=[
                 pl.BlockSpec((query_count, top_count), lambda i, *_: (0, 0)),
                 pl.BlockSpec(memory_space=pltpu.HBM),
@@ -495,13 +475,11 @@
             scratch_shapes=[
                 pltpu.VMEM((back.shape[0], LANES), jnp.float32),
                 pltpu.VMEM((chunks, entries // chunks * rows, width), jnp.bfloat16),
-                pltpu.VMEM((entries, body, LANES), jnp.bfloat16),
-                pltpu.VMEM((back.shape[0], EXTRA, LANES), jnp.bfloat16),
                 pltpu.VMEM(text.shape, text.dtype),
                 pltpu.VMEM(w_out.shape, w_out.dtype),
                 pltpu.VMEM(gain.shape, gain.dtype),
                 pltpu.VMEM((query_count, top_count, rows, width), jnp.bfloat16),
-                pltpu.SemaphoreType.DMA((2 * chunks + 4,)),
+                pltpu.SemaphoreType.DMA((chunks + 3,)),
             ],
         ),
         out_shape=[
@@ -513,7 +491,7 @@
             flops=2 * entries * rows * width * width, bytes_accessed=7 << 20, transcendentals=0
         ),
         name="finish",
-    )(shards, place, in_hbm(back), in_hbm(text), in_hbm(w_out), in_hbm(gain))
+    )(shards, place, in_vmem(back), in_hbm(text), in_hbm(w_out), in_hbm(gain))
 
 
 def project_rows(rows_in, weight):

time: 193 us -> 196 us (1.016)
  no operation moved by 1% of the time
where the time goes in v10:
time: 196 us; the launch traced here: 195 us
  waiting for transfers between devices  114 us (58%)
  Pallas kernels  27.1 us (14%)
  starting transfers between devices  21.7 us (11%)
  blocking collectives  20.1 us (10%)
  matrix products  7.02 us (4%)
  other arithmetic  2.5 us (1%)
    all_to_all x1, waiting for transfers between devices, on_device(): lax.all_to_all(context, 'shard', split_axis=0, concat_axis=0, tiled=True)  73.7 us
    all_to_all x1, waiting for transfers between devices, on_device(): lax.all_to_all(request, 'shard', split_axis=0, concat_axis=0, tiled=True,...  37.2 us
    all_gather x1, blocking collectives, on_device(): lax.all_gather(sent, 'shard', axis=0, tiled=True, axis_index_groups=columns)  20.1 us
    pallas_call x1, Pallas kernels, serve(): pl.pallas_call(functools.partial(serve_kernel, grid_y=grid_y, grid_x=grid...  13.4 us
    all_to_all x1, starting transfers between devices, on_device(): lax.all_to_all(context, 'shard', split_axis=0, concat_axis=0, tiled=True)  12.2 us
    all_to_all x1, starting transfers between devices, on_device(): lax.all_to_all(request, 'shard', split_axis=0, concat_axis=0, tiled=True,...  8.75 us
    pallas_call x1, Pallas kernels, finish(): pl.pallas_call(functools.partial(finish_kernel, top_count=top_count, quer...  7.55 us
    dot_general x2, matrix products, project_rows(): jnp.einsum('spc,cd->spd', rows_in, weight, preferred_element_type=jnp.flo...  7.02 us
  transfers between devices with their start and end apart: 6, of which 4 were waited for; matrix products, arithmetic and copies ran while one was open for 6% of the time, Pallas kernels for 1%

profile of v10, /device:TPU:32, one launch (start us, length us, event | category | flops | bytes accessed | tf_op | source)
XLA Modules:
  0.0 195.4 jit_solution(15144627633468859089)
XLA Ops:
  0.6 0.0 copy-start
  0.6 0.1 collective-permute-start
  0.8 1.1 pack.1
  1.9 20.1 %all_gather.3 = bf16[320,768]{1,0:T(8,128)(2,1)} all-gather(bf16[80,768]{1,0:T(8,128)(2,1)S(1)} %pack.1), channel_id=1, replica_groups={{0,16,32,48},{8,24,40,56},{2,18,34,50},{10,26,42,58},{4,20,36,52},{12,2..., dimensions={0}, use_global_device_ids=true | all-gather | bytes 614400 | tf_op jit(solution)/shard_map/all_gather | solution.py:534
  22.0 0.0 collective-permute-done.w_other
  22.0 5.1 %request.1 = bf16[32,488,128]{2,1,0:T(8,128)(2,1)} custom-call(s32[1]{0:T(128)} %bitcast.1.place, bf16[4,80,768]{2,1,0:T(8,128)(2,1)} %bitcast.16, bf16[768,384]{1,0:T(8,128)(2,1)} %w_own.1, bf16[768,384]{1,0:T(8,128)(2,1)S(1)} %collective-permute-done.w_other), custom_call_target="tpu_custom_call" | custom-call | flops 536870912 | bytes 6291456 | tf_op jit(solution)/shard_map/request/pallas_call | solution.py:158
  27.0 0.0 copy-start.4
  27.0 8.7 %all-to-all-start = ((bf16[32,488,128]{2,1,0:T(8,128)(2,1)}), bf16[32,488,128]{2,1,0:T(8,128)(2,1)}, u32[]{:S(2)}, u32[]{:S(2)}) async-start(bf16[32,488,128]{2,1,0:T(8,128)(2,1)} %request.1), calls=%async_computation | async-start | bytes 7995392 | tf_op jit(solution)/shard_map/all_to_all | solution.py:546
  35.8 0.0 copy-start.5
  35.8 0.1 collective-permute-start.1
  35.9 0.5 collective-permute-start.2
  36.4 1.9 collective-permute-done.1
  38.3 0.0 copy-done
  38.3 3.6 %convert_bitcast_fusion.1.keys_hbm = bf16[32,40,768]{2,1,0:T(8,128)(2,1)} fusion(bf16[32,40,1024]{2,1,0:T(8,128)(2,1)S(1)} %copy-done, bf16[1024,384]{1,0:T(8,128)(2,1)S(1)} %collective-permute-done.1, bf16[1024,384]{1,0:T(8,128)(2,1)S(1)} %copy-done.4), kind=kOutput, calls=%fused_computation.1 | convolution fusion | flops 2017394688 | bytes 6160384 | tf_op jit(solution)/shard_map/spc,cd->spd/dot_general | solution.py:498
  41.9 0.0 collective-permute-done.2
  41.9 3.5 %convert_bitcast_fusion.values_hbm = bf16[32,40,768]{2,1,0:T(8,128)(2,1)} fusion(bf16[32,40,1024]{2,1,0:T(8,128)(2,1)S(1)} %copy-done, bf16[1024,384]{1,0:T(8,128)(2,1)S(1)} %collective-permute-done.2, bf16[1024,384]{1,0:T(8,128)(2,1)S(1)} %copy-done.5), kind=kOutput, calls=%fused_computation | convolution fusion | flops 2017394688 | bytes 6160384 | tf_op jit(solution)/shard_map/spc,cd->spd/dot_general | solution.py:498
  45.3 37.2 %all-to-all-done.got = bf16[32,488,128]{2,1,0:T(8,128)(2,1)} async-done(((bf16[32,488,128]{2,1,0:T(8,128)(2,1)}), bf16[32,488,128]{2,1,0:T(8,128)(2,1)}, u32[]{:S(2)}, u32[]{:S(2)}) %all-to-all-start) | async-done | bytes 3997728 | tf_op jit(solution)/shard_map/all_to_all | solution.py:546
  82.5 13.4 %serve.1 = bf16[128,104,128]{2,1,0:T(8,128)(2,1)} custom-call(bf16[32,488,128]{2,1,0:T(8,128)(2,1)} %all-to-all-done.got, bf16[2048,768]{1,0:T(8,128)(2,1)} %slab_hbm.1, bf16[32,40,768]{2,1,0:T(8,128)(2,1)} %convert_bitcast_fusion.1.keys_hbm, bf16[32,40,768]{2,1,0:T(8,128)(2,1)} %convert_bitcast_fusion.values_hbm), custom_call_target="tpu_custom_call" | custom-call | flops 8589934592 | bytes 14680064 | tf_op jit(solution)/shard_map/serve/pallas_call | solution.py:370
  95.9 0.0 copy-start.1
  95.9 0.0 copy-start.2
  95.9 0.0 copy-start.3
  95.9 12.2 %all-to-all-start.1 = ((bf16[128,104,128]{2,1,0:T(8,128)(2,1)}), bf16[128,104,128]{2,1,0:T(8,128)(2,1)}, u32[]{:S(2)}, u32[]{:S(2)}) async-start(bf16[128,104,128]{2,1,0:T(8,128)(2,1)} %serve.1), calls=%async_computation.1 | async-start | bytes 6815744 | tf_op jit(solution)/shard_map/all_to_all | solution.py:567
  108.1 0.0 copy-done.1
  108.1 0.1 collective-permute-start.3
  108.2 0.1 reshape.22
  108.3 0.6 reshape.27.gain_hbm
  108.9 0.1 fusion.7
  109.0 1.4 collective-permute-done.3
  110.3 1.1 fusion.6
  111.5 2.5 %maximum_select_fusion.w_out_hbm = bf16[768,768]{1,0:T(8,128)(2,1)} fusion(bf16[768,384]{1,0:T(8,128)(2,1)} %collective-permute-done.3, bf16[768,384]{1,0:T(8,128)(2,1)S(1)} %copy-done.1, bf16[384,384]{1,0:T(8,128)(2,1)S(1)} %get-tuple-element.5, bf16[384,384]{1,0:T(8,128)(2,1)S(1)} %get-tuple-element.3, bf16[384,384]{1,0:T(8,128)(2,1)S(1)} %get-tuple-element.4, ...), kind=kLoop, calls=%fused_computation.8 | loop fusion | flops 7667712 | bytes 3538945 | tf_op jit(solution)/shard_map/jit(_where)/select_n | solution.py:552
  113.9 73.7 %all-to-all-done.1.back = bf16[128,104,128]{2,1,0:T(8,128)(2,1)} async-done(((bf16[128,104,128]{2,1,0:T(8,128)(2,1)}), bf16[128,104,128]{2,1,0:T(8,128)(2,1)}, u32[]{:S(2)}, u32[]{:S(2)}) %all-to-all-start.1) | async-done | bytes 3407904 | tf_op jit(solution)/shard_map/all_to_all | solution.py:567
  187.7 7.5 %finish.1 = (f32[4,16]{1,0:T(4,128)}, bf16[4,16,16,768]{3,2,1,0:T(8,128)(2,1)}) custom-call(s32[64]{0:T(128)S(1)} %and_select_fusion.shards, s32[1]{0:T(128)} %bitcast.place, bf16[128,104,128]{2,1,0:T(8,128)(2,1)} %all-to-all-done.1.back, bf16[4,16,768]{2,1,0:T(8,128)(2,1)} %text_hbm.1, bf16[768,768]{1,0:T(8,128)(2,1)} %maximum_select_fusion.w_out_hbm, ...), custom_call_target="tpu_custom_call" | custom-call | flops 1207959552 | bytes 7340032 | tf_op jit(solution)/shard_map/finish/pallas_call | solution.py:465
  (5 shorter events, 0.0 us)
Async XLA Ops:
  0.6 37.7 %copy-start = (bf16[32,40,1024]{2,1,0:T(8,128)(2,1)S(1)}, bf16[32,40,1024]{2,1,0:T(8,128)(2,1)}, u32[]{:S(2)}) copy-start(bf16[32,40,1024]{2,1,0:T(8,128)(2,1)} %param.13) | copy-start | bytes 7864324
  0.6 21.3 %collective-permute-start = (bf16[768,384]{1,0:T(8,128)(2,1)}, bf16[768,384]{1,0:T(8,128)(2,1)S(1)}, u32[]{:S(2)}, u32[]{:S(2)}) collective-permute-start(bf16[768,384]{1,0:T(8,128)(2,1)} %w_own.1), channel_id=1, source_target_pairs={{0,1},{1,0},{2,3},{3,2},{4,5},{5,4},{6,7},{7,6},{8,9},{9,8},{10,11... | collective-permute-start | bytes 1769480 | tf_op jit(solution)/shard_map/ppermute | solution.py:530
  27.0 8.8 %copy-start.4 = (bf16[1024,384]{1,0:T(8,128)(2,1)S(1)}, bf16[1024,384]{1,0:T(8,128)(2,1)}, u32[]{:S(2)}) copy-start(bf16[1024,384]{1,0:T(8,128)(2,1)} %param.16) | copy-start | bytes 2359300
  27.0 55.5 %all-to-all-start = ((bf16[32,488,128]{2,1,0:T(8,128)(2,1)}), bf16[32,488,128]{2,1,0:T(8,128)(2,1)}, u32[]{:S(2)}, u32[]{:S(2)}) async-start(bf16[32,488,128]{2,1,0:T(8,128)(2,1)} %request.1), calls=%async_computation | async-start | bytes 7995392 | tf_op jit(solution)/shard_map/all_to_all | solution.py:546
  35.8 6.1 %copy-start.5 = (bf16[1024,384]{1,0:T(8,128)(2,1)S(1)}, bf16[1024,384]{1,0:T(8,128)(2,1)}, u32[]{:S(2)}) copy-start(bf16[1024,384]{1,0:T(8,128)(2,1)} %param.17) | copy-start | bytes 2359300
  35.8 2.5 %collective-permute-start.1 = (bf16[1024,384]{1,0:T(8,128)(2,1)S(1)}, bf16[1024,384]{1,0:T(8,128)(2,1)S(1)}, u32[]{:S(2)}, u32[]{:S(2)}) collective-permute-start(bf16[1024,384]{1,0:T(8,128)(2,1)S(1)} %copy-done.4), channel_id=1, source_target_pairs={{0,1},{1,0},{2,3},{3,2},{4,5},{5,4},{6,7},{7,6},{8,9},{9,8},{10,11... | collective-permute-start | bytes 2359304 | tf_op jit(solution)/shard_map/ppermute | solution.py:548
  35.9 5.9 %collective-permute-start.2 = (bf16[1024,384]{1,0:T(8,128)(2,1)}, bf16[1024,384]{1,0:T(8,128)(2,1)S(1)}, u32[]{:S(2)}, u32[]{:S(2)}) collective-permute-start(bf16[1024,384]{1,0:T(8,128)(2,1)} %param.17), channel_id=1, source_target_pairs={{0,1},{1,0},{2,3},{3,2},{4,5},{5,4},{6,7},{7,6},{8,9},{9,8},{10,11... | collective-permute-start | bytes 2359304 | tf_op jit(solution)/shard_map/ppermute | solution.py:549
  95.9 12.2 %copy-start.1 = (bf16[768,384]{1,0:T(8,128)(2,1)S(1)}, bf16[768,384]{1,0:T(8,128)(2,1)}, u32[]{:S(2)}) copy-start(bf16[768,384]{1,0:T(8,128)(2,1)} %param.18) | copy-start | bytes 1769476
  95.9 12.3 %copy-start.2 = (s32[4,16]{1,0:T(4,128)S(1)}, s32[4,16]{1,0:T(4,128)}, u32[]{:S(2)}) copy-start(s32[4,16]{1,0:T(4,128)} %ids_hbm.1) | copy-start | bytes 772
  95.9 12.4 %copy-start.3 = (f32[768]{0:T(1024)S(1)}, f32[768]{0:T(1024)}, u32[]{:S(2)}) copy-start(f32[768]{0:T(1024)} %param.19) | copy-start | bytes 9220
  95.9 91.8 %all-to-all-start.1 = ((bf16[128,104,128]{2,1,0:T(8,128)(2,1)}), bf16[128,104,128]{2,1,0:T(8,128)(2,1)}, u32[]{:S(2)}, u32[]{:S(2)}) async-start(bf16[128,104,128]{2,1,0:T(8,128)(2,1)} %serve.1), calls=%async_computation.1 | async-start | bytes 6815744 | tf_op jit(solution)/shard_map/all_to_all | solution.py:567
  108.1 2.2 %collective-permute-start.3 = (bf16[768,384]{1,0:T(8,128)(2,1)S(1)}, bf16[768,384]{1,0:T(8,128)(2,1)}, u32[]{:S(2)}, u32[]{:S(2)}) collective-permute-start(bf16[768,384]{1,0:T(8,128)(2,1)S(1)} %copy-done.1), channel_id=1, source_target_pairs={{0,1},{1,0},{2,3},{3,2},{4,5},{5,4},{6,7},{7,6},{8,9},{9,8},{10,11... | collective-permute-start | bytes 1769480 | tf_op jit(solution)/shard_map/ppermute | solution.py:550

commit v11 on v9

--- a/solution.py
+++ b/solution.py
@@ -218,14 +218,12 @@
     columns = keys.shape[2]
     body = columns // LANES * rows
     slot_rows = depth * body
-    late = got.shape[1] - slot_rows
     copies = [
         pltpu.make_async_copy(source, target, sems.at[i])
         for i, (source, target) in enumerate(
             [
-                (got_hbm.at[:, pl.ds(slot_rows, late), :], got.at[:, pl.ds(slot_rows, late), :]),
+                (got_hbm, got),
                 (slab_hbm, slab),
-                (got_hbm.at[:, pl.ds(0, slot_rows), :], got.at[:, pl.ds(0, slot_rows), :]),
                 (keys_hbm, keys),
                 (values_hbm, values),
             ]
@@ -289,17 +287,8 @@
             tile = jnp.where(place == at, tiles[0], jnp.where(place == (at + 1) % per_chunk, tiles[1], tiles[2]))
             out[owner, body:, :] = tile.astype(jnp.bfloat16)
 
-    stats_out = pltpu.make_async_copy(
-        out.at[:, pl.ds(body, EXTRA), :], out_hbm.at[:, pl.ds(body, EXTRA), :], sems.at[6]
-    )
-    stats_out.start()
-
-    def send(owner):
-        return pltpu.make_async_copy(out.at[owner, pl.ds(0, body), :], out_hbm.at[owner, pl.ds(0, body), :], sems.at[7])
-
     copies[2].wait()
     copies[3].wait()
-    copies[4].wait()
     spans = []
     at = 0
     while at < columns:
@@ -349,19 +338,12 @@
                 out[owners[g], (at // LANES + c) * rows : (at // LANES + c + 1) * rows, :] = context[
                     :, c * LANES : (c + 1) * LANES
                 ]
-        for owner in owners:
-            send(owner).start()
         return carry
 
-    def drain(index, carry):
-        for _ in range(UNROLL):
-            send(0).wait()
-        return carry
-
-    groups = lax.div(count + UNROLL - 1, UNROLL)
-    lax.fori_loop(0, groups, group, 0)
-    lax.fori_loop(0, groups, drain, 0)
-    stats_out.wait()
+    lax.fori_loop(0, lax.div(count + UNROLL - 1, UNROLL), group, 0)
+    copy = pltpu.make_async_copy(out, out_hbm, sems.at[6])
+    copy.start()
+    copy.wait()
 
 
 def serve(got, slab, keys, values, grid_y, grid_x, depth, rows, query_count, top_count, head_size):
@@ -403,21 +385,18 @@
 
 def finish_kernel(
     shards, place, back_hbm, text_hbm, w_out_hbm, gain_hbm, found, out_hbm,
-    exact, gathered, back, sent, text, w_out, gain, out, sems, *, top_count, query_count, chunks, shift
+    exact, gathered, back, text, w_out, gain, out, sems, *, top_count, query_count, chunks, shift
 ):
     rows, width = text.shape[1:]
-    body = back.shape[1]
+    body = back.shape[1] - EXTRA
     entries = query_count * top_count // chunks
     queries = query_count // chunks
-
-    def fetch(entry, chunk):
-        return pltpu.make_async_copy(back_hbm.at[shards[entry], pl.ds(0, body), :], back.at[entry], sems.at[chunk])
 
     loads = [
         pltpu.make_async_copy(source, target, sems.at[chunks + i])
         for i, (source, target) in enumerate(
             [
-                (back_hbm.at[:, pl.ds(body, EXTRA), :], sent),
+                (back_hbm, back),
                 (w_out_hbm, w_out),
                 (text_hbm, text),
                 (gain_hbm, gain),
@@ -426,12 +405,8 @@
     ]
     for load in loads:
         load.start()
-    for chunk in range(chunks):
-        for entry in range(chunk * entries, (chunk + 1) * entries):
-            fetch(entry, chunk).start()
-
     loads[0].wait()
-    parts = sent[...].astype(jnp.float32)
+    parts = back[:, body:, :].astype(jnp.float32)
     joined = jnp.sum(jnp.where(row_of(parts.shape, 1) < 3, parts, 0.0), axis=1)
     joined = pltpu.roll(joined, lax.rem(LANES - place[0] * query_count, LANES), 1)
     exact[...] = joined
@@ -453,12 +428,11 @@
     stores = []
     for chunk in range(chunks):
         first = chunk * queries
-        for entry in range(chunk * entries, (chunk + 1) * entries):
-            fetch(entry, chunk).wait()
         for k in range(entries):
+            shard = shards[chunk * entries + k]
             for j in range(body // rows):
                 gathered[chunk, k * rows : (k + 1) * rows, j * LANES : (j + 1) * LANES] = back[
-                    chunk * entries + k, j * rows : (j + 1) * rows, :
+                    shard, j * rows : (j + 1) * rows, :
                 ]
         mixed = jnp.dot(gathered[chunk], w_out[...], preferred_element_type=jnp.float32)
         states = text[first : first + queries].astype(jnp.float32).reshape(queries, 1, rows, width)
@@ -495,8 +469,7 @@
             scratch_shapes=[
                 pltpu.VMEM((back.shape[0], LANES), jnp.float32),
                 pltpu.VMEM((chunks, entries // chunks * rows, width), jnp.bfloat16),
-                pltpu.VMEM((entries, body, LANES), jnp.bfloat16),
-                pltpu.VMEM((back.shape[0], EXTRA, LANES), jnp.bfloat16),
+                pltpu.VMEM(back.shape, back.dtype),
                 pltpu.VMEM(text.shape, text.dtype),
                 pltpu.VMEM(w_out.shape, w_out.dtype),
                 pltpu.VMEM(gain.shape, gain.dtype),

time: 193 us -> 194 us (level)
  no operation moved by 1% of the time
where the time goes in v11:
time: 194 us
  waiting for transfers between devices  114 us (59%)
  Pallas kernels  26.3 us (14%)
  starting transfers between devices  21.1 us (11%)
  blocking collectives  20.1 us (10%)
  matrix products  7.02 us (4%)
  other arithmetic  2.5 us (1%)
    all_to_all x1, waiting for transfers between devices, on_device(): lax.all_to_all(context, 'shard', split_axis=0, concat_axis=0, tiled=True)  73.6 us
    all_to_all x1, waiting for transfers between devices, on_device(): lax.all_to_all(request, 'shard', split_axis=0, concat_axis=0, tiled=True,...  37.2 us
    all_gather x1, blocking collectives, on_device(): lax.all_gather(sent, 'shard', axis=0, tiled=True, axis_index_groups=columns)  20.1 us
    pallas_call x1, Pallas kernels, serve(): pl.pallas_call(functools.partial(serve_kernel, grid_y=grid_y, grid_x=grid...  13.7 us
    all_to_all x1, starting transfers between devices, on_device(): lax.all_to_all(context, 'shard', split_axis=0, concat_axis=0, tiled=True)  11.6 us
    all_to_all x1, starting transfers between devices, on_device(): lax.all_to_all(request, 'shard', split_axis=0, concat_axis=0, tiled=True,...  8.75 us
    dot_general x2, matrix products, project_rows(): jnp.einsum('spc,cd->spd', rows_in, weight, preferred_element_type=jnp.flo...  7.02 us
    pallas_call x1, Pallas kernels, finish(): pl.pallas_call(functools.partial(finish_kernel, top_count=top_count, quer...  6.46 us
  transfers between devices with their start and end apart: 6, of which 4 were waited for; matrix products, arithmetic and copies ran while one was open for 6% of the time, Pallas kernels for 1%

profile of v11, /device:TPU:32, one launch (start us, length us, event | category | flops | bytes accessed | tf_op | source)
XLA Modules:
  0.0 193.9 jit_solution(17283117025948351424)
XLA Ops:
  0.6 0.0 copy-start
  0.6 0.1 collective-permute-start
  0.8 1.1 pack.1
  1.9 20.1 %all_gather.3 = bf16[320,768]{1,0:T(8,128)(2,1)} all-gather(bf16[80,768]{1,0:T(8,128)(2,1)S(1)} %pack.1), channel_id=1, replica_groups={{0,16,32,48},{8,24,40,56},{2,18,34,50},{10,26,42,58},{4,20,36,52},{12,2..., dimensions={0}, use_global_device_ids=true | all-gather | bytes 614400 | tf_op jit(solution)/shard_map/all_gather | solution.py:529
  22.0 0.0 collective-permute-done.w_other
  22.0 5.1 %request.1 = bf16[32,488,128]{2,1,0:T(8,128)(2,1)} custom-call(s32[1]{0:T(128)} %bitcast.1.place, bf16[4,80,768]{2,1,0:T(8,128)(2,1)} %bitcast.16, bf16[768,384]{1,0:T(8,128)(2,1)} %w_own.1, bf16[768,384]{1,0:T(8,128)(2,1)S(1)} %collective-permute-done.w_other), custom_call_target="tpu_custom_call" | custom-call | flops 536870912 | bytes 6291456 | tf_op jit(solution)/shard_map/request/pallas_call | solution.py:154
  27.0 0.0 copy-start.4
  27.0 8.7 %all-to-all-start = ((bf16[32,488,128]{2,1,0:T(8,128)(2,1)}), bf16[32,488,128]{2,1,0:T(8,128)(2,1)}, u32[]{:S(2)}, u32[]{:S(2)}) async-start(bf16[32,488,128]{2,1,0:T(8,128)(2,1)} %request.1), calls=%async_computation | async-start | bytes 7995392 | tf_op jit(solution)/shard_map/all_to_all | solution.py:541
  35.8 0.0 copy-start.5
  35.8 0.1 collective-permute-start.1
  35.9 0.5 collective-permute-start.2
  36.4 1.9 collective-permute-done.1
  38.3 0.0 copy-done
  38.3 3.6 %convert_bitcast_fusion.1.keys_hbm = bf16[32,40,768]{2,1,0:T(8,128)(2,1)} fusion(bf16[32,40,1024]{2,1,0:T(8,128)(2,1)S(1)} %copy-done, bf16[1024,384]{1,0:T(8,128)(2,1)S(1)} %collective-permute-done.1, bf16[1024,384]{1,0:T(8,128)(2,1)S(1)} %copy-done.4), kind=kOutput, calls=%fused_computation.1 | convolution fusion | flops 2017394688 | bytes 6160384 | tf_op jit(solution)/shard_map/spc,cd->spd/dot_general | solution.py:493
  41.9 0.0 collective-permute-done.2
  41.9 3.5 %convert_bitcast_fusion.values_hbm = bf16[32,40,768]{2,1,0:T(8,128)(2,1)} fusion(bf16[32,40,1024]{2,1,0:T(8,128)(2,1)S(1)} %copy-done, bf16[1024,384]{1,0:T(8,128)(2,1)S(1)} %collective-permute-done.2, bf16[1024,384]{1,0:T(8,128)(2,1)S(1)} %copy-done.5), kind=kOutput, calls=%fused_computation | convolution fusion | flops 2017394688 | bytes 6160384 | tf_op jit(solution)/shard_map/spc,cd->spd/dot_general | solution.py:493
  45.3 37.2 %all-to-all-done.got_hbm = bf16[32,488,128]{2,1,0:T(8,128)(2,1)} async-done(((bf16[32,488,128]{2,1,0:T(8,128)(2,1)}), bf16[32,488,128]{2,1,0:T(8,128)(2,1)}, u32[]{:S(2)}, u32[]{:S(2)}) %all-to-all-start) | async-done | bytes 3997728 | tf_op jit(solution)/shard_map/all_to_all | solution.py:541
  82.5 13.7 %serve.1 = bf16[128,104,128]{2,1,0:T(8,128)(2,1)} custom-call(bf16[32,488,128]{2,1,0:T(8,128)(2,1)} %all-to-all-done.got_hbm, bf16[2048,768]{1,0:T(8,128)(2,1)} %slab_hbm.1, bf16[32,40,768]{2,1,0:T(8,128)(2,1)} %convert_bitcast_fusion.1.keys_hbm, bf16[32,40,768]{2,1,0:T(8,128)(2,1)} %convert_bitcast_fusion.values_hbm), custom_call_target="tpu_custom_call" | custom-call | flops 8589934592 | bytes 14680064 | tf_op jit(solution)/shard_map/serve/pallas_call | solution.py:356
  96.2 0.0 copy-start.1
  96.2 0.0 copy-start.2
  96.2 0.0 copy-start.3
  96.2 11.6 %all-to-all-start.1 = ((bf16[128,104,128]{2,1,0:T(8,128)(2,1)}), bf16[128,104,128]{2,1,0:T(8,128)(2,1)}, u32[]{:S(2)}, u32[]{:S(2)}) async-start(bf16[128,104,128]{2,1,0:T(8,128)(2,1)} %serve.1), calls=%async_computation.1 | async-start | bytes 6815744 | tf_op jit(solution)/shard_map/all_to_all | solution.py:562
  107.9 0.0 copy-done.1
  107.9 0.1 collective-permute-start.3
  108.0 0.1 reshape.22
  108.1 0.6 reshape.27.gain_hbm
  108.7 0.1 fusion.7
  108.7 1.4 collective-permute-done.3
  110.1 1.1 fusion.6
  111.2 2.5 %maximum_select_fusion.w_out_hbm = bf16[768,768]{1,0:T(8,128)(2,1)} fusion(bf16[768,384]{1,0:T(8,128)(2,1)} %collective-permute-done.3, bf16[768,384]{1,0:T(8,128)(2,1)S(1)} %copy-done.1, bf16[384,384]{1,0:T(8,128)(2,1)S(1)} %get-tuple-element.5, bf16[384,384]{1,0:T(8,128)(2,1)S(1)} %get-tuple-element.3, bf16[384,384]{1,0:T(8,128)(2,1)S(1)} %get-tuple-element.4, ...), kind=kLoop, calls=%fused_computation.8 | loop fusion | flops 7667712 | bytes 3538945 | tf_op jit(solution)/shard_map/jit(_where)/select_n | solution.py:547
  113.7 73.6 %all-to-all-done.1.back_hbm = bf16[128,104,128]{2,1,0:T(8,128)(2,1)} async-done(((bf16[128,104,128]{2,1,0:T(8,128)(2,1)}), bf16[128,104,128]{2,1,0:T(8,128)(2,1)}, u32[]{:S(2)}, u32[]{:S(2)}) %all-to-all-start.1) | async-done | bytes 3407904 | tf_op jit(solution)/shard_map/all_to_all | solution.py:562
  187.3 6.5 %finish.1 = (f32[4,16]{1,0:T(4,128)}, bf16[4,16,16,768]{3,2,1,0:T(8,128)(2,1)}) custom-call(s32[64]{0:T(128)S(1)} %and_select_fusion.shards, s32[1]{0:T(128)} %bitcast.place, bf16[128,104,128]{2,1,0:T(8,128)(2,1)} %all-to-all-done.1.back_hbm, bf16[4,16,768]{2,1,0:T(8,128)(2,1)} %text_hbm.1, bf16[768,768]{1,0:T(8,128)(2,1)} %maximum_select_fusion.w_out_hbm, ...), custom_call_target="tpu_custom_call" | custom-call | flops 1207959552 | bytes 7340032 | tf_op jit(solution)/shard_map/finish/pallas_call | solution.py:459
  (5 shorter events, 0.0 us)
Async XLA Ops:
  0.6 37.7 %copy-start = (bf16[32,40,1024]{2,1,0:T(8,128)(2,1)S(1)}, bf16[32,40,1024]{2,1,0:T(8,128)(2,1)}, u32[]{:S(2)}) copy-start(bf16[32,40,1024]{2,1,0:T(8,128)(2,1)} %param.13) | copy-start | bytes 7864324
  0.6 21.3 %collective-permute-start = (bf16[768,384]{1,0:T(8,128)(2,1)}, bf16[768,384]{1,0:T(8,128)(2,1)S(1)}, u32[]{:S(2)}, u32[]{:S(2)}) collective-permute-start(bf16[768,384]{1,0:T(8,128)(2,1)} %w_own.1), channel_id=1, source_target_pairs={{0,1},{1,0},{2,3},{3,2},{4,5},{5,4},{6,7},{7,6},{8,9},{9,8},{10,11... | collective-permute-start | bytes 1769480 | tf_op jit(solution)/shard_map/ppermute | solution.py:525
  27.0 8.8 %copy-start.4 = (bf16[1024,384]{1,0:T(8,128)(2,1)S(1)}, bf16[1024,384]{1,0:T(8,128)(2,1)}, u32[]{:S(2)}) copy-start(bf16[1024,384]{1,0:T(8,128)(2,1)} %param.16) | copy-start | bytes 2359300
  27.0 55.5 %all-to-all-start = ((bf16[32,488,128]{2,1,0:T(8,128)(2,1)}), bf16[32,488,128]{2,1,0:T(8,128)(2,1)}, u32[]{:S(2)}, u32[]{:S(2)}) async-start(bf16[32,488,128]{2,1,0:T(8,128)(2,1)} %request.1), calls=%async_computation | async-start | bytes 7995392 | tf_op jit(solution)/shard_map/all_to_all | solution.py:541
  35.8 6.1 %copy-start.5 = (bf16[1024,384]{1,0:T(8,128)(2,1)S(1)}, bf16[1024,384]{1,0:T(8,128)(2,1)}, u32[]{:S(2)}) copy-start(bf16[1024,384]{1,0:T(8,128)(2,1)} %param.17) | copy-start | bytes 2359300
  35.8 2.5 %collective-permute-start.1 = (bf16[1024,384]{1,0:T(8,128)(2,1)S(1)}, bf16[1024,384]{1,0:T(8,128)(2,1)S(1)}, u32[]{:S(2)}, u32[]{:S(2)}) collective-permute-start(bf16[1024,384]{1,0:T(8,128)(2,1)S(1)} %copy-done.4), channel_id=1, source_target_pairs={{0,1},{1,0},{2,3},{3,2},{4,5},{5,4},{6,7},{7,6},{8,9},{9,8},{10,11... | collective-permute-start | bytes 2359304 | tf_op jit(solution)/shard_map/ppermute | solution.py:543
  35.9 5.9 %collective-permute-start.2 = (bf16[1024,384]{1,0:T(8,128)(2,1)}, bf16[1024,384]{1,0:T(8,128)(2,1)S(1)}, u32[]{:S(2)}, u32[]{:S(2)}) collective-permute-start(bf16[1024,384]{1,0:T(8,128)(2,1)} %param.17), channel_id=1, source_target_pairs={{0,1},{1,0},{2,3},{3,2},{4,5},{5,4},{6,7},{7,6},{8,9},{9,8},{10,11... | collective-permute-start | bytes 2359304 | tf_op jit(solution)/shard_map/ppermute | solution.py:544
  96.2 11.7 %copy-start.1 = (bf16[768,384]{1,0:T(8,128)(2,1)S(1)}, bf16[768,384]{1,0:T(8,128)(2,1)}, u32[]{:S(2)}) copy-start(bf16[768,384]{1,0:T(8,128)(2,1)} %param.18) | copy-start | bytes 1769476
  96.2 11.8 %copy-start.2 = (s32[4,16]{1,0:T(4,128)S(1)}, s32[4,16]{1,0:T(4,128)}, u32[]{:S(2)}) copy-start(s32[4,16]{1,0:T(4,128)} %ids_hbm.1) | copy-start | bytes 772
  96.2 11.9 %copy-start.3 = (f32[768]{0:T(1024)S(1)}, f32[768]{0:T(1024)}, u32[]{:S(2)}) copy-start(f32[768]{0:T(1024)} %param.19) | copy-start | bytes 9220
  96.2 91.0 %all-to-all-start.1 = ((bf16[128,104,128]{2,1,0:T(8,128)(2,1)}), bf16[128,104,128]{2,1,0:T(8,128)(2,1)}, u32[]{:S(2)}, u32[]{:S(2)}) async-start(bf16[128,104,128]{2,1,0:T(8,128)(2,1)} %serve.1), calls=%async_computation.1 | async-start | bytes 6815744 | tf_op jit(solution)/shard_map/all_to_all | solution.py:562
  107.9 2.2 %collective-permute-start.3 = (bf16[768,384]{1,0:T(8,128)(2,1)S(1)}, bf16[768,384]{1,0:T(8,128)(2,1)}, u32[]{:S(2)}, u32[]{:S(2)}) collective-permute-start(bf16[768,384]{1,0:T(8,128)(2,1)S(1)} %copy-done.1), channel_id=1, source_target_pairs={{0,1},{1,0},{2,3},{3,2},{4,5},{5,4},{6,7},{7,6},{8,9},{9,8},{10,11... | collective-permute-start | bytes 1769480 | tf_op jit(solution)/shard_map/ppermute | solution.py:545
